TPU v7x, 32 devices: a whole 2x2x4 slice. The times are simulated.
32 devices in a mesh: feat: 2 (over core), tok: 16 (over z, y, x).
Axes of the slice: x: 2, y: 2, z: 4, core: 2. Of those that a mesh axis runs over, the one named last changes fastest.
Arguments:
- activations: bfloat16 [4096, 28672], P('tok', 'feat'), may hold values from -160 to 160
- dense_rows: float32 [64, 28672], P(None, 'feat'), may hold values from -6 to 6
- targets: float32 [4096, 64], P('tok'), may hold values from -6 to 6
Outputs:
- pruned_rows: float32 [64, 28672], P(None, 'feat')
All inputs are finite; a program needn't handle non-finite values.
Results may differ from a plain program's by a relative error of at most 0.0055.
Values may be sent and summed in bfloat16 or wider, within the bound.
No kernel may reach another device: no remote copies, remote signals or barrier semaphores. Data moves between devices by JAX's collectives and lax.ppermute only.
A program may use at most 64 MiB of HBM per device.

v0:
```python
import math

import jax
import jax.numpy as jnp
from jax import lax
from jax.sharding import PartitionSpec as P

DIN = 28672
ROWS = 64
ITERS = 4


step_size = 0.25
threshold = 0.2
epsilon = 1e-06


def momentum_terms(iterations):
    values = []
    current = 1.0
    for _ in range(iterations):
        upcoming = (1.0 + math.sqrt(1.0 + 4.0 * current * current)) / 2.0
        values.append((current - 1.0) / upcoming)
        current = upcoming
    return values


def shrink_step(advance, gradient, total_square):
    mean_square = total_square / (ROWS * DIN)
    moved = advance - step_size * gradient * lax.rsqrt(mean_square + epsilon)
    return jnp.sign(moved) * jnp.maximum(jnp.abs(moved) - threshold, 0.0)


def token_gradient(residual, activations):
    return lax.dot_general(
        residual, activations, (((0,), (0,)), ((), ())), preferred_element_type=jnp.float32
    )


def shards(activations, dense_rows, targets):
    factor = DIN ** (-0.5)
    momentum = momentum_terms(ITERS)
    block_rows = activations.shape[0] // lax.axis_size("feat")
    weights = dense_rows
    advance = dense_rows
    for iteration in range(ITERS):
        rounded = advance.astype(jnp.bfloat16)
        own_rows = lax.psum_scatter(
            lax.dot_general(
                activations, rounded, (((1,), (1,)), ((), ())), preferred_element_type=jnp.float32
            ),
            "feat",
            scatter_dimension=0,
            tiled=True,
        )
        wanted = lax.dynamic_slice_in_dim(
            targets, lax.axis_index("feat") * block_rows, block_rows, 0
        )
        residual = (factor * own_rows - wanted).astype(jnp.bfloat16)
        residual = lax.all_gather(residual, "feat", axis=0, tiled=True)
        gradient = lax.psum(token_gradient(residual, activations), "tok")
        total_square = lax.psum(jnp.sum(gradient * gradient), "feat")
        shrunk = shrink_step(advance, gradient, total_square)
        advance = shrunk + momentum[iteration] * (shrunk - weights)
        weights = shrunk
    return weights


def solution(mesh):
    in_specs = (P("tok", "feat"), P(None, "feat"), P("tok", None))
    out_specs = P(None, "feat")
    return jax.shard_map(shards, mesh=mesh, in_specs=in_specs, out_specs=out_specs, check_vma=False)
```

profile of v0, /device:TPU:0, one launch (start us, length us, event | category | flops | bytes accessed | tf_op | source)
XLA Modules:
  0.0 791.3 jit_solution(15761114982791566618)
XLA Ops:
  6.5 7.1 fusion.8
  13.8 10.2 %reduce-scatter.5.cloned.1.call-done = f32[128,64]{0,1:T(8,128)} async-done(((f32[256,64]{0,1:T(8,128)}), f32[128,64]{0,1:T(8,128)}) %reduce-scatter.5.cloned.1.call-update) | async-done | bytes 32784 | tf_op jit(solution)/shard_map/reduce_scatter | solution.py:48
  24.0 0.8 subtract_convert_fusion.3
  24.8 1.8 all_gather.12
  26.6 6.3 fusion.24
  33.0 158.5 %all-reduce.5.cloned.1.call-done = f32[64,14336]{1,0:T(8,128)} async-done(((f32[64,14336]{1,0:T(8,128)}), f32[64,14336]{1,0:T(8,128)}) %all-reduce.5.cloned.1.call-update) | async-done | bytes 3670032 | tf_op jit(solution)/shard_map/psum | solution.py:61
  191.5 3.6 multiply_reduce_fusion.3
  195.1 3.1 psum.57
  198.8 8.7 %fusion.10 = f32[256,64]{0,1:T(8,128)} fusion(bf16[256,14336]{1,0:T(8,128)(2,1)} %param.3, f32[64,14336]{1,0:T(8,128)} %param.4, f32[64,14336]{1,0:T(8,128)} %all-reduce.5.cloned.1.call-done, f32[]{:T(128)S(6)} %mul.96), kind=kOutput, calls=%fused_computation.19 | convolution fusion | flops 479854592 | bytes 14745604 | tf_op jit(solution)/shard_map/dot_general | solution.py:49
  207.6 6.6 reduce-scatter.7.cloned.1.call-done
  215.0 1.8 all_gather.13
  216.8 6.3 fusion.25
  223.2 158.4 %all-reduce.7.cloned.1.call-done = f32[64,14336]{1,0:T(8,128)} async-done(((f32[64,14336]{1,0:T(8,128)}), f32[64,14336]{1,0:T(8,128)}) %all-reduce.7.cloned.1.call-update) | async-done | bytes 3670032 | tf_op jit(solution)/shard_map/psum | solution.py:61
  381.6 3.6 multiply_reduce_fusion.2
  385.2 3.3 psum.59
  389.2 11.6 %fusion.16 = f32[256,64]{0,1:T(8,128)} fusion(bf16[256,14336]{1,0:T(8,128)(2,1)} %param.3, f32[64,14336]{1,0:T(8,128)} %all-reduce.7.cloned.1.call-done, f32[]{:T(128)S(6)} %mul.103, f32[64,14336]{1,0:T(8,128)} %param.4, f32[64,14336]{1,0:T(8,128)} %all-reduce.5.cloned.1.call-done, f32[]{:T(128)S(6)} %mul.96), kind=kOutput, calls=%fused_computation.21 | convolution fusion | flops 489029632 | bytes 18415624 | tf_op jit(solution)/shard_map/dot_general | solution.py:49
  400.8 6.6 reduce-scatter.9.cloned.1.call-done
  408.2 1.8 all_gather.14
  410.0 6.3 fusion.26
  416.4 158.4 %all-reduce.9.cloned.1.call-done = f32[64,14336]{1,0:T(8,128)} async-done(((f32[64,14336]{1,0:T(8,128)}), f32[64,14336]{1,0:T(8,128)}) %all-reduce.9.cloned.1.call-update) | async-done | bytes 3670032 | tf_op jit(solution)/shard_map/psum | solution.py:61
  574.9 3.7 multiply_reduce_fusion.1
  578.6 3.1 psum.61
  582.4 9.0 %multiply_add_fusion = f32[64,14336]{1,0:T(8,128)S(1)} fusion(f32[64,14336]{1,0:T(8,128)} %all-reduce.9.cloned.1.call-done, f32[]{:T(128)S(6)} %mul.111, f32[64,14336]{1,0:T(8,128)} %all-reduce.7.cloned.1.call-done, f32[]{:T(128)S(6)} %mul.103, f32[64,14336]{1,0:T(8,128)} %param.4, f32[64,14336]{1,0:T(8,128)} %all-reduce.5.cloned.1.call-done, f32[]{:T(128)S(6)} %mul.96), kind=kLoop, calls=%fused_computation.2 | loop fusion | flops 27525120 | bytes 18350092 | tf_op jit(solution)/shard_map/add | solution.py:64
  591.4 1.8 copy-done
  593.3 3.0 fusion.13
  596.4 6.6 reduce-scatter.11.cloned.1.call-done
  603.7 2.0 all_gather.15
  605.8 6.3 fusion.27
  612.1 158.5 %all-reduce.11.cloned.1.call-done = f32[64,14336]{1,0:T(8,128)} async-done(((f32[64,14336]{1,0:T(8,128)}), f32[64,14336]{1,0:T(8,128)}) %all-reduce.11.cloned.1.call-update) | async-done | bytes 3670032 | tf_op jit(solution)/shard_map/psum | solution.py:61
  770.6 3.6 multiply_reduce_fusion
  774.2 3.1 psum.63
  777.9 6.5 maximum_multiply_fusion
  (27 shorter events, 2.7 us)
Async XLA Ops:
  6.5 17.5 %copy-start.1 = (f32[256,64]{0,1:T(8,128)S(1)}, f32[256,64]{0,1:T(8,128)}, u32[]{:S(2)}) copy-start(f32[256,64]{0,1:T(8,128)} %param.5) | copy-start | bytes 196612
  6.5 17.5 %reduce-scatter.5.cloned.1.call-start = ((), (), s32[]{:S(2)}) async-start(), calls=%async_computation.4 | async-start | bytes 98304 | tf_op jit(solution)/shard_map/reduce_scatter | solution.py:48
  13.7 177.8 %all-reduce.5.cloned.1.call-start = ((), (), s32[]{:S(2)}) async-start(), calls=%async_computation.5 | async-start | bytes 7340032 | tf_op jit(solution)/shard_map/psum | solution.py:61
  32.9 181.3 %reduce-scatter.7.cloned.1.call-start = ((), (), s32[]{:S(2)}) async-start(), calls=%async_computation.6 | async-start | bytes 98304 | tf_op jit(solution)/shard_map/reduce_scatter | solution.py:48
  207.5 174.1 %all-reduce.7.cloned.1.call-start = ((), (), s32[]{:S(2)}) async-start(), calls=%async_computation.7 | async-start | bytes 7340032 | tf_op jit(solution)/shard_map/psum | solution.py:61
  223.1 184.3 %reduce-scatter.9.cloned.1.call-start = ((), (), s32[]{:S(2)}) async-start(), calls=%async_computation.8 | async-start | bytes 98304 | tf_op jit(solution)/shard_map/reduce_scatter | solution.py:48
  400.8 174.1 %all-reduce.9.cloned.1.call-start = ((), (), s32[]{:S(2)}) async-start(), calls=%async_computation.9 | async-start | bytes 7340032 | tf_op jit(solution)/shard_map/psum | solution.py:61
  416.4 186.6 %reduce-scatter.11.cloned.1.call-start = ((), (), s32[]{:S(2)}) async-start(), calls=%async_computation.10 | async-start | bytes 98304 | tf_op jit(solution)/shard_map/reduce_scatter | solution.py:48
  574.9 18.4 %slice-start = ((s8[7340032]{0:T(1024)(128)(4,1)}), s8[3145728]{0:T(1024)(128)(4,1)S(1)}, s32[]{:S(2)}) async-start(s8[7340032]{0:T(1024)(128)(4,1)} %bitcast.18), calls=%async_computation.12 | async-start | bytes 6291456
  582.4 10.9 %slice-start.1 = ((s8[7340032]{0:T(1024)(128)(4,1)}), s8[4194304]{0:T(1024)(128)(4,1)S(1)}, s32[]{:S(2)}) async-start(s8[7340032]{0:T(1024)(128)(4,1)} %bitcast.18), calls=%async_computation.13 | async-start | bytes 8388608
  591.4 1.8 copy-start
  596.3 174.3 %all-reduce.11.cloned.1.call-start = ((), (), s32[]{:S(2)}) async-start(), calls=%async_computation.11 | async-start | bytes 7340032 | tf_op jit(solution)/shard_map/psum | solution.py:61
Sparse Core Ops, SparseCore 0:
  13.8 10.1 reduce-scatter.4
  33.1 158.3 all-reduce.4
  207.7 6.4 reduce-scatter.6
  223.3 158.3 all-reduce.6
  400.9 6.4 reduce-scatter.8
  416.5 158.3 all-reduce.8
  596.4 6.4 reduce-scatter.10
  612.2 158.3 all-reduce.10
where the time goes:
time: 792 us; the launch traced here: 791 us
  waiting for transfers between devices  664 us (84%)
  matrix products  55.8 us (7%)
  other arithmetic  33.1 us (4%)
  blocking collectives  20 us (3%)
  between operations  16.2 us (2%)
    psum x4, waiting for transfers between devices, shards(): gradient = lax.psum(token_gradient(residual, activations), 'tok')  634 us
    dot_general x4, matrix products, shards(): lax.dot_general(activations, rounded, (((1,), (1,)), ((), ())), preferred...  30.4 us
    reduce_scatter x4, waiting for transfers between devices, shards(): lax.psum_scatter(lax.dot_general(activations, rounded, (((1,), (1,)), (()...  30.1 us
    dot_general x4, matrix products, token_gradient(): lax.dot_general(residual, activations, (((0,), (0,)), ((), ())), preferre...  25.4 us
  transfers between devices with their start and end apart: 8, of which 8 were waited for; matrix products, arithmetic and copies ran while one was open for 0% of the time, Pallas kernels for 0%

commit v1 on v0

v1 whole, which is shorter than its diff:
```python
import functools
import math

import jax
import jax.numpy as jnp
from jax import lax
from jax.experimental import pallas as pl
from jax.experimental.pallas import tpu as pltpu
from jax.sharding import PartitionSpec as P

ITERS = 4
STEP = 0.25
THRESHOLD = 0.2
EPSILON = 1e-06
GROUP = 8
PARTS = 3
VMEM_BYTES = 4 * 1024 * 1024

f32 = jnp.float32
bf16 = jnp.bfloat16


def momentum_terms(iterations):
    values = []
    current = 1.0
    for _ in range(iterations):
        upcoming = (1.0 + math.sqrt(1.0 + 4.0 * current * current)) / 2.0
        values.append((current - 1.0) / upcoming)
        current = upcoming
    return values


def swap(x, axis, bit):
    pairs = [(i, i ^ (1 << bit)) for i in range(lax.axis_size(axis))]
    return lax.ppermute(x, axis, pairs)


def bits_of(axis):
    return lax.axis_size(axis).bit_length() - 1


class Plan:
    def __init__(self, rows, columns):
        self.rows = rows
        self.columns = columns
        self.rows_bits = min(bits_of("tok"), (rows // GROUP).bit_length() - 1)
        self.places = 1 << self.rows_bits
        self.height = rows >> self.rows_bits
        self.unit = next(u for u in (512, 256, 128) if columns % u == 0)
        units = columns // self.unit
        edges = [units * p // PARTS for p in range(PARTS + 1)]
        self.spans = list(zip(edges[:-1], edges[1:]))
        self.widths = [(b - a) * self.unit for a, b in self.spans]
        self.orders = [[(p + s) % self.rows_bits for s in range(self.rows_bits)] for p in range(PARTS)]

    def bit_value(self, level):
        return self.places >> (level + 1)

    def arrangement(self, p):
        result = [0]
        for level in reversed(self.orders[p]):
            result = result + [g + self.bit_value(level) for g in result]
        return result

    def mask(self):
        index = lax.axis_index("tok")
        return sum(((index >> level) & 1) * self.bit_value(level) for level in range(self.rows_bits))

    def rearranged(self, x, places):
        h = self.height
        return jnp.concatenate([x[h * g : h * (g + 1)] for g in places], 0)

    def to_part(self, p, x):
        return self.rearranged(x, self.arrangement(p))

    def from_part(self, p, x):
        order = self.arrangement(p)
        return self.rearranged(x, [order.index(g) for g in range(self.places)])


def dot_nt(a, b):
    return lax.dot_general(a, b, (((1,), (1,)), ((), ())), preferred_element_type=f32)


def vmem(count):
    return [pl.BlockSpec(memory_space=pltpu.VMEM)] * count


PARAMS = pltpu.CompilerParams(vmem_limit_bytes=VMEM_BYTES)


def first_kernel(plan, mask_ref, dense_ref, act_ref, start_ref, product_ref):
    mask = mask_ref[0]
    h = plan.height
    total = jnp.zeros(product_ref.shape, f32)

    def step(i, total):
        columns = pl.ds(pl.multiple_of(i * plan.unit, plan.unit), plan.unit)
        groups = []
        for g in range(plan.places):
            rows = pl.ds(pl.multiple_of((g ^ mask) * h, h), h)
            groups.append(dense_ref[rows, columns])
        block = jnp.concatenate(groups, 0)
        start_ref[:, columns] = block
        return total + dot_nt(block.astype(bf16), act_ref[:, columns])

    product_ref[...] = lax.fori_loop(0, plan.columns // plan.unit, step, total, unroll=2)


def gradient_kernel(plan, factor, own_ref, other_ref, wanted_ref, act_ref, *outs):
    product = own_ref[...] + other_ref[...]
    residual = factor * product - wanted_ref[...]
    half = plan.rows // 2
    for p, (first, last) in enumerate(plan.spans):
        arranged = plan.to_part(p, residual).astype(bf16)
        keep_ref, send_ref = outs[2 * p], outs[2 * p + 1]

        def step(i, carry):
            source = pl.ds(pl.multiple_of((first + i) * plan.unit, plan.unit), plan.unit)
            target = pl.ds(pl.multiple_of(i * plan.unit, plan.unit), plan.unit)
            block = jnp.dot(arranged, act_ref[:, source], preferred_element_type=f32)
            keep_ref[:, target] = block[:half]
            send_ref[:, target] = block[half:].astype(bf16)
            return carry

        lax.fori_loop(0, last - first, step, 0, unroll=2)


def square_kernel(plan, *refs):
    *halves, out_ref = refs
    total = jnp.zeros((8, 128), f32)
    for ref in halves:

        def step(i, total):
            columns = pl.ds(pl.multiple_of(i * plan.unit, plan.unit), plan.unit)
            block = ref[:, columns].astype(f32)
            block = block * block
            for r in range(0, block.shape[0], 8):
                for c in range(0, plan.unit, 128):
                    total = total + block[r : r + 8, c : c + 128]
            return total

        total = lax.fori_loop(0, ref.shape[1] // plan.unit, step, total, unroll=2)
    out_ref[...] = total


def update_kernel(plan, momentum, last, *refs):
    if last:
        mask_ref, *refs = refs
    own_ref, other_ref, *refs = refs
    halves, refs = refs[: 2 * PARTS], refs[2 * PARTS :]
    if last:
        weights_ref, ahead_ref, out_ref = refs
    else:
        weights_ref, ahead_ref, act_ref, new_weights_ref, new_ahead_ref, product_ref = refs
        total = jnp.zeros(product_ref.shape, f32)
    mean_square = jnp.sum(own_ref[...] + other_ref[...], keepdims=True) / plan.entries
    scale = STEP * lax.rsqrt(mean_square + EPSILON)
    h = plan.height
    for p, (begin, end) in enumerate(plan.spans):
        kept_ref, came_ref = halves[2 * p], halves[2 * p + 1]

        def step(i, carry):
            source = pl.ds(pl.multiple_of(i * plan.unit, plan.unit), plan.unit)
            target = pl.ds(pl.multiple_of((begin + i) * plan.unit, plan.unit), plan.unit)
            gradient = jnp.concatenate([kept_ref[:, source].astype(f32), came_ref[:, source].astype(f32)], 0)
            gradient = plan.from_part(p, gradient)
            moved = ahead_ref[:, target] - scale * gradient
            shrunk = moved - jnp.clip(moved, -THRESHOLD, THRESHOLD)
            if last:
                for g in range(plan.places):
                    rows = pl.ds(pl.multiple_of((g ^ mask_ref[0]) * h, h), h)
                    out_ref[rows, target] = shrunk[h * g : h * (g + 1)]
                return carry
            ahead = shrunk + momentum * (shrunk - weights_ref[:, target])
            new_weights_ref[:, target] = shrunk
            new_ahead_ref[:, target] = ahead
            return carry + dot_nt(ahead.astype(bf16), act_ref[:, target])

        carried = lax.fori_loop(0, end - begin, step, 0 if last else total, unroll=2)
        if not last:
            total = carried
    if not last:
        product_ref[...] = total


def all_sum(plan, pieces):
    count = len(pieces)
    current = [kept for kept, _ in pieces]
    sends = [sent for _, sent in pieces]
    for stage in range(plan.rows_bits):
        came = [swap(sends[p], "tok", plan.orders[p][stage]) for p in range(count)]
        current = [c + r.astype(f32) for c, r in zip(current, came)]
        if stage + 1 < plan.rows_bits:
            middle = current[0].shape[0] // 2
            sends = [c[middle:].astype(bf16) for c in current]
            current = [c[:middle] for c in current]
    for bit in range(plan.rows_bits, bits_of("tok")):
        low = [c.astype(bf16) for c in current]
        came = [swap(c, "tok", bit) for c in low]
        current = [a.astype(f32) + b.astype(f32) for a, b in zip(low, came)]
    current = [c.astype(bf16) for c in current]
    for stage in reversed(range(plan.rows_bits)):
        came = [swap(current[p], "tok", plan.orders[p][stage]) for p in range(count)]
        if stage:
            current = [jnp.concatenate([a, b], 0) for a, b in zip(current, came)]
    return [x for pair in zip(current, came) for x in pair]


def across_features(x):
    count = bits_of("feat")
    for bit in range(count - 1):
        x = x + swap(x, "feat", bit)
    return x, swap(x, "feat", count - 1)


def shards(activations, dense_rows, targets):
    rows, columns = dense_rows.shape
    tokens = activations.shape[0]
    plan = Plan(rows, columns)
    features = columns * lax.axis_size("feat")
    plan.entries = rows * features
    factor = features ** (-0.5)
    momentum = momentum_terms(ITERS)
    mask = plan.mask()
    wanted = targets.T
    for level in range(plan.rows_bits):
        half = rows >> (level + 1)
        cut = wanted.reshape(-1, 2, half, tokens)
        bit = (lax.axis_index("tok") >> level) & 1
        wanted = jnp.where(bit == 1, cut[:, ::-1], cut).reshape(rows, tokens)
    mask = mask.reshape(1).astype(jnp.int32)
    smem = [pl.BlockSpec(memory_space=pltpu.SMEM)]
    state = jax.ShapeDtypeStruct((rows, columns), f32)
    small = jax.ShapeDtypeStruct((rows, tokens), f32)
    tile = jax.ShapeDtypeStruct((8, 128), f32)
    halves = []
    for width in plan.widths:
        halves.append(jax.ShapeDtypeStruct((rows // 2, width), f32))
        halves.append(jax.ShapeDtypeStruct((rows // 2, width), bf16))

    ahead, product = pl.pallas_call(
        functools.partial(first_kernel, plan),
        out_shape=(state, small),
        in_specs=smem + vmem(2),
        out_specs=tuple(vmem(2)),
        compiler_params=PARAMS,
        name="first",
    )(mask, dense_rows, activations)
    weights = ahead
    for iteration in range(ITERS):
        own, other = across_features(product)
        pieces = pl.pallas_call(
            functools.partial(gradient_kernel, plan, factor),
            out_shape=tuple(halves),
            in_specs=vmem(4),
            out_specs=tuple(vmem(2 * PARTS)),
            compiler_params=PARAMS,
            name="gradient",
        )(own, other, wanted, activations)
        summed = all_sum(plan, list(zip(pieces[::2], pieces[1::2])))
        square = pl.pallas_call(
            functools.partial(square_kernel, plan),
            out_shape=tile,
            in_specs=vmem(2 * PARTS),
            out_specs=vmem(1)[0],
            compiler_params=PARAMS,
            name="square",
        )(*summed)
        own, other = across_features(square)
        if iteration + 1 < ITERS:
            weights, ahead, product = pl.pallas_call(
                functools.partial(update_kernel, plan, momentum[iteration], False),
                out_shape=(state, state, small),
                in_specs=vmem(2 + 2 * PARTS + 3),
                out_specs=tuple(vmem(3)),
                compiler_params=PARAMS,
                name="update",
            )(own, other, *summed, weights, ahead, activations)
        else:
            weights = pl.pallas_call(
                functools.partial(update_kernel, plan, momentum[iteration], True),
                out_shape=state,
                in_specs=smem + vmem(2 + 2 * PARTS + 2),
                out_specs=vmem(1)[0],
                compiler_params=PARAMS,
                name="last",
            )(mask, own, other, *summed, weights, ahead)
    return weights


def solution(mesh):
    in_specs = (P("tok", "feat"), P(None, "feat"), P("tok", None))
    out_specs = P(None, "feat")
    return jax.shard_map(shards, mesh=mesh, in_specs=in_specs, out_specs=out_specs, check_vma=False)
```

time: 792 us -> 258 us (0.33)
  waiting for transfers between devices: 664 us -> 98.1 us
  starting transfers between devices: 0.29 us -> 109 us
  matrix products: 55.8 us -> 0 us
  Pallas kernels: 0 us -> 37.2 us
  other arithmetic: 33.1 us -> 2.01 us
  blocking collectives: 20 us -> 0 us
  between operations: 16.2 us -> 0.67 us
  local copies, waits for them, and re-layouts: 1.85 us -> 10.4 us
    psum x4 -> x0, waiting for transfers between devices: 634 us -> none  [shards(): gradient = lax.psum(token_gradient(residual, activations), 'tok')]
    ppermute x0 -> x92, starting transfers between devices: none -> 109 us  [swap(): return lax.ppermute(x, axis, pairs)]
    ppermute x0 -> x92, waiting for transfers between devices: none -> 98.1 us  [swap(): return lax.ppermute(x, axis, pairs)]
    dot_general x8 -> x0, matrix products: 55.8 us -> none  [the longest x4 30.4 us: shards(): lax.dot_general(activations, rounded, (((1,), (1,)), ((), ())), preferred...]
    pallas_call x0 -> x13, Pallas kernels: none -> 37.2 us  [the longest x4 16.6 us: shards(): pl.pallas_call(functools.partial(update_kernel, plan, momentum[iteration]...]
    reduce_scatter x4 -> x0, waiting for transfers between devices: 30.1 us -> none  [shards(): lax.psum_scatter(lax.dot_general(activations, rounded, (((1,), (1,)), (()...]
    reduce_sum x4 -> x0, other arithmetic: 14.5 us -> none  [shards(): total_square = lax.psum(jnp.sum(gradient * gradient), 'feat')]
    psum x4 -> x0, blocking collectives: 12.5 us -> none  [shards(): total_square = lax.psum(jnp.sum(gradient * gradient), 'feat')]
  transfers between devices with their start and end apart: 8 -> 92, of which waited for: 8 -> 63; matrix products, arithmetic and copies ran while one was open for 0% -> 1% of each run, Pallas kernels for 0% -> 0%
where the time goes in v1:
time: 258 us
  starting transfers between devices  109 us (42%)
  waiting for transfers between devices  98.1 us (38%)
  Pallas kernels  37.2 us (14%)
  local copies, waits for them, and re-layouts  10.4 us (4%)
    ppermute x92, starting transfers between devices, swap(): return lax.ppermute(x, axis, pairs)  109 us
    ppermute x92, waiting for transfers between devices, swap(): return lax.ppermute(x, axis, pairs)  98.1 us
    pallas_call x4, Pallas kernels, shards(): pl.pallas_call(functools.partial(update_kernel, plan, momentum[iteration]...  16.6 us
    pallas_call x4, Pallas kernels, shards(): pl.pallas_call(functools.partial(gradient_kernel, plan, factor), out_shap...  12.5 us
    unnamed x16, local copies, waits for them, and re-layouts  10.1 us
  transfers between devices with their start and end apart: 92, of which 63 were waited for; matrix products, arithmetic and copies ran while one was open for 1% of the time, Pallas kernels for 0%

profile of v1, /device:TPU:0, one launch (start us, length us, event | category | flops | bytes accessed | tf_op | source)
XLA Modules:
  0.0 257.5 jit_solution(11883243194366775960)
XLA Ops:
  0.0 3.1 %copy-done = bf16[256,14336]{1,0:T(8,128)(2,1)S(1)} copy-done((bf16[256,14336]{1,0:T(8,128)(2,1)S(1)}, bf16[256,14336]{1,0:T(8,128)(2,1)}, u32[]{:S(2)}) %copy-start) | copy-done | bytes 7340056
  5.1 4.0 %first.1 = (f32[64,14336]{1,0:T(8,128)S(1)}, f32[64,256]{1,0:T(8,128)S(1)}) custom-call(s32[1]{0:T(128)} %bitcast.mask_ref.refs_0_, f32[64,14336]{1,0:T(8,128)S(1)} %copy-done.4, bf16[256,14336]{1,0:T(8,128)(2,1)S(1)} %copy-done), custom_call_target="tpu_custom_call" | custom-call | tf_op jit(solution)/shard_map/first/pallas_call | solution.py:242
  12.3 3.1 %copy-done.1 = bf16[256,14336]{1,0:T(8,128)(2,1)S(1)} copy-done((bf16[256,14336]{1,0:T(8,128)(2,1)S(1)}, bf16[256,14336]{1,0:T(8,128)(2,1)}, u32[]{:S(2)}) %copy-start.1) | copy-done | bytes 7340056
  15.4 3.1 %gradient.4 = (f32[32,4608]{1,0:T(8,128)S(1)}, bf16[32,4608]{1,0:T(8,128)(2,1)S(1)}, f32[32,4608]{1,0:T(8,128)S(1)}, bf16[32,4608]{1,0:T(8,128)(2,1)S(1)}, f32[3...) custom-call(f32[64,256]{1,0:T(8,128)S(1)} %get-tuple-element.40.own_ref, f32[64,256]{1,0:T(8,128)S(1)} %collective-permute-done.other_ref, ...), custom_call_target="tpu_custom_call" | custom-call | tf_op jit(solution)/shard_map/gradient/pallas_call | solution.py:253
  18.5 2.9 %collective-permute-start.1 = (bf16[32,4608]{1,0:T(8,128)(2,1)S(1)}, bf16[32,4608]{1,0:T(8,128)(2,1)S(1)}, u32[]{:S(2)}, u32[]{:S(2)}) collective-permute-start(bf16[32,4608]{1,0:T(8,128)(2,1)S(1)} %get-tuple-element.42), channel_id=1, source_target_pairs={{0,1},{1,0},{2,3},{3,2},{4,5},{5,4},{6,7},{7,6},{8,9},{9,8},{10,11... | collective-permute-start | bytes 884744 | tf_op jit(solution)/shard_map/ppermute | solution.py:35
  24.5 4.2 %collective-permute-done.1 = bf16[32,4608]{1,0:T(8,128)(2,1)S(1)} collective-permute-done((bf16[32,4608]{1,0:T(8,128)(2,1)S(1)}, bf16[32,4608]{1,0:T(8,128)(2,1)S(1)}, u32[]{:S(2)}, u32[]{:S(2)}) %collective-permute-start.1) | collective-permute-done | bytes 294944 | tf_op jit(solution)/shard_map/ppermute | solution.py:35
  36.2 2.2 collective-permute-start.10
  39.9 2.7 %collective-permute-start.4 = (bf16[8,4608]{1,0:T(8,128)(2,1)S(1)}, bf16[8,4608]{1,0:T(8,128)(2,1)S(1)}, u32[]{:S(2)}, u32[]{:S(2)}) collective-permute-start(bf16[8,4608]{1,0:T(8,128)(2,1)S(1)} %fusion.11), channel_id=1, source_target_pairs={{0,8},{1,9},{2,10},{3,11},{4,12},{5,13},{6,14},{7,15},{8,0},{9,1},... | collective-permute-start | bytes 221192 | tf_op jit(solution)/shard_map/ppermute | solution.py:35
  45.9 2.7 %collective-permute-done.4 = bf16[8,4608]{1,0:T(8,128)(2,1)S(1)} collective-permute-done((bf16[8,4608]{1,0:T(8,128)(2,1)S(1)}, bf16[8,4608]{1,0:T(8,128)(2,1)S(1)}, u32[]{:S(2)}, u32[]{:S(2)}) %collective-permute-start.4) | collective-permute-done | bytes 73760 | tf_op jit(solution)/shard_map/ppermute | solution.py:35
  59.4 2.6 %collective-permute-done.20 = bf16[16,5120]{1,0:T(8,128)(2,1)S(1)} collective-permute-done((bf16[16,5120]{1,0:T(8,128)(2,1)S(1)}, bf16[16,5120]{1,0:T(8,128)(2,1)S(1)}, u32[]{:S(2)}, u32[]{:S(2)}) %collective-permute-start.20) | collective-permute-done | bytes 163872 | tf_op jit(solution)/shard_map/ppermute | solution.py:35
  65.1 4.7 %collective-permute-done.14.refs_3_.refs_5_ = bf16[32,4608]{1,0:T(8,128)(2,1)S(1)} collective-permute-done((bf16[32,4608]{1,0:T(8,128)(2,1)S(1)}, bf16[32,4608]{1,0:T(8,128)(2,1)S(1)}, u32[]{:S(2)}, u32[]{:S(2)}) %collective-permute-start.14) | collective-permute-done | bytes 294944 | tf_op jit(solution)/shard_map/ppermute | solution.py:35
  72.1 4.6 %update.3 = (f32[64,14336]{1,0:T(8,128)S(1)}, f32[64,14336]{1,0:T(8,128)S(1)}, f32[64,256]{1,0:T(8,128)S(1)}) custom-call(f32[8,128]{1,0:T(8,128)S(1)} %square.4.refs_0_, f32[8,128]{1,0:T(8,128)S(1)} %collective-permute-done.22.refs_1_, bf16[32,4608]{1,0:T(8,128)(2,1)S(1)} %pad_maximum_fusion.4.refs_0_.refs_2_, ...), custom_call_target="tpu_custom_call" | custom-call | tf_op jit(solution)/shard_map/update/pallas_call | solution.py:272
  78.0 3.1 %gradient.5 = (f32[32,4608]{1,0:T(8,128)S(1)}, bf16[32,4608]{1,0:T(8,128)(2,1)S(1)}, f32[32,4608]{1,0:T(8,128)S(1)}, bf16[32,4608]{1,0:T(8,128)(2,1)S(1)}, f32[3...) custom-call(f32[64,256]{1,0:T(8,128)S(1)} %get-tuple-element.48.own_ref, ...), custom_call_target="tpu_custom_call" | custom-call | tf_op jit(solution)/shard_map/gradient/pallas_call | solution.py:253
  84.6 5.6 %collective-permute-done.24 = bf16[32,4608]{1,0:T(8,128)(2,1)S(1)} collective-permute-done((bf16[32,4608]{1,0:T(8,128)(2,1)S(1)}, bf16[32,4608]{1,0:T(8,128)(2,1)S(1)}, u32[]{:S(2)}, u32[]{:S(2)}) %collective-permute-start.24) | collective-permute-done | bytes 294944 | tf_op jit(solution)/shard_map/ppermute | solution.py:35
  100.0 4.3 %collective-permute-start.27 = (bf16[8,4608]{1,0:T(8,128)(2,1)S(1)}, bf16[8,4608]{1,0:T(8,128)(2,1)S(1)}, u32[]{:S(2)}, u32[]{:S(2)}) collective-permute-start(bf16[8,4608]{1,0:T(8,128)(2,1)S(1)} %fusion.9), channel_id=1, source_target_pairs={{0,8},{1,9},{2,10},{3,11},{4,12},{5,13},{6,14},{7,15},{8,0},{9,1},... | collective-permute-start | bytes 221192 | tf_op jit(solution)/shard_map/ppermute | solution.py:35
  107.5 2.3 collective-permute-done.27
  120.9 3.6 %collective-permute-done.43 = bf16[16,5120]{1,0:T(8,128)(2,1)S(1)} collective-permute-done((bf16[16,5120]{1,0:T(8,128)(2,1)S(1)}, bf16[16,5120]{1,0:T(8,128)(2,1)S(1)}, u32[]{:S(2)}, u32[]{:S(2)}) %collective-permute-start.43) | collective-permute-done | bytes 163872 | tf_op jit(solution)/shard_map/ppermute | solution.py:35
  127.7 3.8 %collective-permute-done.37.refs_3_.refs_5_ = bf16[32,4608]{1,0:T(8,128)(2,1)S(1)} collective-permute-done((bf16[32,4608]{1,0:T(8,128)(2,1)S(1)}, bf16[32,4608]{1,0:T(8,128)(2,1)S(1)}, u32[]{:S(2)}, u32[]{:S(2)}) %collective-permute-start.37) | collective-permute-done | bytes 294944 | tf_op jit(solution)/shard_map/ppermute | solution.py:35
  134.0 4.5 %update.4 = (f32[64,14336]{1,0:T(8,128)S(1)}, f32[64,14336]{1,0:T(8,128)S(1)}, f32[64,256]{1,0:T(8,128)S(1)}) custom-call(f32[8,128]{1,0:T(8,128)S(1)} %square.5.refs_0_, f32[8,128]{1,0:T(8,128)S(1)} %collective-permute-done.45.refs_1_, bf16[32,4608]{1,0:T(8,128)(2,1)S(1)} %pad_maximum_fusion.6.refs_0_.refs_2_, ...), custom_call_target="tpu_custom_call" | custom-call | tf_op jit(solution)/shard_map/update/pallas_call | solution.py:272
  139.9 3.1 %gradient.6 = (f32[32,4608]{1,0:T(8,128)S(1)}, bf16[32,4608]{1,0:T(8,128)(2,1)S(1)}, f32[32,4608]{1,0:T(8,128)S(1)}, bf16[32,4608]{1,0:T(8,128)(2,1)S(1)}, f32[3...) custom-call(f32[64,256]{1,0:T(8,128)S(1)} %get-tuple-element.57.own_ref, ...), custom_call_target="tpu_custom_call" | custom-call | tf_op jit(solution)/shard_map/gradient/pallas_call | solution.py:253
  147.3 4.8 %collective-permute-done.47 = bf16[32,4608]{1,0:T(8,128)(2,1)S(1)} collective-permute-done((bf16[32,4608]{1,0:T(8,128)(2,1)S(1)}, bf16[32,4608]{1,0:T(8,128)(2,1)S(1)}, u32[]{:S(2)}, u32[]{:S(2)}) %collective-permute-start.47) | collective-permute-done | bytes 294944 | tf_op jit(solution)/shard_map/ppermute | solution.py:35
  166.8 4.0 %collective-permute-done.50 = bf16[8,4608]{1,0:T(8,128)(2,1)S(1)} collective-permute-done((bf16[8,4608]{1,0:T(8,128)(2,1)S(1)}, bf16[8,4608]{1,0:T(8,128)(2,1)S(1)}, u32[]{:S(2)}, u32[]{:S(2)}) %collective-permute-start.50) | collective-permute-done | bytes 73760 | tf_op jit(solution)/shard_map/ppermute | solution.py:35
  187.4 4.0 %collective-permute-done.60.refs_3_.refs_5_ = bf16[32,4608]{1,0:T(8,128)(2,1)S(1)} collective-permute-done((bf16[32,4608]{1,0:T(8,128)(2,1)S(1)}, bf16[32,4608]{1,0:T(8,128)(2,1)S(1)}, u32[]{:S(2)}, u32[]{:S(2)}) %collective-permute-start.60) | collective-permute-done | bytes 294944 | tf_op jit(solution)/shard_map/ppermute | solution.py:35
  193.6 4.6 %update.5 = (f32[64,14336]{1,0:T(8,128)S(1)}, f32[64,14336]{1,0:T(8,128)S(1)}, f32[64,256]{1,0:T(8,128)S(1)}) custom-call(f32[8,128]{1,0:T(8,128)S(1)} %square.6.refs_0_, f32[8,128]{1,0:T(8,128)S(1)} %collective-permute-done.68.refs_1_, bf16[32,4608]{1,0:T(8,128)(2,1)S(1)} %pad_maximum_fusion.8.refs_0_.refs_2_, ...), custom_call_target="tpu_custom_call" | custom-call | tf_op jit(solution)/shard_map/update/pallas_call | solution.py:272
  199.5 3.2 %gradient.7 = (f32[32,4608]{1,0:T(8,128)S(1)}, bf16[32,4608]{1,0:T(8,128)(2,1)S(1)}, f32[32,4608]{1,0:T(8,128)S(1)}, bf16[32,4608]{1,0:T(8,128)(2,1)S(1)}, f32[3...) custom-call(f32[64,256]{1,0:T(8,128)S(1)} %get-tuple-element.66.own_ref, ...), custom_call_target="tpu_custom_call" | custom-call | tf_op jit(solution)/shard_map/gradient/pallas_call | solution.py:253
  206.3 5.6 %collective-permute-done.70 = bf16[32,4608]{1,0:T(8,128)(2,1)S(1)} collective-permute-done((bf16[32,4608]{1,0:T(8,128)(2,1)S(1)}, bf16[32,4608]{1,0:T(8,128)(2,1)S(1)}, u32[]{:S(2)}, u32[]{:S(2)}) %collective-permute-start.70) | collective-permute-done | bytes 294944 | tf_op jit(solution)/shard_map/ppermute | solution.py:35
  221.7 3.3 %collective-permute-start.73 = (bf16[8,4608]{1,0:T(8,128)(2,1)S(1)}, bf16[8,4608]{1,0:T(8,128)(2,1)S(1)}, u32[]{:S(2)}, u32[]{:S(2)}) collective-permute-start(bf16[8,4608]{1,0:T(8,128)(2,1)S(1)} %fusion.5), channel_id=1, source_target_pairs={{0,8},{1,9},{2,10},{3,11},{4,12},{5,13},{6,14},{7,15},{8,0},{9,1},... | collective-permute-start | bytes 221192 | tf_op jit(solution)/shard_map/ppermute | solution.py:35
  228.2 2.4 collective-permute-done.73
  240.6 2.4 collective-permute-start.76
  243.0 2.3 collective-permute-done.89
  248.4 3.9 %collective-permute-done.83.refs_3_.refs_6_ = bf16[32,4608]{1,0:T(8,128)(2,1)S(1)} collective-permute-done((bf16[32,4608]{1,0:T(8,128)(2,1)S(1)}, bf16[32,4608]{1,0:T(8,128)(2,1)S(1)}, u32[]{:S(2)}, u32[]{:S(2)}) %collective-permute-start.83) | collective-permute-done | bytes 294944 | tf_op jit(solution)/shard_map/ppermute | solution.py:35
  254.7 2.9 %last.1 = f32[64,14336]{1,0:T(8,128)} custom-call(s32[1]{0:T(128)} %bitcast.mask_ref.refs_0_, f32[8,128]{1,0:T(8,128)S(1)} %square.7.refs_1_, f32[8,128]{1,0:T(8,128)S(1)} %collective-permute-done.91.refs_2_, bf16[32,4608]{1,0:T(8,128)(2,1)S(1)} %pad_maximum_fusion.10.refs_0_.refs_3_, bf16[32,4608]{1,0:T(8,128)(2,1)S(1)} %collective-permute-done.76.refs_1_.refs_4_, ...), custom_call_target="tpu_custom_call" | custom-call | tf_op jit(solution)/shard_map/last/pallas_call | solution.py:281
  (281 shorter events, 143.4 us)
Async XLA Ops:
  18.5 10.2 %collective-permute-start.1 = (bf16[32,4608]{1,0:T(8,128)(2,1)S(1)}, bf16[32,4608]{1,0:T(8,128)(2,1)S(1)}, u32[]{:S(2)}, u32[]{:S(2)}) collective-permute-start(bf16[32,4608]{1,0:T(8,128)(2,1)S(1)} %get-tuple-element.42), channel_id=1, source_target_pairs={{0,1},{1,0},{2,3},{3,2},{4,5},{5,4},{6,7},{7,6},{8,9},{9,8},{10,11... | collective-permute-start | bytes 884744 | tf_op jit(solution)/shard_map/ppermute | solution.py:35
  21.4 9.2 %collective-permute-start.8 = (bf16[32,4608]{1,0:T(8,128)(2,1)S(1)}, bf16[32,4608]{1,0:T(8,128)(2,1)S(1)}, u32[]{:S(2)}, u32[]{:S(2)}) collective-permute-start(bf16[32,4608]{1,0:T(8,128)(2,1)S(1)} %get-tuple-element.44), channel_id=1, source_target_pairs={{0,2},{1,3},{2,0},{3,1},{4,6},{5,7},{6,4},{7,5},{8,10},{9,11},{10,... | collective-permute-start | bytes 884744 | tf_op jit(solution)/shard_map/ppermute | solution.py:35
  22.9 9.5 %collective-permute-start.15 = (bf16[32,5120]{1,0:T(8,128)(2,1)S(1)}, bf16[32,5120]{1,0:T(8,128)(2,1)S(1)}, u32[]{:S(2)}, u32[]{:S(2)}) collective-permute-start(bf16[32,5120]{1,0:T(8,128)(2,1)S(1)} %get-tuple-element.46), channel_id=1, source_target_pairs={{0,4},{1,5},{2,6},{3,7},{4,0},{5,1},{6,2},{7,3},{8,12},{9,13},{10,... | collective-permute-start | bytes 983048 | tf_op jit(solution)/shard_map/ppermute | solution.py:35
  39.9 8.8 %collective-permute-start.4 = (bf16[8,4608]{1,0:T(8,128)(2,1)S(1)}, bf16[8,4608]{1,0:T(8,128)(2,1)S(1)}, u32[]{:S(2)}, u32[]{:S(2)}) collective-permute-start(bf16[8,4608]{1,0:T(8,128)(2,1)S(1)} %fusion.11), channel_id=1, source_target_pairs={{0,8},{1,9},{2,10},{3,11},{4,12},{5,13},{6,14},{7,15},{8,0},{9,1},... | collective-permute-start | bytes 221192 | tf_op jit(solution)/shard_map/ppermute | solution.py:35
  43.9 7.4 %collective-permute-start.18 = (bf16[8,5120]{1,0:T(8,128)(2,1)S(1)}, bf16[8,5120]{1,0:T(8,128)(2,1)S(1)}, u32[]{:S(2)}, u32[]{:S(2)}) collective-permute-start(bf16[8,5120]{1,0:T(8,128)(2,1)S(1)} %fusion.3), channel_id=1, source_target_pairs={{0,8},{1,9},{2,10},{3,11},{4,12},{5,13},{6,14},{7,15},{8,0},{9,1},... | collective-permute-start | bytes 245768 | tf_op jit(solution)/shard_map/ppermute | solution.py:35
  54.2 8.8 %collective-permute-start.13 = (bf16[16,4608]{1,0:T(8,128)(2,1)S(1)}, bf16[16,4608]{1,0:T(8,128)(2,1)S(1)}, u32[]{:S(2)}, u32[]{:S(2)}) collective-permute-start(bf16[16,4608]{1,0:T(8,128)(2,1)S(1)} %pad_maximum_fusion.17), channel_id=1, source_target_pairs={{0,4},{1,5},{2,6},{3,7},{4,0},{5,1},{6,2},{7,3},{8,12},{9,13},{10,... | collective-permute-start | bytes 442376 | tf_op jit(solution)/shard_map/ppermute | solution.py:35
  62.0 7.8 %collective-permute-start.21 = (bf16[32,5120]{1,0:T(8,128)(2,1)S(1)}, bf16[32,5120]{1,0:T(8,128)(2,1)S(1)}, u32[]{:S(2)}, u32[]{:S(2)}) collective-permute-start(bf16[32,5120]{1,0:T(8,128)(2,1)S(1)} %pad_maximum_fusion.refs_4_.refs_6_), channel_id=1, source_target_pairs={{0,4},{1,5},{2,6},{3,7},{4,0},{5,1},{6,2},{7,3},{8,12},{9,13},{10,... | collective-permute-start | bytes 983048 | tf_op jit(solution)/shard_map/ppermute | solution.py:35
  81.1 9.1 %collective-permute-start.24 = (bf16[32,4608]{1,0:T(8,128)(2,1)S(1)}, bf16[32,4608]{1,0:T(8,128)(2,1)S(1)}, u32[]{:S(2)}, u32[]{:S(2)}) collective-permute-start(bf16[32,4608]{1,0:T(8,128)(2,1)S(1)} %get-tuple-element.50), channel_id=1, source_target_pairs={{0,1},{1,0},{2,3},{3,2},{4,5},{5,4},{6,7},{7,6},{8,9},{9,8},{10,11... | collective-permute-start | bytes 884744 | tf_op jit(solution)/shard_map/ppermute | solution.py:35
  82.3 9.3 %collective-permute-start.31 = (bf16[32,4608]{1,0:T(8,128)(2,1)S(1)}, bf16[32,4608]{1,0:T(8,128)(2,1)S(1)}, u32[]{:S(2)}, u32[]{:S(2)}) collective-permute-start(bf16[32,4608]{1,0:T(8,128)(2,1)S(1)} %get-tuple-element.52), channel_id=1, source_target_pairs={{0,2},{1,3},{2,0},{3,1},{4,6},{5,7},{6,4},{7,5},{8,10},{9,11},{10,... | collective-permute-start | bytes 884744 | tf_op jit(solution)/shard_map/ppermute | solution.py:35
  83.1 9.7 %collective-permute-start.38 = (bf16[32,5120]{1,0:T(8,128)(2,1)S(1)}, bf16[32,5120]{1,0:T(8,128)(2,1)S(1)}, u32[]{:S(2)}, u32[]{:S(2)}) collective-permute-start(bf16[32,5120]{1,0:T(8,128)(2,1)S(1)} %get-tuple-element.54), channel_id=1, source_target_pairs={{0,4},{1,5},{2,6},{3,7},{4,0},{5,1},{6,2},{7,3},{8,12},{9,13},{10,... | collective-permute-start | bytes 983048 | tf_op jit(solution)/shard_map/ppermute | solution.py:35
  100.0 9.7 %collective-permute-start.27 = (bf16[8,4608]{1,0:T(8,128)(2,1)S(1)}, bf16[8,4608]{1,0:T(8,128)(2,1)S(1)}, u32[]{:S(2)}, u32[]{:S(2)}) collective-permute-start(bf16[8,4608]{1,0:T(8,128)(2,1)S(1)} %fusion.9), channel_id=1, source_target_pairs={{0,8},{1,9},{2,10},{3,11},{4,12},{5,13},{6,14},{7,15},{8,0},{9,1},... | collective-permute-start | bytes 221192 | tf_op jit(solution)/shard_map/ppermute | solution.py:35
  104.4 7.6 %collective-permute-start.34 = (bf16[8,4608]{1,0:T(8,128)(2,1)S(1)}, bf16[8,4608]{1,0:T(8,128)(2,1)S(1)}, u32[]{:S(2)}, u32[]{:S(2)}) collective-permute-start(bf16[8,4608]{1,0:T(8,128)(2,1)S(1)} %fusion.8), channel_id=1, source_target_pairs={{0,8},{1,9},{2,10},{3,11},{4,12},{5,13},{6,14},{7,15},{8,0},{9,1},... | collective-permute-start | bytes 221192 | tf_op jit(solution)/shard_map/ppermute | solution.py:35
  105.6 7.7 %collective-permute-start.41 = (bf16[8,5120]{1,0:T(8,128)(2,1)S(1)}, bf16[8,5120]{1,0:T(8,128)(2,1)S(1)}, u32[]{:S(2)}, u32[]{:S(2)}) collective-permute-start(bf16[8,5120]{1,0:T(8,128)(2,1)S(1)} %fusion.2), channel_id=1, source_target_pairs={{0,8},{1,9},{2,10},{3,11},{4,12},{5,13},{6,14},{7,15},{8,0},{9,1},... | collective-permute-start | bytes 245768 | tf_op jit(solution)/shard_map/ppermute | solution.py:35
  116.4 8.3 %collective-permute-start.36 = (bf16[16,4608]{1,0:T(8,128)(2,1)S(1)}, bf16[16,4608]{1,0:T(8,128)(2,1)S(1)}, u32[]{:S(2)}, u32[]{:S(2)}) collective-permute-start(bf16[16,4608]{1,0:T(8,128)(2,1)S(1)} %pad_maximum_fusion.19), channel_id=1, source_target_pairs={{0,4},{1,5},{2,6},{3,7},{4,0},{5,1},{6,2},{7,3},{8,12},{9,13},{10,... | collective-permute-start | bytes 442376 | tf_op jit(solution)/shard_map/ppermute | solution.py:35
  119.6 8.1 %collective-permute-start.30 = (bf16[32,4608]{1,0:T(8,128)(2,1)S(1)}, bf16[32,4608]{1,0:T(8,128)(2,1)S(1)}, u32[]{:S(2)}, u32[]{:S(2)}) collective-permute-start(bf16[32,4608]{1,0:T(8,128)(2,1)S(1)} %pad_maximum_fusion.6.refs_0_.refs_2_), channel_id=1, source_target_pairs={{0,1},{1,0},{2,3},{3,2},{4,5},{5,4},{6,7},{7,6},{8,9},{9,8},{10,11... | collective-permute-start | bytes 884744 | tf_op jit(solution)/shard_map/ppermute | solution.py:35
  142.9 9.1 %collective-permute-start.47 = (bf16[32,4608]{1,0:T(8,128)(2,1)S(1)}, bf16[32,4608]{1,0:T(8,128)(2,1)S(1)}, u32[]{:S(2)}, u32[]{:S(2)}) collective-permute-start(bf16[32,4608]{1,0:T(8,128)(2,1)S(1)} %get-tuple-element.59), channel_id=1, source_target_pairs={{0,1},{1,0},{2,3},{3,2},{4,5},{5,4},{6,7},{7,6},{8,9},{9,8},{10,11... | collective-permute-start | bytes 884744 | tf_op jit(solution)/shard_map/ppermute | solution.py:35
  144.4 8.8 %collective-permute-start.54 = (bf16[32,4608]{1,0:T(8,128)(2,1)S(1)}, bf16[32,4608]{1,0:T(8,128)(2,1)S(1)}, u32[]{:S(2)}, u32[]{:S(2)}) collective-permute-start(bf16[32,4608]{1,0:T(8,128)(2,1)S(1)} %get-tuple-element.61), channel_id=1, source_target_pairs={{0,2},{1,3},{2,0},{3,1},{4,6},{5,7},{6,4},{7,5},{8,10},{9,11},{10,... | collective-permute-start | bytes 884744 | tf_op jit(solution)/shard_map/ppermute | solution.py:35
  145.5 9.6 %collective-permute-start.61 = (bf16[32,5120]{1,0:T(8,128)(2,1)S(1)}, bf16[32,5120]{1,0:T(8,128)(2,1)S(1)}, u32[]{:S(2)}, u32[]{:S(2)}) collective-permute-start(bf16[32,5120]{1,0:T(8,128)(2,1)S(1)} %get-tuple-element.63), channel_id=1, source_target_pairs={{0,4},{1,5},{2,6},{3,7},{4,0},{5,1},{6,2},{7,3},{8,12},{9,13},{10,... | collective-permute-start | bytes 983048 | tf_op jit(solution)/shard_map/ppermute | solution.py:35
  162.7 8.1 %collective-permute-start.50 = (bf16[8,4608]{1,0:T(8,128)(2,1)S(1)}, bf16[8,4608]{1,0:T(8,128)(2,1)S(1)}, u32[]{:S(2)}, u32[]{:S(2)}) collective-permute-start(bf16[8,4608]{1,0:T(8,128)(2,1)S(1)} %fusion.7), channel_id=1, source_target_pairs={{0,8},{1,9},{2,10},{3,11},{4,12},{5,13},{6,14},{7,15},{8,0},{9,1},... | collective-permute-start | bytes 221192 | tf_op jit(solution)/shard_map/ppermute | solution.py:35
  163.8 8.7 %collective-permute-start.57 = (bf16[8,4608]{1,0:T(8,128)(2,1)S(1)}, bf16[8,4608]{1,0:T(8,128)(2,1)S(1)}, u32[]{:S(2)}, u32[]{:S(2)}) collective-permute-start(bf16[8,4608]{1,0:T(8,128)(2,1)S(1)} %fusion.6), channel_id=1, source_target_pairs={{0,8},{1,9},{2,10},{3,11},{4,12},{5,13},{6,14},{7,15},{8,0},{9,1},... | collective-permute-start | bytes 221192 | tf_op jit(solution)/shard_map/ppermute | solution.py:35
  166.0 7.4 %collective-permute-start.64 = (bf16[8,5120]{1,0:T(8,128)(2,1)S(1)}, bf16[8,5120]{1,0:T(8,128)(2,1)S(1)}, u32[]{:S(2)}, u32[]{:S(2)}) collective-permute-start(bf16[8,5120]{1,0:T(8,128)(2,1)S(1)} %fusion.1), channel_id=1, source_target_pairs={{0,8},{1,9},{2,10},{3,11},{4,12},{5,13},{6,14},{7,15},{8,0},{9,1},... | collective-permute-start | bytes 245768 | tf_op jit(solution)/shard_map/ppermute | solution.py:35
  177.0 7.6 %collective-permute-start.59 = (bf16[16,4608]{1,0:T(8,128)(2,1)S(1)}, bf16[16,4608]{1,0:T(8,128)(2,1)S(1)}, u32[]{:S(2)}, u32[]{:S(2)}) collective-permute-start(bf16[16,4608]{1,0:T(8,128)(2,1)S(1)} %pad_maximum_fusion.21), channel_id=1, source_target_pairs={{0,4},{1,5},{2,6},{3,7},{4,0},{5,1},{6,2},{7,3},{8,12},{9,13},{10,... | collective-permute-start | bytes 442376 | tf_op jit(solution)/shard_map/ppermute | solution.py:35
  183.7 7.7 %collective-permute-start.67 = (bf16[32,5120]{1,0:T(8,128)(2,1)S(1)}, bf16[32,5120]{1,0:T(8,128)(2,1)S(1)}, u32[]{:S(2)}, u32[]{:S(2)}) collective-permute-start(bf16[32,5120]{1,0:T(8,128)(2,1)S(1)} %pad_maximum_fusion.2.refs_4_.refs_6_), channel_id=1, source_target_pairs={{0,4},{1,5},{2,6},{3,7},{4,0},{5,1},{6,2},{7,3},{8,12},{9,13},{10,... | collective-permute-start | bytes 983048 | tf_op jit(solution)/shard_map/ppermute | solution.py:35
  202.8 9.2 %collective-permute-start.70 = (bf16[32,4608]{1,0:T(8,128)(2,1)S(1)}, bf16[32,4608]{1,0:T(8,128)(2,1)S(1)}, u32[]{:S(2)}, u32[]{:S(2)}) collective-permute-start(bf16[32,4608]{1,0:T(8,128)(2,1)S(1)} %get-tuple-element.68), channel_id=1, source_target_pairs={{0,1},{1,0},{2,3},{3,2},{4,5},{5,4},{6,7},{7,6},{8,9},{9,8},{10,11... | collective-permute-start | bytes 884744 | tf_op jit(solution)/shard_map/ppermute | solution.py:35
  203.9 9.3 %collective-permute-start.77 = (bf16[32,4608]{1,0:T(8,128)(2,1)S(1)}, bf16[32,4608]{1,0:T(8,128)(2,1)S(1)}, u32[]{:S(2)}, u32[]{:S(2)}) collective-permute-start(bf16[32,4608]{1,0:T(8,128)(2,1)S(1)} %get-tuple-element.70), channel_id=1, source_target_pairs={{0,2},{1,3},{2,0},{3,1},{4,6},{5,7},{6,4},{7,5},{8,10},{9,11},{10,... | collective-permute-start | bytes 884744 | tf_op jit(solution)/shard_map/ppermute | solution.py:35
  204.8 9.6 %collective-permute-start.84 = (bf16[32,5120]{1,0:T(8,128)(2,1)S(1)}, bf16[32,5120]{1,0:T(8,128)(2,1)S(1)}, u32[]{:S(2)}, u32[]{:S(2)}) collective-permute-start(bf16[32,5120]{1,0:T(8,128)(2,1)S(1)} %get-tuple-element.72), channel_id=1, source_target_pairs={{0,4},{1,5},{2,6},{3,7},{4,0},{5,1},{6,2},{7,3},{8,12},{9,13},{10,... | collective-permute-start | bytes 983048 | tf_op jit(solution)/shard_map/ppermute | solution.py:35
  221.7 8.8 %collective-permute-start.73 = (bf16[8,4608]{1,0:T(8,128)(2,1)S(1)}, bf16[8,4608]{1,0:T(8,128)(2,1)S(1)}, u32[]{:S(2)}, u32[]{:S(2)}) collective-permute-start(bf16[8,4608]{1,0:T(8,128)(2,1)S(1)} %fusion.5), channel_id=1, source_target_pairs={{0,8},{1,9},{2,10},{3,11},{4,12},{5,13},{6,14},{7,15},{8,0},{9,1},... | collective-permute-start | bytes 221192 | tf_op jit(solution)/shard_map/ppermute | solution.py:35
  225.0 7.7 %collective-permute-start.80 = (bf16[8,4608]{1,0:T(8,128)(2,1)S(1)}, bf16[8,4608]{1,0:T(8,128)(2,1)S(1)}, u32[]{:S(2)}, u32[]{:S(2)}) collective-permute-start(bf16[8,4608]{1,0:T(8,128)(2,1)S(1)} %fusion.4), channel_id=1, source_target_pairs={{0,8},{1,9},{2,10},{3,11},{4,12},{5,13},{6,14},{7,15},{8,0},{9,1},... | collective-permute-start | bytes 221192 | tf_op jit(solution)/shard_map/ppermute | solution.py:35
  226.5 7.7 %collective-permute-start.87 = (bf16[8,5120]{1,0:T(8,128)(2,1)S(1)}, bf16[8,5120]{1,0:T(8,128)(2,1)S(1)}, u32[]{:S(2)}, u32[]{:S(2)}) collective-permute-start(bf16[8,5120]{1,0:T(8,128)(2,1)S(1)} %fusion), channel_id=1, source_target_pairs={{0,8},{1,9},{2,10},{3,11},{4,12},{5,13},{6,14},{7,15},{8,0},{9,1},... | collective-permute-start | bytes 245768 | tf_op jit(solution)/shard_map/ppermute | solution.py:35
  237.1 8.3 %collective-permute-start.82 = (bf16[16,4608]{1,0:T(8,128)(2,1)S(1)}, bf16[16,4608]{1,0:T(8,128)(2,1)S(1)}, u32[]{:S(2)}, u32[]{:S(2)}) collective-permute-start(bf16[16,4608]{1,0:T(8,128)(2,1)S(1)} %pad_maximum_fusion.23), channel_id=1, source_target_pairs={{0,4},{1,5},{2,6},{3,7},{4,0},{5,1},{6,2},{7,3},{8,12},{9,13},{10,... | collective-permute-start | bytes 442376 | tf_op jit(solution)/shard_map/ppermute | solution.py:35
  240.6 7.8 %collective-permute-start.76 = (bf16[32,4608]{1,0:T(8,128)(2,1)S(1)}, bf16[32,4608]{1,0:T(8,128)(2,1)S(1)}, u32[]{:S(2)}, u32[]{:S(2)}) collective-permute-start(bf16[32,4608]{1,0:T(8,128)(2,1)S(1)} %pad_maximum_fusion.10.refs_0_.refs_3_), channel_id=1, source_target_pairs={{0,1},{1,0},{2,3},{3,2},{4,5},{5,4},{6,7},{7,6},{8,9},{9,8},{10,11... | collective-permute-start | bytes 884744 | tf_op jit(solution)/shard_map/ppermute | solution.py:35
  245.3 7.1 %collective-permute-start.90 = (bf16[32,5120]{1,0:T(8,128)(2,1)S(1)}, bf16[32,5120]{1,0:T(8,128)(2,1)S(1)}, u32[]{:S(2)}, u32[]{:S(2)}) collective-permute-start(bf16[32,5120]{1,0:T(8,128)(2,1)S(1)} %pad_maximum_fusion.3.refs_4_.refs_7_), channel_id=1, source_target_pairs={{0,4},{1,5},{2,6},{3,7},{4,0},{5,1},{6,2},{7,3},{8,12},{9,13},{10,... | collective-permute-start | bytes 983048 | tf_op jit(solution)/shard_map/ppermute | solution.py:35
  (68 other events, 449.1 us)

commit v2 on v0

v2 whole, which is shorter than its diff:
```python
import functools
import math

import jax
import jax.numpy as jnp
from jax import lax
from jax.experimental import pallas as pl
from jax.experimental.pallas import tpu as pltpu
from jax.sharding import PartitionSpec as P

ITERS = 4
STEP = 0.25
THRESHOLD = 0.2
EPSILON = 1e-06
GROUP = 8
SHARES = (20, 19, 17)
PARTS = len(SHARES)
LANES = 128
VMEM_BYTES = 4 * 1024 * 1024

f32 = jnp.float32
bf16 = jnp.bfloat16


def momentum_terms(iterations):
    values = []
    current = 1.0
    for _ in range(iterations):
        upcoming = (1.0 + math.sqrt(1.0 + 4.0 * current * current)) / 2.0
        values.append((current - 1.0) / upcoming)
        current = upcoming
    return values


def swap(x, axis, bit):
    pairs = [(i, i ^ (1 << bit)) for i in range(lax.axis_size(axis))]
    return lax.ppermute(x, axis, pairs)


def bits_of(axis):
    return lax.axis_size(axis).bit_length() - 1


class Plan:
    def __init__(self, rows, columns, tokens):
        self.rows = rows
        self.columns = columns
        self.tokens = tokens
        self.rows_bits = min(bits_of("tok"), (rows // GROUP).bit_length() - 1)
        self.places = 1 << self.rows_bits
        self.height = rows >> self.rows_bits
        self.unit = next(u for u in (256, 128) if columns % u == 0)
        units = columns // self.unit
        self.entries = rows * columns * lax.axis_size("feat")
        self.factor = (columns * lax.axis_size("feat")) ** (-0.5)
        marks = [0]
        for share in SHARES:
            marks.append(marks[-1] + share)
        edges = [self.unit * round(units * m / marks[-1]) for m in marks]
        self.spans = list(zip(edges[:-1], edges[1:]))
        self.widths = [b - a for a, b in self.spans]
        self.orders = [[(p + s) % self.rows_bits for s in range(self.rows_bits)] for p in range(PARTS)]

    def blocks(self, p):
        a, b = self.spans[p]
        return [(slice(x - a, x - a + self.unit), slice(x, x + self.unit)) for x in range(a, b, self.unit)]

    def bit_value(self, level):
        return self.places >> (level + 1)

    def arrangement(self, p):
        result = [0]
        for level in reversed(self.orders[p]):
            result = result + [g + self.bit_value(level) for g in result]
        return result

    def mask(self):
        index = lax.axis_index("tok")
        return sum(((index >> level) & 1) * self.bit_value(level) for level in range(self.rows_bits))

    def rearranged(self, x, places):
        h = self.height
        return jnp.concatenate([x[h * g : h * (g + 1)] for g in places], 0)

    def to_part(self, p, x):
        return self.rearranged(x, self.arrangement(p))

    def from_part(self, p, x):
        order = self.arrangement(p)
        return self.rearranged(x, [order.index(g) for g in range(self.places)])


def dot_nt(a, b):
    return lax.dot_general(a, b, (((1,), (1,)), ((), ())), preferred_element_type=f32)


VMEM = pl.BlockSpec(memory_space=pltpu.VMEM)
SMEM = pl.BlockSpec(memory_space=pltpu.SMEM)


def run(kernel, name, outs, specs, args):
    return pl.pallas_call(
        kernel,
        out_shape=tuple(jax.ShapeDtypeStruct(shape, dtype) for shape, dtype in outs),
        in_specs=list(specs),
        out_specs=(VMEM,) * len(outs),
        compiler_params=pltpu.CompilerParams(vmem_limit_bytes=VMEM_BYTES),
        name=name,
    )(*args)


def first_kernel(plan, mask_ref, dense_ref, act_ref, *refs):
    *start_refs, product_ref = refs
    h = plan.height
    total = jnp.zeros(product_ref.shape, f32)
    for p, (a, b) in enumerate(plan.spans):
        for start in range(a, b, plan.unit):
            groups = []
            for g in range(plan.places):
                rows = pl.ds(pl.multiple_of((g ^ mask_ref[0]) * h, h), h)
                groups.append(dense_ref[rows, start : start + plan.unit])
            block = jnp.concatenate(groups, 0)
            start_refs[p][:, start - a : start - a + plan.unit] = block
            total = total + dot_nt(block.astype(bf16), act_ref[:, start : start + plan.unit])
    product_ref[...] = total


def gradient_kernel(plan, p, own_ref, other_ref, wanted_ref, act_ref, keep_ref, send_ref):
    residual = plan.factor * (own_ref[...] + other_ref[...]) - wanted_ref[...]
    half = plan.rows // 2
    arranged = plan.to_part(p, residual).astype(bf16)

    for here, there in plan.blocks(p):
        block = jnp.dot(arranged, act_ref[:, there], preferred_element_type=f32)
        keep_ref[:, here] = block[:half]
        send_ref[:, here] = block[half:].astype(bf16)


def pair_tile(value, rows):
    value = jnp.broadcast_to(value, (rows, LANES))
    high = value.astype(bf16).astype(f32)
    lane = lax.broadcasted_iota(jnp.int32, (rows, LANES), 1)
    return jnp.where(lane < LANES // 2, high, value - high).astype(bf16)


def pair_value(tile):
    tile = tile.astype(f32)
    return jnp.sum(tile, keepdims=True) / (tile.shape[0] * (LANES // 2))


def combine_kernel(plan, low_ref, came_ref, *outs):
    h = plan.height
    total = jnp.zeros((h, LANES), f32)
    for p, (a, b) in enumerate(plan.spans):
        for start in range(a, b, plan.unit):
            block = low_ref[:, start : start + plan.unit].astype(f32) + came_ref[:, start : start + plan.unit].astype(f32)
            block = block.astype(bf16)
            outs[p][:, start - a : start - a + plan.unit] = block
            block = block.astype(f32)
            for lane in range(0, plan.unit, LANES):
                piece = block[:, lane : lane + LANES]
                total = total + piece * piece
    outs[0][:, plan.widths[0] :] = pair_tile(jnp.sum(total, keepdims=True), h)


def join_kernel(plan, own_ref, came_ref, out_ref):
    h, width = own_ref.shape
    last = width - LANES
    for start in range(0, last, plan.unit):
        here = slice(start, start + plan.unit)
        out_ref[:, here] = jnp.concatenate([own_ref[:, here].astype(f32), came_ref[:, here].astype(f32)], 0).astype(bf16)
    square = pair_value(own_ref[:, last:]) + pair_value(came_ref[:, last:])
    out_ref[:, last:] = pair_tile(square, 2 * h)


def scale_of(plan, own_ref, other_ref):
    mean_square = pair_value(own_ref[...] + other_ref[...]) / plan.entries
    return STEP * lax.rsqrt(mean_square + EPSILON)


def shrink(plan, p, scale, kept_ref, came_ref, ahead_ref, here):
    gradient = jnp.concatenate([kept_ref[:, here].astype(f32), came_ref[:, here].astype(f32)], 0)
    moved = ahead_ref[:, here] - scale * plan.from_part(p, gradient)
    return moved - jnp.clip(moved, -THRESHOLD, THRESHOLD)


def update_kernel(plan, p, momentum, *refs):
    own_ref, other_ref, kept_ref, came_ref, weights_ref, ahead_ref, act_ref, *refs = refs
    *before, new_weights_ref, new_ahead_ref, product_ref = refs
    scale = scale_of(plan, own_ref, other_ref)
    total = before[0][...] if before else jnp.zeros(product_ref.shape, f32)

    for here, there in plan.blocks(p):
        shrunk = shrink(plan, p, scale, kept_ref, came_ref, ahead_ref, here)
        ahead = shrunk + momentum * (shrunk - weights_ref[:, here])
        new_weights_ref[:, here] = shrunk
        new_ahead_ref[:, here] = ahead
        total = total + dot_nt(ahead.astype(bf16), act_ref[:, there])
    product_ref[...] = total


def last_kernel(plan, mask_ref, own_ref, other_ref, *refs):
    *refs, out_ref = refs
    scale = scale_of(plan, own_ref, other_ref)
    h = plan.height
    for p in range(PARTS):
        kept_ref, came_ref, ahead_ref = refs[3 * p : 3 * p + 3]
        for here, there in plan.blocks(p):
            shrunk = shrink(plan, p, scale, kept_ref, came_ref, ahead_ref, here)
            for g in range(plan.places):
                rows = pl.ds(pl.multiple_of((g ^ mask_ref[0]) * h, h), h)
                out_ref[rows, there] = shrunk[h * g : h * (g + 1)]


def after(x, earlier):
    return lax.optimization_barrier((x, *earlier))[0]


def all_sum(plan, pieces):
    current = [kept for kept, _ in pieces]
    sends = [sent for _, sent in pieces]
    for stage in range(plan.rows_bits):
        came = [swap(sends[p], "tok", plan.orders[p][stage]) for p in range(PARTS)]
        for p in range(PARTS):
            arrived = after(came[p], sends[:p]) if p else came[p]
            whole = current[p] + arrived.astype(f32)
            middle = whole.shape[0] // 2 if stage + 1 < plan.rows_bits else 0
            sends[p] = whole[middle:].astype(bf16)
            current[p] = whole[:middle]
    low = jnp.concatenate(sends, 1)
    came = jnp.zeros_like(low)
    for bit in range(plan.rows_bits, bits_of("tok")):
        if bit > plan.rows_bits:
            low = (low.astype(f32) + came.astype(f32)).astype(bf16)
        came = swap(low, "tok", bit)
    outs = [((plan.height, width + (0 if p else LANES)), bf16) for p, width in enumerate(plan.widths)]
    current = run(functools.partial(combine_kernel, plan), "combine", outs, [VMEM] * 2, (low, came))
    current = list(current)
    for stage in reversed(range(plan.rows_bits)):
        came = [swap(current[p], "tok", plan.orders[p][stage]) for p in range(PARTS)]
        if stage:
            for p in range(PARTS):
                rows, width = current[p].shape
                arrived = after(came[p], current[:p]) if p else came[p]
                if p:
                    current[p] = jnp.concatenate([current[p], arrived], 0)
                else:
                    (current[p],) = run(
                        functools.partial(join_kernel, plan), "join", [((2 * rows, width), bf16)], [VMEM] * 2, (current[p], arrived)
                    )
    return list(zip(current, came))


def across_features(x):
    count = bits_of("feat")
    for bit in range(count - 1):
        x = x + swap(x, "feat", bit)
    return x, swap(x, "feat", count - 1)


def shards(activations, dense_rows, targets):
    rows, columns = dense_rows.shape
    tokens = activations.shape[0]
    plan = Plan(rows, columns, tokens)
    momentum = momentum_terms(ITERS)
    wanted = targets.T
    for level in range(plan.rows_bits):
        cut = wanted.reshape(-1, 2, rows >> (level + 1), tokens)
        bit = (lax.axis_index("tok") >> level) & 1
        wanted = jnp.where(bit == 1, cut[:, ::-1], cut).reshape(rows, tokens)
    mask = plan.mask().reshape(1).astype(jnp.int32)
    states = [((rows, width), f32) for width in plan.widths]
    small = ((rows, tokens), f32)

    *ahead, product = run(
        functools.partial(first_kernel, plan),
        "first",
        states + [small],
        [SMEM, VMEM, VMEM],
        (mask, dense_rows, activations),
    )
    weights = list(ahead)
    for iteration in range(ITERS):
        own, other = across_features(product)
        pieces = [
            run(
                functools.partial(gradient_kernel, plan, p),
                "gradient",
                [((rows // 2, plan.widths[p]), f32), ((rows // 2, plan.widths[p]), bf16)],
                [VMEM] * 4,
                (own, other, wanted, activations),
            )
            for p in range(PARTS)
        ]
        halves = all_sum(plan, pieces)
        kept, came = halves[0]
        last = plan.widths[0]
        own, other = across_features(kept[:8, last:].astype(f32) + came[:8, last:].astype(f32))
        if iteration + 1 < ITERS:
            before = ()
            for p in range(PARTS):
                weights[p], ahead[p], product = run(
                    functools.partial(update_kernel, plan, p, momentum[iteration]),
                    "update",
                    [states[p], states[p], small],
                    [VMEM] * (7 + len(before)),
                    (own, other, *halves[p], weights[p], ahead[p], activations, *before),
                )
                before = (product,)
        else:
            args = [x for p in range(PARTS) for x in (*halves[p], ahead[p])]
            (result,) = run(
                functools.partial(last_kernel, plan),
                "last",
                [((rows, columns), f32)],
                [SMEM] + [VMEM] * (2 + len(args)),
                (mask, own, other, *args),
            )
    return result


def solution(mesh):
    in_specs = (P("tok", "feat"), P(None, "feat"), P("tok", None))
    out_specs = P(None, "feat")
    return jax.shard_map(shards, mesh=mesh, in_specs=in_specs, out_specs=out_specs, check_vma=False)
```

time: 792 us -> 251 us (0.32)
  waiting for transfers between devices: 664 us -> 127 us
  starting transfers between devices: 0.29 us -> 86.4 us
  matrix products: 55.8 us -> 0 us
  other arithmetic: 33.1 us -> 1.56 us
  Pallas kernels: 0 us -> 25.1 us
  blocking collectives: 20 us -> 0 us
  between operations: 16.2 us -> 0.77 us
  local copies, waits for them, and re-layouts: 1.85 us -> 9.94 us
    psum x4 -> x0, waiting for transfers between devices: 634 us -> none  [shards(): gradient = lax.psum(token_gradient(residual, activations), 'tok')]
    ppermute x0 -> x84, waiting for transfers between devices: none -> 127 us  [swap(): return lax.ppermute(x, axis, pairs)]
    ppermute x0 -> x84, starting transfers between devices: none -> 86.4 us  [swap(): return lax.ppermute(x, axis, pairs)]
    dot_general x8 -> x0, matrix products: 55.8 us -> none  [the longest x4 30.4 us: shards(): lax.dot_general(activations, rounded, (((1,), (1,)), ((), ())), preferred...]
    reduce_scatter x4 -> x0, waiting for transfers between devices: 30.1 us -> none  [shards(): lax.psum_scatter(lax.dot_general(activations, rounded, (((1,), (1,)), (()...]
    pallas_call x0 -> x35, Pallas kernels: none -> 25.1 us  [run(): pl.pallas_call(kernel, out_shape=tuple((jax.ShapeDtypeStruct(shape, dtype...]
    reduce_sum x4 -> x0, other arithmetic: 14.5 us -> none  [shards(): total_square = lax.psum(jnp.sum(gradient * gradient), 'feat')]
    psum x4 -> x0, blocking collectives: 12.5 us -> none  [shards(): total_square = lax.psum(jnp.sum(gradient * gradient), 'feat')]
  transfers between devices with their start and end apart: 8 -> 84, of which waited for: 8 -> 49; matrix products, arithmetic and copies ran while one was open for 0% -> 1% of each run, Pallas kernels for 0% -> 5%
where the time goes in v2:
time: 251 us; the launch traced here: 250 us
  waiting for transfers between devices  127 us (51%)
  starting transfers between devices  86.4 us (34%)
  Pallas kernels  25.1 us (10%)
  local copies, waits for them, and re-layouts  9.94 us (4%)
    ppermute x84, waiting for transfers between devices, swap(): return lax.ppermute(x, axis, pairs)  127 us
    ppermute x84, starting transfers between devices, swap(): return lax.ppermute(x, axis, pairs)  86.4 us
    pallas_call x35, Pallas kernels, run(): pl.pallas_call(kernel, out_shape=tuple((jax.ShapeDtypeStruct(shape, dtype...  25.1 us
    unnamed x31, local copies, waits for them, and re-layouts  9.51 us
  transfers between devices with their start and end apart: 84, of which 49 were waited for; matrix products, arithmetic and copies ran while one was open for 1% of the time, Pallas kernels for 5%

profile of v2, /device:TPU:0, one launch (start us, length us, event | category | flops | bytes accessed | tf_op | source)
XLA Modules:
  0.0 250.4 jit_solution(17310949593060273679)
XLA Ops:
  0.0 3.1 %copy-done = bf16[256,14336]{1,0:T(8,128)(2,1)S(1)} copy-done((bf16[256,14336]{1,0:T(8,128)(2,1)S(1)}, bf16[256,14336]{1,0:T(8,128)(2,1)}, u32[]{:S(2)}) %copy-start) | copy-done | bytes 7340056
  5.1 2.3 first.1
  9.8 3.1 %copy-done.1 = bf16[256,14336]{1,0:T(8,128)(2,1)S(1)} copy-done((bf16[256,14336]{1,0:T(8,128)(2,1)S(1)}, bf16[256,14336]{1,0:T(8,128)(2,1)}, u32[]{:S(2)}) %copy-start.1) | copy-done | bytes 7340056
  13.5 2.9 %collective-permute-start.1 = (bf16[32,5120]{1,0:T(8,128)(2,1)S(1)}, bf16[32,5120]{1,0:T(8,128)(2,1)S(1)}, u32[]{:S(2)}, u32[]{:S(2)}) collective-permute-start(bf16[32,5120]{1,0:T(8,128)(2,1)S(1)} %get-tuple-element.111), channel_id=1, source_target_pairs={{0,1},{1,0},{2,3},{3,2},{4,5},{5,4},{6,7},{7,6},{8,9},{9,8},{10,11... | collective-permute-start | bytes 983048 | tf_op jit(solution)/shard_map/ppermute | solution.py:37
  20.6 3.8 %collective-permute-done.1 = bf16[32,5120]{1,0:T(8,128)(2,1)S(1)} collective-permute-done((bf16[32,5120]{1,0:T(8,128)(2,1)S(1)}, bf16[32,5120]{1,0:T(8,128)(2,1)S(1)}, u32[]{:S(2)}, u32[]{:S(2)}) %collective-permute-start.1) | collective-permute-done | bytes 327712 | tf_op jit(solution)/shard_map/ppermute | solution.py:37
  38.3 2.7 %collective-permute-start.10 = (bf16[8,14336]{1,0:T(8,128)(2,1)S(1)}, bf16[8,14336]{1,0:T(8,128)(2,1)S(1)}, u32[]{:S(2)}, u32[]{:S(2)}) collective-permute-start(bf16[8,14336]{1,0:T(8,128)(2,1)S(1)} %pad_maximum_fusion.low_ref), channel_id=1, source_target_pairs={{0,8},{1,9},{2,10},{3,11},{4,12},{5,13},{6,14},{7,15},{8,0},{9,1},... | collective-permute-start | bytes 688136 | tf_op jit(solution)/shard_map/ppermute | solution.py:37
  40.9 7.5 %collective-permute-done.10.came_ref = bf16[8,14336]{1,0:T(8,128)(2,1)S(1)} collective-permute-done((bf16[8,14336]{1,0:T(8,128)(2,1)S(1)}, bf16[8,14336]{1,0:T(8,128)(2,1)S(1)}, u32[]{:S(2)}, u32[]{:S(2)}) %collective-permute-start.10) | collective-permute-done | bytes 229408 | tf_op jit(solution)/shard_map/ppermute | solution.py:37
  50.9 3.4 %collective-permute-done.11.came_ref = bf16[8,5248]{1,0:T(8,128)(2,1)S(1)} collective-permute-done((bf16[8,5248]{1,0:T(8,128)(2,1)S(1)}, bf16[8,5248]{1,0:T(8,128)(2,1)S(1)}, u32[]{:S(2)}, u32[]{:S(2)}) %collective-permute-start.11) | collective-permute-done | bytes 84000 | tf_op jit(solution)/shard_map/ppermute | solution.py:37
  56.8 3.1 %collective-permute-done.12.came_ref = bf16[16,5248]{1,0:T(8,128)(2,1)S(1)} collective-permute-done((bf16[16,5248]{1,0:T(8,128)(2,1)S(1)}, bf16[16,5248]{1,0:T(8,128)(2,1)S(1)}, u32[]{:S(2)}, u32[]{:S(2)}) %collective-permute-start.12) | collective-permute-done | bytes 167968 | tf_op jit(solution)/shard_map/ppermute | solution.py:37
  64.1 3.3 %collective-permute-done.13.refs_3_ = bf16[32,5248]{1,0:T(8,128)(2,1)S(1)} collective-permute-done((bf16[32,5248]{1,0:T(8,128)(2,1)S(1)}, bf16[32,5248]{1,0:T(8,128)(2,1)S(1)}, u32[]{:S(2)}, u32[]{:S(2)}) %collective-permute-start.13) | collective-permute-done | bytes 335904 | tf_op jit(solution)/shard_map/ppermute | solution.py:37
  77.6 6.0 %collective-permute-done.22 = bf16[32,5120]{1,0:T(8,128)(2,1)S(1)} collective-permute-done((bf16[32,5120]{1,0:T(8,128)(2,1)S(1)}, bf16[32,5120]{1,0:T(8,128)(2,1)S(1)}, u32[]{:S(2)}, u32[]{:S(2)}) %collective-permute-start.22) | collective-permute-done | bytes 327712 | tf_op jit(solution)/shard_map/ppermute | solution.py:37
  86.7 2.5 %collective-permute-done.23 = bf16[16,5120]{1,0:T(8,128)(2,1)S(1)} collective-permute-done((bf16[16,5120]{1,0:T(8,128)(2,1)S(1)}, bf16[16,5120]{1,0:T(8,128)(2,1)S(1)}, u32[]{:S(2)}, u32[]{:S(2)}) %collective-permute-start.23) | collective-permute-done | bytes 163872 | tf_op jit(solution)/shard_map/ppermute | solution.py:37
  96.1 4.5 %collective-permute-start.31 = (bf16[8,14336]{1,0:T(8,128)(2,1)S(1)}, bf16[8,14336]{1,0:T(8,128)(2,1)S(1)}, u32[]{:S(2)}, u32[]{:S(2)}) collective-permute-start(bf16[8,14336]{1,0:T(8,128)(2,1)S(1)} %pad_maximum_fusion.1.low_ref), channel_id=1, source_target_pairs={{0,8},{1,9},{2,10},{3,11},{4,12},{5,13},{6,14},{7,15},{8,0},{9,1},... | collective-permute-start | bytes 688136 | tf_op jit(solution)/shard_map/ppermute | solution.py:37
  100.6 7.1 %collective-permute-done.31.came_ref = bf16[8,14336]{1,0:T(8,128)(2,1)S(1)} collective-permute-done((bf16[8,14336]{1,0:T(8,128)(2,1)S(1)}, bf16[8,14336]{1,0:T(8,128)(2,1)S(1)}, u32[]{:S(2)}, u32[]{:S(2)}) %collective-permute-start.31) | collective-permute-done | bytes 229408 | tf_op jit(solution)/shard_map/ppermute | solution.py:37
  110.5 3.5 %collective-permute-done.32.came_ref = bf16[8,5248]{1,0:T(8,128)(2,1)S(1)} collective-permute-done((bf16[8,5248]{1,0:T(8,128)(2,1)S(1)}, bf16[8,5248]{1,0:T(8,128)(2,1)S(1)}, u32[]{:S(2)}, u32[]{:S(2)}) %collective-permute-start.32) | collective-permute-done | bytes 84000 | tf_op jit(solution)/shard_map/ppermute | solution.py:37
  116.6 3.2 %collective-permute-done.33.came_ref = bf16[16,5248]{1,0:T(8,128)(2,1)S(1)} collective-permute-done((bf16[16,5248]{1,0:T(8,128)(2,1)S(1)}, bf16[16,5248]{1,0:T(8,128)(2,1)S(1)}, u32[]{:S(2)}, u32[]{:S(2)}) %collective-permute-start.33) | collective-permute-done | bytes 167968 | tf_op jit(solution)/shard_map/ppermute | solution.py:37
  123.6 4.0 %collective-permute-done.34.refs_3_ = bf16[32,5248]{1,0:T(8,128)(2,1)S(1)} collective-permute-done((bf16[32,5248]{1,0:T(8,128)(2,1)S(1)}, bf16[32,5248]{1,0:T(8,128)(2,1)S(1)}, u32[]{:S(2)}, u32[]{:S(2)}) %collective-permute-start.34) | collective-permute-done | bytes 335904 | tf_op jit(solution)/shard_map/ppermute | solution.py:37
  137.4 6.3 %collective-permute-done.43 = bf16[32,5120]{1,0:T(8,128)(2,1)S(1)} collective-permute-done((bf16[32,5120]{1,0:T(8,128)(2,1)S(1)}, bf16[32,5120]{1,0:T(8,128)(2,1)S(1)}, u32[]{:S(2)}, u32[]{:S(2)}) %collective-permute-start.43) | collective-permute-done | bytes 327712 | tf_op jit(solution)/shard_map/ppermute | solution.py:37
  155.8 2.8 %collective-permute-start.52 = (bf16[8,14336]{1,0:T(8,128)(2,1)S(1)}, bf16[8,14336]{1,0:T(8,128)(2,1)S(1)}, u32[]{:S(2)}, u32[]{:S(2)}) collective-permute-start(bf16[8,14336]{1,0:T(8,128)(2,1)S(1)} %pad_maximum_fusion.2.low_ref), channel_id=1, source_target_pairs={{0,8},{1,9},{2,10},{3,11},{4,12},{5,13},{6,14},{7,15},{8,0},{9,1},... | collective-permute-start | bytes 688136 | tf_op jit(solution)/shard_map/ppermute | solution.py:37
  158.5 7.3 %collective-permute-done.52.came_ref = bf16[8,14336]{1,0:T(8,128)(2,1)S(1)} collective-permute-done((bf16[8,14336]{1,0:T(8,128)(2,1)S(1)}, bf16[8,14336]{1,0:T(8,128)(2,1)S(1)}, u32[]{:S(2)}, u32[]{:S(2)}) %collective-permute-start.52) | collective-permute-done | bytes 229408 | tf_op jit(solution)/shard_map/ppermute | solution.py:37
  168.9 3.7 %collective-permute-done.53.came_ref = bf16[8,5248]{1,0:T(8,128)(2,1)S(1)} collective-permute-done((bf16[8,5248]{1,0:T(8,128)(2,1)S(1)}, bf16[8,5248]{1,0:T(8,128)(2,1)S(1)}, u32[]{:S(2)}, u32[]{:S(2)}) %collective-permute-start.53) | collective-permute-done | bytes 84000 | tf_op jit(solution)/shard_map/ppermute | solution.py:37
  174.7 4.2 %collective-permute-done.54.came_ref = bf16[16,5248]{1,0:T(8,128)(2,1)S(1)} collective-permute-done((bf16[16,5248]{1,0:T(8,128)(2,1)S(1)}, bf16[16,5248]{1,0:T(8,128)(2,1)S(1)}, u32[]{:S(2)}, u32[]{:S(2)}) %collective-permute-start.54) | collective-permute-done | bytes 167968 | tf_op jit(solution)/shard_map/ppermute | solution.py:37
  182.3 4.1 %collective-permute-done.55.refs_3_ = bf16[32,5248]{1,0:T(8,128)(2,1)S(1)} collective-permute-done((bf16[32,5248]{1,0:T(8,128)(2,1)S(1)}, bf16[32,5248]{1,0:T(8,128)(2,1)S(1)}, u32[]{:S(2)}, u32[]{:S(2)}) %collective-permute-start.55) | collective-permute-done | bytes 335904 | tf_op jit(solution)/shard_map/ppermute | solution.py:37
  197.8 6.6 %collective-permute-done.64 = bf16[32,5120]{1,0:T(8,128)(2,1)S(1)} collective-permute-done((bf16[32,5120]{1,0:T(8,128)(2,1)S(1)}, bf16[32,5120]{1,0:T(8,128)(2,1)S(1)}, u32[]{:S(2)}, u32[]{:S(2)}) %collective-permute-start.64) | collective-permute-done | bytes 327712 | tf_op jit(solution)/shard_map/ppermute | solution.py:37
  207.1 2.8 %collective-permute-done.65 = bf16[16,5120]{1,0:T(8,128)(2,1)S(1)} collective-permute-done((bf16[16,5120]{1,0:T(8,128)(2,1)S(1)}, bf16[16,5120]{1,0:T(8,128)(2,1)S(1)}, u32[]{:S(2)}, u32[]{:S(2)}) %collective-permute-start.65) | collective-permute-done | bytes 163872 | tf_op jit(solution)/shard_map/ppermute | solution.py:37
  216.3 2.1 collective-permute-start.73
  218.4 8.0 %collective-permute-done.73.came_ref = bf16[8,14336]{1,0:T(8,128)(2,1)S(1)} collective-permute-done((bf16[8,14336]{1,0:T(8,128)(2,1)S(1)}, bf16[8,14336]{1,0:T(8,128)(2,1)S(1)}, u32[]{:S(2)}, u32[]{:S(2)}) %collective-permute-start.73) | collective-permute-done | bytes 229408 | tf_op jit(solution)/shard_map/ppermute | solution.py:37
  229.5 2.6 %collective-permute-done.74.came_ref = bf16[8,5248]{1,0:T(8,128)(2,1)S(1)} collective-permute-done((bf16[8,5248]{1,0:T(8,128)(2,1)S(1)}, bf16[8,5248]{1,0:T(8,128)(2,1)S(1)}, u32[]{:S(2)}, u32[]{:S(2)}) %collective-permute-start.74) | collective-permute-done | bytes 84000 | tf_op jit(solution)/shard_map/ppermute | solution.py:37
  234.9 2.8 %collective-permute-done.75.came_ref = bf16[16,5248]{1,0:T(8,128)(2,1)S(1)} collective-permute-done((bf16[16,5248]{1,0:T(8,128)(2,1)S(1)}, bf16[16,5248]{1,0:T(8,128)(2,1)S(1)}, u32[]{:S(2)}, u32[]{:S(2)}) %collective-permute-start.75) | collective-permute-done | bytes 167968 | tf_op jit(solution)/shard_map/ppermute | solution.py:37
  242.8 2.3 collective-permute-done.76.refs_1_
  245.1 2.5 %collective-permute-done.83.refs_7_ = bf16[32,4352]{1,0:T(8,128)(2,1)S(1)} collective-permute-done((bf16[32,4352]{1,0:T(8,128)(2,1)S(1)}, bf16[32,4352]{1,0:T(8,128)(2,1)S(1)}, u32[]{:S(2)}, u32[]{:S(2)}) %collective-permute-start.83) | collective-permute-done | bytes 278560 | tf_op jit(solution)/shard_map/ppermute | solution.py:37
  247.7 2.7 %last.1 = f32[64,14336]{1,0:T(8,128)} custom-call(s32[1]{0:T(128)} %bitcast.mask_ref, f32[8,128]{1,0:T(8,128)S(1)} %convert_add_fusion.12.own_ref, f32[8,128]{1,0:T(8,128)S(1)} %collective-permute-done.77.other_ref, bf16[32,5248]{1,0:T(8,128)(2,1)S(1)} %join.15.refs_0_, bf16[32,5248]{1,0:T(8,128)(2,1)S(1)} %collective-permute-done.76.refs_1_, ...), custom_call_target="tpu_custom_call" | custom-call | tf_op jit(solution)/shard_map/last/pallas_call | solution.py:102
  (287 shorter events, 122.6 us)
Async XLA Ops:
  13.5 10.9 %collective-permute-start.1 = (bf16[32,5120]{1,0:T(8,128)(2,1)S(1)}, bf16[32,5120]{1,0:T(8,128)(2,1)S(1)}, u32[]{:S(2)}, u32[]{:S(2)}) collective-permute-start(bf16[32,5120]{1,0:T(8,128)(2,1)S(1)} %get-tuple-element.111), channel_id=1, source_target_pairs={{0,1},{1,0},{2,3},{3,2},{4,5},{5,4},{6,7},{7,6},{8,9},{9,8},{10,11... | collective-permute-start | bytes 983048 | tf_op jit(solution)/shard_map/ppermute | solution.py:37
  16.9 9.4 %collective-permute-start.4 = (bf16[32,4864]{1,0:T(8,128)(2,1)S(1)}, bf16[32,4864]{1,0:T(8,128)(2,1)S(1)}, u32[]{:S(2)}, u32[]{:S(2)}) collective-permute-start(bf16[32,4864]{1,0:T(8,128)(2,1)S(1)} %get-tuple-element.113), channel_id=1, source_target_pairs={{0,2},{1,3},{2,0},{3,1},{4,6},{5,7},{6,4},{7,5},{8,10},{9,11},{10,... | collective-permute-start | bytes 933896 | tf_op jit(solution)/shard_map/ppermute | solution.py:37
  19.0 9.1 %collective-permute-start.7 = (bf16[32,4352]{1,0:T(8,128)(2,1)S(1)}, bf16[32,4352]{1,0:T(8,128)(2,1)S(1)}, u32[]{:S(2)}, u32[]{:S(2)}) collective-permute-start(bf16[32,4352]{1,0:T(8,128)(2,1)S(1)} %get-tuple-element.118), channel_id=1, source_target_pairs={{0,4},{1,5},{2,6},{3,7},{4,0},{5,1},{6,2},{7,3},{8,12},{9,13},{10,... | collective-permute-start | bytes 835592 | tf_op jit(solution)/shard_map/ppermute | solution.py:37
  38.3 10.1 %collective-permute-start.10 = (bf16[8,14336]{1,0:T(8,128)(2,1)S(1)}, bf16[8,14336]{1,0:T(8,128)(2,1)S(1)}, u32[]{:S(2)}, u32[]{:S(2)}) collective-permute-start(bf16[8,14336]{1,0:T(8,128)(2,1)S(1)} %pad_maximum_fusion.low_ref), channel_id=1, source_target_pairs={{0,8},{1,9},{2,10},{3,11},{4,12},{5,13},{6,14},{7,15},{8,0},{9,1},... | collective-permute-start | bytes 688136 | tf_op jit(solution)/shard_map/ppermute | solution.py:37
  55.7 7.0 %collective-permute-start.17 = (bf16[16,4352]{1,0:T(8,128)(2,1)S(1)}, bf16[16,4352]{1,0:T(8,128)(2,1)S(1)}, u32[]{:S(2)}, u32[]{:S(2)}) collective-permute-start(bf16[16,4352]{1,0:T(8,128)(2,1)S(1)} %pad_maximum_fusion.4), channel_id=1, source_target_pairs={{0,1},{1,0},{2,3},{3,2},{4,5},{5,4},{6,7},{7,6},{8,9},{9,8},{10,11... | collective-permute-start | bytes 417800 | tf_op jit(solution)/shard_map/ppermute | solution.py:37
  60.1 7.3 %collective-permute-start.13 = (bf16[32,5248]{1,0:T(8,128)(2,1)S(1)}, bf16[32,5248]{1,0:T(8,128)(2,1)S(1)}, u32[]{:S(2)}, u32[]{:S(2)}) collective-permute-start(bf16[32,5248]{1,0:T(8,128)(2,1)S(1)} %join.9.refs_2_), channel_id=1, source_target_pairs={{0,1},{1,0},{2,3},{3,2},{4,5},{5,4},{6,7},{7,6},{8,9},{9,8},{10,11... | collective-permute-start | bytes 1007624 | tf_op jit(solution)/shard_map/ppermute | solution.py:37
  61.4 8.3 %collective-permute-start.20 = (bf16[32,4864]{1,0:T(8,128)(2,1)S(1)}, bf16[32,4864]{1,0:T(8,128)(2,1)S(1)}, u32[]{:S(2)}, u32[]{:S(2)}) collective-permute-start(bf16[32,4864]{1,0:T(8,128)(2,1)S(1)} %constant_dynamic-update-slice_fusion.2.refs_2_), channel_id=1, source_target_pairs={{0,2},{1,3},{2,0},{3,1},{4,6},{5,7},{6,4},{7,5},{8,10},{9,11},{10,... | collective-permute-start | bytes 933896 | tf_op jit(solution)/shard_map/ppermute | solution.py:37
  62.7 8.0 %collective-permute-start.19 = (bf16[32,4352]{1,0:T(8,128)(2,1)S(1)}, bf16[32,4352]{1,0:T(8,128)(2,1)S(1)}, u32[]{:S(2)}, u32[]{:S(2)}) collective-permute-start(bf16[32,4352]{1,0:T(8,128)(2,1)S(1)} %constant_dynamic-update-slice_fusion.5.refs_2_), channel_id=1, source_target_pairs={{0,4},{1,5},{2,6},{3,7},{4,0},{5,1},{6,2},{7,3},{8,12},{9,13},{10,... | collective-permute-start | bytes 835592 | tf_op jit(solution)/shard_map/ppermute | solution.py:37
  73.7 9.8 %collective-permute-start.22 = (bf16[32,5120]{1,0:T(8,128)(2,1)S(1)}, bf16[32,5120]{1,0:T(8,128)(2,1)S(1)}, u32[]{:S(2)}, u32[]{:S(2)}) collective-permute-start(bf16[32,5120]{1,0:T(8,128)(2,1)S(1)} %get-tuple-element.136), channel_id=1, source_target_pairs={{0,1},{1,0},{2,3},{3,2},{4,5},{5,4},{6,7},{7,6},{8,9},{9,8},{10,11... | collective-permute-start | bytes 983048 | tf_op jit(solution)/shard_map/ppermute | solution.py:37
  75.8 9.2 %collective-permute-start.25 = (bf16[32,4864]{1,0:T(8,128)(2,1)S(1)}, bf16[32,4864]{1,0:T(8,128)(2,1)S(1)}, u32[]{:S(2)}, u32[]{:S(2)}) collective-permute-start(bf16[32,4864]{1,0:T(8,128)(2,1)S(1)} %get-tuple-element.138), channel_id=1, source_target_pairs={{0,2},{1,3},{2,0},{3,1},{4,6},{5,7},{6,4},{7,5},{8,10},{9,11},{10,... | collective-permute-start | bytes 933896 | tf_op jit(solution)/shard_map/ppermute | solution.py:37
  77.3 8.5 %collective-permute-start.28 = (bf16[32,4352]{1,0:T(8,128)(2,1)S(1)}, bf16[32,4352]{1,0:T(8,128)(2,1)S(1)}, u32[]{:S(2)}, u32[]{:S(2)}) collective-permute-start(bf16[32,4352]{1,0:T(8,128)(2,1)S(1)} %get-tuple-element.143), channel_id=1, source_target_pairs={{0,4},{1,5},{2,6},{3,7},{4,0},{5,1},{6,2},{7,3},{8,12},{9,13},{10,... | collective-permute-start | bytes 835592 | tf_op jit(solution)/shard_map/ppermute | solution.py:37
  96.1 11.6 %collective-permute-start.31 = (bf16[8,14336]{1,0:T(8,128)(2,1)S(1)}, bf16[8,14336]{1,0:T(8,128)(2,1)S(1)}, u32[]{:S(2)}, u32[]{:S(2)}) collective-permute-start(bf16[8,14336]{1,0:T(8,128)(2,1)S(1)} %pad_maximum_fusion.1.low_ref), channel_id=1, source_target_pairs={{0,8},{1,9},{2,10},{3,11},{4,12},{5,13},{6,14},{7,15},{8,0},{9,1},... | collective-permute-start | bytes 688136 | tf_op jit(solution)/shard_map/ppermute | solution.py:37
  108.0 6.9 %collective-permute-start.37 = (bf16[8,4864]{1,0:T(8,128)(2,1)S(1)}, bf16[8,4864]{1,0:T(8,128)(2,1)S(1)}, u32[]{:S(2)}, u32[]{:S(2)}) collective-permute-start(bf16[8,4864]{1,0:T(8,128)(2,1)S(1)} %get-tuple-element.149), channel_id=1, source_target_pairs={{0,1},{1,0},{2,3},{3,2},{4,5},{5,4},{6,7},{7,6},{8,9},{9,8},{10,11... | collective-permute-start | bytes 233480 | tf_op jit(solution)/shard_map/ppermute | solution.py:37
  120.0 7.6 %collective-permute-start.34 = (bf16[32,5248]{1,0:T(8,128)(2,1)S(1)}, bf16[32,5248]{1,0:T(8,128)(2,1)S(1)}, u32[]{:S(2)}, u32[]{:S(2)}) collective-permute-start(bf16[32,5248]{1,0:T(8,128)(2,1)S(1)} %join.11.refs_2_), channel_id=1, source_target_pairs={{0,1},{1,0},{2,3},{3,2},{4,5},{5,4},{6,7},{7,6},{8,9},{9,8},{10,11... | collective-permute-start | bytes 1007624 | tf_op jit(solution)/shard_map/ppermute | solution.py:37
  120.4 9.4 %collective-permute-start.41 = (bf16[32,4864]{1,0:T(8,128)(2,1)S(1)}, bf16[32,4864]{1,0:T(8,128)(2,1)S(1)}, u32[]{:S(2)}, u32[]{:S(2)}) collective-permute-start(bf16[32,4864]{1,0:T(8,128)(2,1)S(1)} %constant_dynamic-update-slice_fusion.10.refs_2_), channel_id=1, source_target_pairs={{0,2},{1,3},{2,0},{3,1},{4,6},{5,7},{6,4},{7,5},{8,10},{9,11},{10,... | collective-permute-start | bytes 933896 | tf_op jit(solution)/shard_map/ppermute | solution.py:37
  122.1 8.8 %collective-permute-start.40 = (bf16[32,4352]{1,0:T(8,128)(2,1)S(1)}, bf16[32,4352]{1,0:T(8,128)(2,1)S(1)}, u32[]{:S(2)}, u32[]{:S(2)}) collective-permute-start(bf16[32,4352]{1,0:T(8,128)(2,1)S(1)} %constant_dynamic-update-slice_fusion.13.refs_2_), channel_id=1, source_target_pairs={{0,4},{1,5},{2,6},{3,7},{4,0},{5,1},{6,2},{7,3},{8,12},{9,13},{10,... | collective-permute-start | bytes 835592 | tf_op jit(solution)/shard_map/ppermute | solution.py:37
  133.9 9.8 %collective-permute-start.43 = (bf16[32,5120]{1,0:T(8,128)(2,1)S(1)}, bf16[32,5120]{1,0:T(8,128)(2,1)S(1)}, u32[]{:S(2)}, u32[]{:S(2)}) collective-permute-start(bf16[32,5120]{1,0:T(8,128)(2,1)S(1)} %get-tuple-element.164), channel_id=1, source_target_pairs={{0,1},{1,0},{2,3},{3,2},{4,5},{5,4},{6,7},{7,6},{8,9},{9,8},{10,11... | collective-permute-start | bytes 983048 | tf_op jit(solution)/shard_map/ppermute | solution.py:37
  135.0 9.4 %collective-permute-start.46 = (bf16[32,4864]{1,0:T(8,128)(2,1)S(1)}, bf16[32,4864]{1,0:T(8,128)(2,1)S(1)}, u32[]{:S(2)}, u32[]{:S(2)}) collective-permute-start(bf16[32,4864]{1,0:T(8,128)(2,1)S(1)} %get-tuple-element.166), channel_id=1, source_target_pairs={{0,2},{1,3},{2,0},{3,1},{4,6},{5,7},{6,4},{7,5},{8,10},{9,11},{10,... | collective-permute-start | bytes 933896 | tf_op jit(solution)/shard_map/ppermute | solution.py:37
  136.7 8.9 %collective-permute-start.49 = (bf16[32,4352]{1,0:T(8,128)(2,1)S(1)}, bf16[32,4352]{1,0:T(8,128)(2,1)S(1)}, u32[]{:S(2)}, u32[]{:S(2)}) collective-permute-start(bf16[32,4352]{1,0:T(8,128)(2,1)S(1)} %get-tuple-element.171), channel_id=1, source_target_pairs={{0,4},{1,5},{2,6},{3,7},{4,0},{5,1},{6,2},{7,3},{8,12},{9,13},{10,... | collective-permute-start | bytes 835592 | tf_op jit(solution)/shard_map/ppermute | solution.py:37
  155.8 10.1 %collective-permute-start.52 = (bf16[8,14336]{1,0:T(8,128)(2,1)S(1)}, bf16[8,14336]{1,0:T(8,128)(2,1)S(1)}, u32[]{:S(2)}, u32[]{:S(2)}) collective-permute-start(bf16[8,14336]{1,0:T(8,128)(2,1)S(1)} %pad_maximum_fusion.2.low_ref), channel_id=1, source_target_pairs={{0,8},{1,9},{2,10},{3,11},{4,12},{5,13},{6,14},{7,15},{8,0},{9,1},... | collective-permute-start | bytes 688136 | tf_op jit(solution)/shard_map/ppermute | solution.py:37
  166.1 7.3 %collective-permute-start.58 = (bf16[8,4864]{1,0:T(8,128)(2,1)S(1)}, bf16[8,4864]{1,0:T(8,128)(2,1)S(1)}, u32[]{:S(2)}, u32[]{:S(2)}) collective-permute-start(bf16[8,4864]{1,0:T(8,128)(2,1)S(1)} %get-tuple-element.177), channel_id=1, source_target_pairs={{0,1},{1,0},{2,3},{3,2},{4,5},{5,4},{6,7},{7,6},{8,9},{9,8},{10,11... | collective-permute-start | bytes 233480 | tf_op jit(solution)/shard_map/ppermute | solution.py:37
  173.6 7.6 %collective-permute-start.59 = (bf16[16,4352]{1,0:T(8,128)(2,1)S(1)}, bf16[16,4352]{1,0:T(8,128)(2,1)S(1)}, u32[]{:S(2)}, u32[]{:S(2)}) collective-permute-start(bf16[16,4352]{1,0:T(8,128)(2,1)S(1)} %pad_maximum_fusion.6), channel_id=1, source_target_pairs={{0,1},{1,0},{2,3},{3,2},{4,5},{5,4},{6,7},{7,6},{8,9},{9,8},{10,11... | collective-permute-start | bytes 417800 | tf_op jit(solution)/shard_map/ppermute | solution.py:37
  179.1 7.2 %collective-permute-start.55 = (bf16[32,5248]{1,0:T(8,128)(2,1)S(1)}, bf16[32,5248]{1,0:T(8,128)(2,1)S(1)}, u32[]{:S(2)}, u32[]{:S(2)}) collective-permute-start(bf16[32,5248]{1,0:T(8,128)(2,1)S(1)} %join.13.refs_2_), channel_id=1, source_target_pairs={{0,1},{1,0},{2,3},{3,2},{4,5},{5,4},{6,7},{7,6},{8,9},{9,8},{10,11... | collective-permute-start | bytes 1007624 | tf_op jit(solution)/shard_map/ppermute | solution.py:37
  179.2 10.2 %collective-permute-start.62 = (bf16[32,4864]{1,0:T(8,128)(2,1)S(1)}, bf16[32,4864]{1,0:T(8,128)(2,1)S(1)}, u32[]{:S(2)}, u32[]{:S(2)}) collective-permute-start(bf16[32,4864]{1,0:T(8,128)(2,1)S(1)} %constant_dynamic-update-slice_fusion.18.refs_2_), channel_id=1, source_target_pairs={{0,2},{1,3},{2,0},{3,1},{4,6},{5,7},{6,4},{7,5},{8,10},{9,11},{10,... | collective-permute-start | bytes 933896 | tf_op jit(solution)/shard_map/ppermute | solution.py:37
  181.2 9.9 %collective-permute-start.61 = (bf16[32,4352]{1,0:T(8,128)(2,1)S(1)}, bf16[32,4352]{1,0:T(8,128)(2,1)S(1)}, u32[]{:S(2)}, u32[]{:S(2)}) collective-permute-start(bf16[32,4352]{1,0:T(8,128)(2,1)S(1)} %constant_dynamic-update-slice_fusion.21.refs_2_), channel_id=1, source_target_pairs={{0,4},{1,5},{2,6},{3,7},{4,0},{5,1},{6,2},{7,3},{8,12},{9,13},{10,... | collective-permute-start | bytes 835592 | tf_op jit(solution)/shard_map/ppermute | solution.py:37
  194.5 9.8 %collective-permute-start.64 = (bf16[32,5120]{1,0:T(8,128)(2,1)S(1)}, bf16[32,5120]{1,0:T(8,128)(2,1)S(1)}, u32[]{:S(2)}, u32[]{:S(2)}) collective-permute-start(bf16[32,5120]{1,0:T(8,128)(2,1)S(1)} %get-tuple-element.192), channel_id=1, source_target_pairs={{0,1},{1,0},{2,3},{3,2},{4,5},{5,4},{6,7},{7,6},{8,9},{9,8},{10,11... | collective-permute-start | bytes 983048 | tf_op jit(solution)/shard_map/ppermute | solution.py:37
  195.2 9.5 %collective-permute-start.67 = (bf16[32,4864]{1,0:T(8,128)(2,1)S(1)}, bf16[32,4864]{1,0:T(8,128)(2,1)S(1)}, u32[]{:S(2)}, u32[]{:S(2)}) collective-permute-start(bf16[32,4864]{1,0:T(8,128)(2,1)S(1)} %get-tuple-element.194), channel_id=1, source_target_pairs={{0,2},{1,3},{2,0},{3,1},{4,6},{5,7},{6,4},{7,5},{8,10},{9,11},{10,... | collective-permute-start | bytes 933896 | tf_op jit(solution)/shard_map/ppermute | solution.py:37
  197.1 8.4 %collective-permute-start.70 = (bf16[32,4352]{1,0:T(8,128)(2,1)S(1)}, bf16[32,4352]{1,0:T(8,128)(2,1)S(1)}, u32[]{:S(2)}, u32[]{:S(2)}) collective-permute-start(bf16[32,4352]{1,0:T(8,128)(2,1)S(1)} %get-tuple-element.199), channel_id=1, source_target_pairs={{0,4},{1,5},{2,6},{3,7},{4,0},{5,1},{6,2},{7,3},{8,12},{9,13},{10,... | collective-permute-start | bytes 835592 | tf_op jit(solution)/shard_map/ppermute | solution.py:37
  216.3 10.1 %collective-permute-start.73 = (bf16[8,14336]{1,0:T(8,128)(2,1)S(1)}, bf16[8,14336]{1,0:T(8,128)(2,1)S(1)}, u32[]{:S(2)}, u32[]{:S(2)}) collective-permute-start(bf16[8,14336]{1,0:T(8,128)(2,1)S(1)} %pad_maximum_fusion.3.low_ref), channel_id=1, source_target_pairs={{0,8},{1,9},{2,10},{3,11},{4,12},{5,13},{6,14},{7,15},{8,0},{9,1},... | collective-permute-start | bytes 688136 | tf_op jit(solution)/shard_map/ppermute | solution.py:37
  226.7 7.5 %collective-permute-start.78 = (bf16[8,4864]{1,0:T(8,128)(2,1)S(1)}, bf16[8,4864]{1,0:T(8,128)(2,1)S(1)}, u32[]{:S(2)}, u32[]{:S(2)}) collective-permute-start(bf16[8,4864]{1,0:T(8,128)(2,1)S(1)} %get-tuple-element.205), channel_id=1, source_target_pairs={{0,1},{1,0},{2,3},{3,2},{4,5},{5,4},{6,7},{7,6},{8,9},{9,8},{10,11... | collective-permute-start | bytes 233480 | tf_op jit(solution)/shard_map/ppermute | solution.py:37
  237.9 7.3 %collective-permute-start.76 = (bf16[32,5248]{1,0:T(8,128)(2,1)S(1)}, bf16[32,5248]{1,0:T(8,128)(2,1)S(1)}, u32[]{:S(2)}, u32[]{:S(2)}) collective-permute-start(bf16[32,5248]{1,0:T(8,128)(2,1)S(1)} %join.15.refs_0_), channel_id=1, source_target_pairs={{0,1},{1,0},{2,3},{3,2},{4,5},{5,4},{6,7},{7,6},{8,9},{9,8},{10,11... | collective-permute-start | bytes 1007624 | tf_op jit(solution)/shard_map/ppermute | solution.py:37
  240.4 7.3 %collective-permute-start.80 = (bf16[32,4864]{1,0:T(8,128)(2,1)S(1)}, bf16[32,4864]{1,0:T(8,128)(2,1)S(1)}, u32[]{:S(2)}, u32[]{:S(2)}) collective-permute-start(bf16[32,4864]{1,0:T(8,128)(2,1)S(1)} %constant_dynamic-update-slice_fusion.26.refs_3_), channel_id=1, source_target_pairs={{0,2},{1,3},{2,0},{3,1},{4,6},{5,7},{6,4},{7,5},{8,10},{9,11},{10,... | collective-permute-start | bytes 933896 | tf_op jit(solution)/shard_map/ppermute | solution.py:37
  (60 other events, 354.8 us)

commit v3 on v2

--- a/solution.py
+++ b/solution.py
@@ -109,9 +109,12 @@
     )(*args)
 
 
-def first_kernel(plan, mask_ref, dense_ref, act_ref, *refs):
-    *start_refs, product_ref = refs
+def first_kernel(plan, mask_ref, dense_ref, targets_ref, act_ref, *refs):
+    *start_refs, wanted_ref, product_ref = refs
     h = plan.height
+    for g in range(plan.places):
+        rows = pl.ds(pl.multiple_of((g ^ mask_ref[0]) * h, h), h)
+        wanted_ref[g * h : (g + 1) * h] = targets_ref[rows, :]
     total = jnp.zeros(product_ref.shape, f32)
     for p, (a, b) in enumerate(plan.spans):
         for start in range(a, b, plan.unit):
@@ -148,19 +151,20 @@
     return jnp.sum(tile, keepdims=True) / (tile.shape[0] * (LANES // 2))
 
 
-def combine_kernel(plan, low_ref, came_ref, *outs):
-    h = plan.height
-    total = jnp.zeros((h, LANES), f32)
-    for p, (a, b) in enumerate(plan.spans):
-        for start in range(a, b, plan.unit):
-            block = low_ref[:, start : start + plan.unit].astype(f32) + came_ref[:, start : start + plan.unit].astype(f32)
-            block = block.astype(bf16)
-            outs[p][:, start - a : start - a + plan.unit] = block
-            block = block.astype(f32)
-            for lane in range(0, plan.unit, LANES):
-                piece = block[:, lane : lane + LANES]
-                total = total + piece * piece
-    outs[0][:, plan.widths[0] :] = pair_tile(jnp.sum(total, keepdims=True), h)
+def combine_kernel(plan, p, low_ref, came_ref, *refs):
+    total = refs[0][...] if p else jnp.zeros((plan.height, LANES), f32)
+    out_ref = refs[1] if p else refs[0]
+    for here, _ in plan.blocks(p):
+        block = (low_ref[:, here].astype(f32) + came_ref[:, here].astype(f32)).astype(bf16)
+        out_ref[:, here] = block
+        block = block.astype(f32)
+        for lane in range(0, plan.unit, LANES):
+            piece = block[:, lane : lane + LANES]
+            total = total + piece * piece
+    if p + 1 < PARTS:
+        refs[-1][...] = total
+    else:
+        out_ref[:, plan.widths[p] :] = pair_tile(jnp.sum(total, keepdims=True), plan.height)
 
 
 def join_kernel(plan, own_ref, came_ref, out_ref):
@@ -227,22 +231,25 @@
             middle = whole.shape[0] // 2 if stage + 1 < plan.rows_bits else 0
             sends[p] = whole[middle:].astype(bf16)
             current[p] = whole[:middle]
-    low = jnp.concatenate(sends, 1)
-    came = jnp.zeros_like(low)
+    came = [None] * PARTS
     for bit in range(plan.rows_bits, bits_of("tok")):
         if bit > plan.rows_bits:
-            low = (low.astype(f32) + came.astype(f32)).astype(bf16)
-        came = swap(low, "tok", bit)
-    outs = [((plan.height, width + (0 if p else LANES)), bf16) for p, width in enumerate(plan.widths)]
-    current = run(functools.partial(combine_kernel, plan), "combine", outs, [VMEM] * 2, (low, came))
-    current = list(current)
+            sends = [(a.astype(f32) + b.astype(f32)).astype(bf16) for a, b in zip(sends, came)]
+        came = [swap(x, "tok", bit) for x in sends]
+    square = ()
+    for p, width in enumerate(plan.widths):
+        last = p + 1 == PARTS
+        outs = [((plan.height, width + LANES * last), bf16)] + [((plan.height, LANES), f32)] * (not last)
+        current[p], *square = run(
+            functools.partial(combine_kernel, plan, p), "combine", outs, [VMEM] * (2 + len(square)), (sends[p], came[p], *square)
+        )
     for stage in reversed(range(plan.rows_bits)):
         came = [swap(current[p], "tok", plan.orders[p][stage]) for p in range(PARTS)]
         if stage:
             for p in range(PARTS):
                 rows, width = current[p].shape
                 arrived = after(came[p], current[:p]) if p else came[p]
-                if p:
+                if p + 1 < PARTS:
                     current[p] = jnp.concatenate([current[p], arrived], 0)
                 else:
                     (current[p],) = run(
@@ -263,21 +270,16 @@
     tokens = activations.shape[0]
     plan = Plan(rows, columns, tokens)
     momentum = momentum_terms(ITERS)
-    wanted = targets.T
-    for level in range(plan.rows_bits):
-        cut = wanted.reshape(-1, 2, rows >> (level + 1), tokens)
-        bit = (lax.axis_index("tok") >> level) & 1
-        wanted = jnp.where(bit == 1, cut[:, ::-1], cut).reshape(rows, tokens)
     mask = plan.mask().reshape(1).astype(jnp.int32)
     states = [((rows, width), f32) for width in plan.widths]
     small = ((rows, tokens), f32)
 
-    *ahead, product = run(
+    *ahead, wanted, product = run(
         functools.partial(first_kernel, plan),
         "first",
-        states + [small],
-        [SMEM, VMEM, VMEM],
-        (mask, dense_rows, activations),
+        states + [small, small],
+        [SMEM, VMEM, VMEM, VMEM],
+        (mask, dense_rows, targets.T, activations),
     )
     weights = list(ahead)
     for iteration in range(ITERS):
@@ -293,8 +295,8 @@
             for p in range(PARTS)
         ]
         halves = all_sum(plan, pieces)
-        kept, came = halves[0]
-        last = plan.widths[0]
+        kept, came = halves[-1]
+        last = plan.widths[-1]
         own, other = across_features(kept[:8, last:].astype(f32) + came[:8, last:].astype(f32))
         if iteration + 1 < ITERS:
             before = ()

time: 251 us -> 236 us (0.940)
  waiting for transfers between devices: 127 us -> 98.5 us
  starting transfers between devices: 86.4 us -> 103 us
  local copies, waits for them, and re-layouts: 9.94 us -> 6.58 us
    ppermute x84 -> x92, waiting for transfers between devices: 127 us -> 98.5 us  [swap(): return lax.ppermute(x, axis, pairs)]
    ppermute x84 -> x92, starting transfers between devices: 86.4 us -> 103 us  [swap(): return lax.ppermute(x, axis, pairs)]
    unnamed x31 -> x24, local copies, waits for them, and re-layouts: 9.51 us -> 6.15 us
    pallas_call x35 -> x43, Pallas kernels: 25.1 us -> 25.3 us  [run(): pl.pallas_call(kernel, out_shape=tuple((jax.ShapeDtypeStruct(shape, dtype...]
  transfers between devices with their start and end apart: 84 -> 92, of which waited for: 49 -> 58; matrix products, arithmetic and copies ran while one was open for 1% -> 1% of each run, Pallas kernels for 5% -> 4%
where the time goes in v3:
time: 236 us
  starting transfers between devices  103 us (44%)
  waiting for transfers between devices  98.5 us (42%)
  Pallas kernels  25.3 us (11%)
  local copies, waits for them, and re-layouts  6.58 us (3%)
    ppermute x92, starting transfers between devices, swap(): return lax.ppermute(x, axis, pairs)  103 us
    ppermute x92, waiting for transfers between devices, swap(): return lax.ppermute(x, axis, pairs)  98.5 us
    pallas_call x43, Pallas kernels, run(): pl.pallas_call(kernel, out_shape=tuple((jax.ShapeDtypeStruct(shape, dtype...  25.3 us
    unnamed x24, local copies, waits for them, and re-layouts  6.15 us
  transfers between devices with their start and end apart: 92, of which 58 were waited for; matrix products, arithmetic and copies ran while one was open for 1% of the time, Pallas kernels for 4%

profile of v3, /device:TPU:0, one launch (start us, length us, event | category | flops | bytes accessed | tf_op | source)
XLA Modules:
  0.0 235.9 jit_solution(1559089633313406691)
XLA Ops:
  0.0 3.1 %copy-done = bf16[256,14336]{1,0:T(8,128)(2,1)S(1)} copy-done((bf16[256,14336]{1,0:T(8,128)(2,1)S(1)}, bf16[256,14336]{1,0:T(8,128)(2,1)}, u32[]{:S(2)}) %copy-start) | copy-done | bytes 7340056
  3.1 2.0 copy-done.2
  6.0 2.3 first.1
  10.3 2.9 %collective-permute-start.2 = (bf16[32,5120]{1,0:T(8,128)(2,1)S(1)}, bf16[32,5120]{1,0:T(8,128)(2,1)S(1)}, u32[]{:S(2)}, u32[]{:S(2)}) collective-permute-start(bf16[32,5120]{1,0:T(8,128)(2,1)S(1)} %get-tuple-element.119), channel_id=1, source_target_pairs={{0,1},{1,0},{2,3},{3,2},{4,5},{5,4},{6,7},{7,6},{8,9},{9,8},{10,11... | collective-permute-start | bytes 983048 | tf_op jit(solution)/shard_map/ppermute | solution.py:37
  17.5 3.8 %collective-permute-done.2 = bf16[32,5120]{1,0:T(8,128)(2,1)S(1)} collective-permute-done((bf16[32,5120]{1,0:T(8,128)(2,1)S(1)}, bf16[32,5120]{1,0:T(8,128)(2,1)S(1)}, u32[]{:S(2)}, u32[]{:S(2)}) %collective-permute-start.2) | collective-permute-done | bytes 327712 | tf_op jit(solution)/shard_map/ppermute | solution.py:37
  21.3 1.8 collective-permute-start.5
  32.0 2.7 %collective-permute-start.12 = (bf16[8,5120]{1,0:T(8,128)(2,1)S(1)}, bf16[8,5120]{1,0:T(8,128)(2,1)S(1)}, u32[]{:S(2)}, u32[]{:S(2)}) collective-permute-start(bf16[8,5120]{1,0:T(8,128)(2,1)S(1)} %fusion.3.low_ref), channel_id=1, source_target_pairs={{0,8},{1,9},{2,10},{3,11},{4,12},{5,13},{6,14},{7,15},{8,0},{9,1},... | collective-permute-start | bytes 245768 | tf_op jit(solution)/shard_map/ppermute | solution.py:37
  37.8 3.3 %collective-permute-done.12.came_ref = bf16[8,5120]{1,0:T(8,128)(2,1)S(1)} collective-permute-done((bf16[8,5120]{1,0:T(8,128)(2,1)S(1)}, bf16[8,5120]{1,0:T(8,128)(2,1)S(1)}, u32[]{:S(2)}, u32[]{:S(2)}) %collective-permute-start.12) | collective-permute-done | bytes 81952 | tf_op jit(solution)/shard_map/ppermute | solution.py:37
  51.4 2.1 collective-permute-done.18
  53.5 2.2 collective-permute-done.16.came_ref
  57.1 2.5 %collective-permute-start.21 = (bf16[32,4864]{1,0:T(8,128)(2,1)S(1)}, bf16[32,4864]{1,0:T(8,128)(2,1)S(1)}, u32[]{:S(2)}, u32[]{:S(2)}) collective-permute-start(bf16[32,4864]{1,0:T(8,128)(2,1)S(1)} %constant_dynamic-update-slice_fusion.7.refs_2_), channel_id=1, source_target_pairs={{0,2},{1,3},{2,0},{3,1},{4,6},{5,7},{6,4},{7,5},{8,10},{9,11},{10,... | collective-permute-start | bytes 933896 | tf_op jit(solution)/shard_map/ppermute | solution.py:37
  59.6 2.9 %collective-permute-done.19.refs_3_ = bf16[32,4480]{1,0:T(8,128)(2,1)S(1)} collective-permute-done((bf16[32,4480]{1,0:T(8,128)(2,1)S(1)}, bf16[32,4480]{1,0:T(8,128)(2,1)S(1)}, u32[]{:S(2)}, u32[]{:S(2)}) %collective-permute-start.19) | collective-permute-done | bytes 286752 | tf_op jit(solution)/shard_map/ppermute | solution.py:37
  69.8 2.6 %collective-permute-start.26 = (bf16[32,4864]{1,0:T(8,128)(2,1)S(1)}, bf16[32,4864]{1,0:T(8,128)(2,1)S(1)}, u32[]{:S(2)}, u32[]{:S(2)}) collective-permute-start(bf16[32,4864]{1,0:T(8,128)(2,1)S(1)} %get-tuple-element.147), channel_id=1, source_target_pairs={{0,2},{1,3},{2,0},{3,1},{4,6},{5,7},{6,4},{7,5},{8,10},{9,11},{10,... | collective-permute-start | bytes 933896 | tf_op jit(solution)/shard_map/ppermute | solution.py:37
  73.6 4.9 %collective-permute-done.25 = bf16[32,5120]{1,0:T(8,128)(2,1)S(1)} collective-permute-done((bf16[32,5120]{1,0:T(8,128)(2,1)S(1)}, bf16[32,5120]{1,0:T(8,128)(2,1)S(1)}, u32[]{:S(2)}, u32[]{:S(2)}) %collective-permute-start.25) | collective-permute-done | bytes 327712 | tf_op jit(solution)/shard_map/ppermute | solution.py:37
  88.7 2.0 collective-permute-start.35
  91.9 2.1 collective-permute-start.33
  94.0 4.2 %collective-permute-done.35.came_ref = bf16[8,5120]{1,0:T(8,128)(2,1)S(1)} collective-permute-done((bf16[8,5120]{1,0:T(8,128)(2,1)S(1)}, bf16[8,5120]{1,0:T(8,128)(2,1)S(1)}, u32[]{:S(2)}, u32[]{:S(2)}) %collective-permute-start.35) | collective-permute-done | bytes 81952 | tf_op jit(solution)/shard_map/ppermute | solution.py:37
  109.4 1.9 collective-permute-done.39.came_ref
  113.8 4.4 %collective-permute-done.42.refs_3_ = bf16[32,4480]{1,0:T(8,128)(2,1)S(1)} collective-permute-done((bf16[32,4480]{1,0:T(8,128)(2,1)S(1)}, bf16[32,4480]{1,0:T(8,128)(2,1)S(1)}, u32[]{:S(2)}, u32[]{:S(2)}) %collective-permute-start.42) | collective-permute-done | bytes 286752 | tf_op jit(solution)/shard_map/ppermute | solution.py:37
  128.8 5.5 %collective-permute-done.48 = bf16[32,5120]{1,0:T(8,128)(2,1)S(1)} collective-permute-done((bf16[32,5120]{1,0:T(8,128)(2,1)S(1)}, bf16[32,5120]{1,0:T(8,128)(2,1)S(1)}, u32[]{:S(2)}, u32[]{:S(2)}) %collective-permute-start.48) | collective-permute-done | bytes 327712 | tf_op jit(solution)/shard_map/ppermute | solution.py:37
  137.9 2.0 collective-permute-done.51
  148.9 4.8 %collective-permute-done.58.came_ref = bf16[8,5120]{1,0:T(8,128)(2,1)S(1)} collective-permute-done((bf16[8,5120]{1,0:T(8,128)(2,1)S(1)}, bf16[8,5120]{1,0:T(8,128)(2,1)S(1)}, u32[]{:S(2)}, u32[]{:S(2)}) %collective-permute-start.58) | collective-permute-done | bytes 81952 | tf_op jit(solution)/shard_map/ppermute | solution.py:37
  161.7 2.0 collective-permute-done.63
  169.4 3.8 %collective-permute-done.65.refs_3_ = bf16[32,4480]{1,0:T(8,128)(2,1)S(1)} collective-permute-done((bf16[32,4480]{1,0:T(8,128)(2,1)S(1)}, bf16[32,4480]{1,0:T(8,128)(2,1)S(1)}, u32[]{:S(2)}, u32[]{:S(2)}) %collective-permute-start.65) | collective-permute-done | bytes 286752 | tf_op jit(solution)/shard_map/ppermute | solution.py:37
  174.4 2.0 update.15
  186.7 4.6 %collective-permute-done.71 = bf16[32,5120]{1,0:T(8,128)(2,1)S(1)} collective-permute-done((bf16[32,5120]{1,0:T(8,128)(2,1)S(1)}, bf16[32,5120]{1,0:T(8,128)(2,1)S(1)}, u32[]{:S(2)}, u32[]{:S(2)}) %collective-permute-start.71) | collective-permute-done | bytes 327712 | tf_op jit(solution)/shard_map/ppermute | solution.py:37
  201.5 2.1 collective-permute-start.81
  204.6 2.1 collective-permute-start.79
  206.7 4.2 %collective-permute-done.81.came_ref = bf16[8,5120]{1,0:T(8,128)(2,1)S(1)} collective-permute-done((bf16[8,5120]{1,0:T(8,128)(2,1)S(1)}, bf16[8,5120]{1,0:T(8,128)(2,1)S(1)}, u32[]{:S(2)}, u32[]{:S(2)}) %collective-permute-start.81) | collective-permute-done | bytes 81952 | tf_op jit(solution)/shard_map/ppermute | solution.py:37
  222.3 2.4 %collective-permute-done.85.came_ref = bf16[16,4480]{1,0:T(8,128)(2,1)S(1)} collective-permute-done((bf16[16,4480]{1,0:T(8,128)(2,1)S(1)}, bf16[16,4480]{1,0:T(8,128)(2,1)S(1)}, u32[]{:S(2)}, u32[]{:S(2)}) %collective-permute-start.85) | collective-permute-done | bytes 143392 | tf_op jit(solution)/shard_map/ppermute | solution.py:37
  227.5 4.1 %collective-permute-done.88.refs_7_ = bf16[32,4480]{1,0:T(8,128)(2,1)S(1)} collective-permute-done((bf16[32,4480]{1,0:T(8,128)(2,1)S(1)}, bf16[32,4480]{1,0:T(8,128)(2,1)S(1)}, u32[]{:S(2)}, u32[]{:S(2)}) %collective-permute-start.88) | collective-permute-done | bytes 286752 | tf_op jit(solution)/shard_map/ppermute | solution.py:37
  233.2 2.7 %last.1 = f32[64,14336]{1,0:T(8,128)} custom-call(s32[1]{0:T(128)} %bitcast.mask_ref, f32[8,128]{1,0:T(8,128)S(1)} %convert_add_fusion.12.own_ref, f32[8,128]{1,0:T(8,128)S(1)} %collective-permute-done.89.other_ref, bf16[32,5120]{1,0:T(8,128)(2,1)S(1)} %constant_dynamic-update-slice_fusion.34.refs_0_, bf16[32,5120]{1,0:T(8,128)(2,1)S(1)} %collective-permute-done.90.refs_1_, ...), custom_call_target="tpu_custom_call" | custom-call | tf_op jit(solution)/shard_map/last/pallas_call | solution.py:102
  (291 shorter events, 139.0 us)
Async XLA Ops:
  10.3 10.9 %collective-permute-start.2 = (bf16[32,5120]{1,0:T(8,128)(2,1)S(1)}, bf16[32,5120]{1,0:T(8,128)(2,1)S(1)}, u32[]{:S(2)}, u32[]{:S(2)}) collective-permute-start(bf16[32,5120]{1,0:T(8,128)(2,1)S(1)} %get-tuple-element.119), channel_id=1, source_target_pairs={{0,1},{1,0},{2,3},{3,2},{4,5},{5,4},{6,7},{7,6},{8,9},{9,8},{10,11... | collective-permute-start | bytes 983048 | tf_op jit(solution)/shard_map/ppermute | solution.py:37
  13.8 9.4 %collective-permute-start.3 = (bf16[32,4864]{1,0:T(8,128)(2,1)S(1)}, bf16[32,4864]{1,0:T(8,128)(2,1)S(1)}, u32[]{:S(2)}, u32[]{:S(2)}) collective-permute-start(bf16[32,4864]{1,0:T(8,128)(2,1)S(1)} %get-tuple-element.121), channel_id=1, source_target_pairs={{0,2},{1,3},{2,0},{3,1},{4,6},{5,7},{6,4},{7,5},{8,10},{9,11},{10,... | collective-permute-start | bytes 933896 | tf_op jit(solution)/shard_map/ppermute | solution.py:37
  15.8 9.1 %collective-permute-start.1 = (bf16[32,4352]{1,0:T(8,128)(2,1)S(1)}, bf16[32,4352]{1,0:T(8,128)(2,1)S(1)}, u32[]{:S(2)}, u32[]{:S(2)}) collective-permute-start(bf16[32,4352]{1,0:T(8,128)(2,1)S(1)} %get-tuple-element.117), channel_id=1, source_target_pairs={{0,4},{1,5},{2,6},{3,7},{4,0},{5,1},{6,2},{7,3},{8,12},{9,13},{10,... | collective-permute-start | bytes 835592 | tf_op jit(solution)/shard_map/ppermute | solution.py:37
  32.0 9.1 %collective-permute-start.12 = (bf16[8,5120]{1,0:T(8,128)(2,1)S(1)}, bf16[8,5120]{1,0:T(8,128)(2,1)S(1)}, u32[]{:S(2)}, u32[]{:S(2)}) collective-permute-start(bf16[8,5120]{1,0:T(8,128)(2,1)S(1)} %fusion.3.low_ref), channel_id=1, source_target_pairs={{0,8},{1,9},{2,10},{3,11},{4,12},{5,13},{6,14},{7,15},{8,0},{9,1},... | collective-permute-start | bytes 245768 | tf_op jit(solution)/shard_map/ppermute | solution.py:37
  34.7 8.2 %collective-permute-start.11 = (bf16[8,4864]{1,0:T(8,128)(2,1)S(1)}, bf16[8,4864]{1,0:T(8,128)(2,1)S(1)}, u32[]{:S(2)}, u32[]{:S(2)}) collective-permute-start(bf16[8,4864]{1,0:T(8,128)(2,1)S(1)} %fusion.7.low_ref), channel_id=1, source_target_pairs={{0,8},{1,9},{2,10},{3,11},{4,12},{5,13},{6,14},{7,15},{8,0},{9,1},... | collective-permute-start | bytes 233480 | tf_op jit(solution)/shard_map/ppermute | solution.py:37
  36.1 8.4 %collective-permute-start.10 = (bf16[8,4352]{1,0:T(8,128)(2,1)S(1)}, bf16[8,4352]{1,0:T(8,128)(2,1)S(1)}, u32[]{:S(2)}, u32[]{:S(2)}) collective-permute-start(bf16[8,4352]{1,0:T(8,128)(2,1)S(1)} %fusion.11.low_ref), channel_id=1, source_target_pairs={{0,8},{1,9},{2,10},{3,11},{4,12},{5,13},{6,14},{7,15},{8,0},{9,1},... | collective-permute-start | bytes 208904 | tf_op jit(solution)/shard_map/ppermute | solution.py:37
  56.0 7.7 %collective-permute-start.22 = (bf16[32,5120]{1,0:T(8,128)(2,1)S(1)}, bf16[32,5120]{1,0:T(8,128)(2,1)S(1)}, u32[]{:S(2)}, u32[]{:S(2)}) collective-permute-start(bf16[32,5120]{1,0:T(8,128)(2,1)S(1)} %constant_dynamic-update-slice_fusion.4.refs_2_), channel_id=1, source_target_pairs={{0,1},{1,0},{2,3},{3,2},{4,5},{5,4},{6,7},{7,6},{8,9},{9,8},{10,11... | collective-permute-start | bytes 983048 | tf_op jit(solution)/shard_map/ppermute | solution.py:37
  57.1 7.7 %collective-permute-start.21 = (bf16[32,4864]{1,0:T(8,128)(2,1)S(1)}, bf16[32,4864]{1,0:T(8,128)(2,1)S(1)}, u32[]{:S(2)}, u32[]{:S(2)}) collective-permute-start(bf16[32,4864]{1,0:T(8,128)(2,1)S(1)} %constant_dynamic-update-slice_fusion.7.refs_2_), channel_id=1, source_target_pairs={{0,2},{1,3},{2,0},{3,1},{4,6},{5,7},{6,4},{7,5},{8,10},{9,11},{10,... | collective-permute-start | bytes 933896 | tf_op jit(solution)/shard_map/ppermute | solution.py:37
  68.7 9.8 %collective-permute-start.25 = (bf16[32,5120]{1,0:T(8,128)(2,1)S(1)}, bf16[32,5120]{1,0:T(8,128)(2,1)S(1)}, u32[]{:S(2)}, u32[]{:S(2)}) collective-permute-start(bf16[32,5120]{1,0:T(8,128)(2,1)S(1)} %get-tuple-element.145), channel_id=1, source_target_pairs={{0,1},{1,0},{2,3},{3,2},{4,5},{5,4},{6,7},{7,6},{8,9},{9,8},{10,11... | collective-permute-start | bytes 983048 | tf_op jit(solution)/shard_map/ppermute | solution.py:37
  69.8 10.7 %collective-permute-start.26 = (bf16[32,4864]{1,0:T(8,128)(2,1)S(1)}, bf16[32,4864]{1,0:T(8,128)(2,1)S(1)}, u32[]{:S(2)}, u32[]{:S(2)}) collective-permute-start(bf16[32,4864]{1,0:T(8,128)(2,1)S(1)} %get-tuple-element.147), channel_id=1, source_target_pairs={{0,2},{1,3},{2,0},{3,1},{4,6},{5,7},{6,4},{7,5},{8,10},{9,11},{10,... | collective-permute-start | bytes 933896 | tf_op jit(solution)/shard_map/ppermute | solution.py:37
  72.8 8.5 %collective-permute-start.24 = (bf16[32,4352]{1,0:T(8,128)(2,1)S(1)}, bf16[32,4352]{1,0:T(8,128)(2,1)S(1)}, u32[]{:S(2)}, u32[]{:S(2)}) collective-permute-start(bf16[32,4352]{1,0:T(8,128)(2,1)S(1)} %get-tuple-element.143), channel_id=1, source_target_pairs={{0,4},{1,5},{2,6},{3,7},{4,0},{5,1},{6,2},{7,3},{8,12},{9,13},{10,... | collective-permute-start | bytes 835592 | tf_op jit(solution)/shard_map/ppermute | solution.py:37
  88.7 9.5 %collective-permute-start.35 = (bf16[8,5120]{1,0:T(8,128)(2,1)S(1)}, bf16[8,5120]{1,0:T(8,128)(2,1)S(1)}, u32[]{:S(2)}, u32[]{:S(2)}) collective-permute-start(bf16[8,5120]{1,0:T(8,128)(2,1)S(1)} %fusion.2.low_ref), channel_id=1, source_target_pairs={{0,8},{1,9},{2,10},{3,11},{4,12},{5,13},{6,14},{7,15},{8,0},{9,1},... | collective-permute-start | bytes 245768 | tf_op jit(solution)/shard_map/ppermute | solution.py:37
  90.9 8.4 %collective-permute-start.34 = (bf16[8,4864]{1,0:T(8,128)(2,1)S(1)}, bf16[8,4864]{1,0:T(8,128)(2,1)S(1)}, u32[]{:S(2)}, u32[]{:S(2)}) collective-permute-start(bf16[8,4864]{1,0:T(8,128)(2,1)S(1)} %fusion.6.low_ref), channel_id=1, source_target_pairs={{0,8},{1,9},{2,10},{3,11},{4,12},{5,13},{6,14},{7,15},{8,0},{9,1},... | collective-permute-start | bytes 233480 | tf_op jit(solution)/shard_map/ppermute | solution.py:37
  91.9 8.8 %collective-permute-start.33 = (bf16[8,4352]{1,0:T(8,128)(2,1)S(1)}, bf16[8,4352]{1,0:T(8,128)(2,1)S(1)}, u32[]{:S(2)}, u32[]{:S(2)}) collective-permute-start(bf16[8,4352]{1,0:T(8,128)(2,1)S(1)} %fusion.10.low_ref), channel_id=1, source_target_pairs={{0,8},{1,9},{2,10},{3,11},{4,12},{5,13},{6,14},{7,15},{8,0},{9,1},... | collective-permute-start | bytes 208904 | tf_op jit(solution)/shard_map/ppermute | solution.py:37
  111.9 7.4 %collective-permute-start.45 = (bf16[32,5120]{1,0:T(8,128)(2,1)S(1)}, bf16[32,5120]{1,0:T(8,128)(2,1)S(1)}, u32[]{:S(2)}, u32[]{:S(2)}) collective-permute-start(bf16[32,5120]{1,0:T(8,128)(2,1)S(1)} %constant_dynamic-update-slice_fusion.14.refs_2_), channel_id=1, source_target_pairs={{0,1},{1,0},{2,3},{3,2},{4,5},{5,4},{6,7},{7,6},{8,9},{9,8},{10,11... | collective-permute-start | bytes 983048 | tf_op jit(solution)/shard_map/ppermute | solution.py:37
  112.8 7.6 %collective-permute-start.44 = (bf16[32,4864]{1,0:T(8,128)(2,1)S(1)}, bf16[32,4864]{1,0:T(8,128)(2,1)S(1)}, u32[]{:S(2)}, u32[]{:S(2)}) collective-permute-start(bf16[32,4864]{1,0:T(8,128)(2,1)S(1)} %constant_dynamic-update-slice_fusion.17.refs_2_), channel_id=1, source_target_pairs={{0,2},{1,3},{2,0},{3,1},{4,6},{5,7},{6,4},{7,5},{8,10},{9,11},{10,... | collective-permute-start | bytes 933896 | tf_op jit(solution)/shard_map/ppermute | solution.py:37
  124.5 9.9 %collective-permute-start.48 = (bf16[32,5120]{1,0:T(8,128)(2,1)S(1)}, bf16[32,5120]{1,0:T(8,128)(2,1)S(1)}, u32[]{:S(2)}, u32[]{:S(2)}) collective-permute-start(bf16[32,5120]{1,0:T(8,128)(2,1)S(1)} %get-tuple-element.174), channel_id=1, source_target_pairs={{0,1},{1,0},{2,3},{3,2},{4,5},{5,4},{6,7},{7,6},{8,9},{9,8},{10,11... | collective-permute-start | bytes 983048 | tf_op jit(solution)/shard_map/ppermute | solution.py:37
  125.7 9.8 %collective-permute-start.49 = (bf16[32,4864]{1,0:T(8,128)(2,1)S(1)}, bf16[32,4864]{1,0:T(8,128)(2,1)S(1)}, u32[]{:S(2)}, u32[]{:S(2)}) collective-permute-start(bf16[32,4864]{1,0:T(8,128)(2,1)S(1)} %get-tuple-element.176), channel_id=1, source_target_pairs={{0,2},{1,3},{2,0},{3,1},{4,6},{5,7},{6,4},{7,5},{8,10},{9,11},{10,... | collective-permute-start | bytes 933896 | tf_op jit(solution)/shard_map/ppermute | solution.py:37
  127.3 9.6 %collective-permute-start.47 = (bf16[32,4352]{1,0:T(8,128)(2,1)S(1)}, bf16[32,4352]{1,0:T(8,128)(2,1)S(1)}, u32[]{:S(2)}, u32[]{:S(2)}) collective-permute-start(bf16[32,4352]{1,0:T(8,128)(2,1)S(1)} %get-tuple-element.172), channel_id=1, source_target_pairs={{0,4},{1,5},{2,6},{3,7},{4,0},{5,1},{6,2},{7,3},{8,12},{9,13},{10,... | collective-permute-start | bytes 835592 | tf_op jit(solution)/shard_map/ppermute | solution.py:37
  144.5 9.2 %collective-permute-start.58 = (bf16[8,5120]{1,0:T(8,128)(2,1)S(1)}, bf16[8,5120]{1,0:T(8,128)(2,1)S(1)}, u32[]{:S(2)}, u32[]{:S(2)}) collective-permute-start(bf16[8,5120]{1,0:T(8,128)(2,1)S(1)} %fusion.1.low_ref), channel_id=1, source_target_pairs={{0,8},{1,9},{2,10},{3,11},{4,12},{5,13},{6,14},{7,15},{8,0},{9,1},... | collective-permute-start | bytes 245768 | tf_op jit(solution)/shard_map/ppermute | solution.py:37
  145.8 8.9 %collective-permute-start.57 = (bf16[8,4864]{1,0:T(8,128)(2,1)S(1)}, bf16[8,4864]{1,0:T(8,128)(2,1)S(1)}, u32[]{:S(2)}, u32[]{:S(2)}) collective-permute-start(bf16[8,4864]{1,0:T(8,128)(2,1)S(1)} %fusion.5.low_ref), channel_id=1, source_target_pairs={{0,8},{1,9},{2,10},{3,11},{4,12},{5,13},{6,14},{7,15},{8,0},{9,1},... | collective-permute-start | bytes 233480 | tf_op jit(solution)/shard_map/ppermute | solution.py:37
  147.6 7.9 %collective-permute-start.56 = (bf16[8,4352]{1,0:T(8,128)(2,1)S(1)}, bf16[8,4352]{1,0:T(8,128)(2,1)S(1)}, u32[]{:S(2)}, u32[]{:S(2)}) collective-permute-start(bf16[8,4352]{1,0:T(8,128)(2,1)S(1)} %fusion.9.low_ref), channel_id=1, source_target_pairs={{0,8},{1,9},{2,10},{3,11},{4,12},{5,13},{6,14},{7,15},{8,0},{9,1},... | collective-permute-start | bytes 208904 | tf_op jit(solution)/shard_map/ppermute | solution.py:37
  166.9 7.5 %collective-permute-start.68 = (bf16[32,5120]{1,0:T(8,128)(2,1)S(1)}, bf16[32,5120]{1,0:T(8,128)(2,1)S(1)}, u32[]{:S(2)}, u32[]{:S(2)}) collective-permute-start(bf16[32,5120]{1,0:T(8,128)(2,1)S(1)} %constant_dynamic-update-slice_fusion.24.refs_2_), channel_id=1, source_target_pairs={{0,1},{1,0},{2,3},{3,2},{4,5},{5,4},{6,7},{7,6},{8,9},{9,8},{10,11... | collective-permute-start | bytes 983048 | tf_op jit(solution)/shard_map/ppermute | solution.py:37
  168.6 7.7 %collective-permute-start.67 = (bf16[32,4864]{1,0:T(8,128)(2,1)S(1)}, bf16[32,4864]{1,0:T(8,128)(2,1)S(1)}, u32[]{:S(2)}, u32[]{:S(2)}) collective-permute-start(bf16[32,4864]{1,0:T(8,128)(2,1)S(1)} %constant_dynamic-update-slice_fusion.27.refs_2_), channel_id=1, source_target_pairs={{0,2},{1,3},{2,0},{3,1},{4,6},{5,7},{6,4},{7,5},{8,10},{9,11},{10,... | collective-permute-start | bytes 933896 | tf_op jit(solution)/shard_map/ppermute | solution.py:37
  181.4 9.8 %collective-permute-start.71 = (bf16[32,5120]{1,0:T(8,128)(2,1)S(1)}, bf16[32,5120]{1,0:T(8,128)(2,1)S(1)}, u32[]{:S(2)}, u32[]{:S(2)}) collective-permute-start(bf16[32,5120]{1,0:T(8,128)(2,1)S(1)} %get-tuple-element.203), channel_id=1, source_target_pairs={{0,1},{1,0},{2,3},{3,2},{4,5},{5,4},{6,7},{7,6},{8,9},{9,8},{10,11... | collective-permute-start | bytes 983048 | tf_op jit(solution)/shard_map/ppermute | solution.py:37
  183.5 9.2 %collective-permute-start.72 = (bf16[32,4864]{1,0:T(8,128)(2,1)S(1)}, bf16[32,4864]{1,0:T(8,128)(2,1)S(1)}, u32[]{:S(2)}, u32[]{:S(2)}) collective-permute-start(bf16[32,4864]{1,0:T(8,128)(2,1)S(1)} %get-tuple-element.205), channel_id=1, source_target_pairs={{0,2},{1,3},{2,0},{3,1},{4,6},{5,7},{6,4},{7,5},{8,10},{9,11},{10,... | collective-permute-start | bytes 933896 | tf_op jit(solution)/shard_map/ppermute | solution.py:37
  185.4 8.8 %collective-permute-start.70 = (bf16[32,4352]{1,0:T(8,128)(2,1)S(1)}, bf16[32,4352]{1,0:T(8,128)(2,1)S(1)}, u32[]{:S(2)}, u32[]{:S(2)}) collective-permute-start(bf16[32,4352]{1,0:T(8,128)(2,1)S(1)} %get-tuple-element.201), channel_id=1, source_target_pairs={{0,4},{1,5},{2,6},{3,7},{4,0},{5,1},{6,2},{7,3},{8,12},{9,13},{10,... | collective-permute-start | bytes 835592 | tf_op jit(solution)/shard_map/ppermute | solution.py:37
  201.5 9.5 %collective-permute-start.81 = (bf16[8,5120]{1,0:T(8,128)(2,1)S(1)}, bf16[8,5120]{1,0:T(8,128)(2,1)S(1)}, u32[]{:S(2)}, u32[]{:S(2)}) collective-permute-start(bf16[8,5120]{1,0:T(8,128)(2,1)S(1)} %fusion.low_ref), channel_id=1, source_target_pairs={{0,8},{1,9},{2,10},{3,11},{4,12},{5,13},{6,14},{7,15},{8,0},{9,1},... | collective-permute-start | bytes 245768 | tf_op jit(solution)/shard_map/ppermute | solution.py:37
  203.6 8.2 %collective-permute-start.80 = (bf16[8,4864]{1,0:T(8,128)(2,1)S(1)}, bf16[8,4864]{1,0:T(8,128)(2,1)S(1)}, u32[]{:S(2)}, u32[]{:S(2)}) collective-permute-start(bf16[8,4864]{1,0:T(8,128)(2,1)S(1)} %fusion.4.low_ref), channel_id=1, source_target_pairs={{0,8},{1,9},{2,10},{3,11},{4,12},{5,13},{6,14},{7,15},{8,0},{9,1},... | collective-permute-start | bytes 233480 | tf_op jit(solution)/shard_map/ppermute | solution.py:37
  204.6 8.8 %collective-permute-start.79 = (bf16[8,4352]{1,0:T(8,128)(2,1)S(1)}, bf16[8,4352]{1,0:T(8,128)(2,1)S(1)}, u32[]{:S(2)}, u32[]{:S(2)}) collective-permute-start(bf16[8,4352]{1,0:T(8,128)(2,1)S(1)} %fusion.8.low_ref), channel_id=1, source_target_pairs={{0,8},{1,9},{2,10},{3,11},{4,12},{5,13},{6,14},{7,15},{8,0},{9,1},... | collective-permute-start | bytes 208904 | tf_op jit(solution)/shard_map/ppermute | solution.py:37
  226.0 7.2 %collective-permute-start.90 = (bf16[32,5120]{1,0:T(8,128)(2,1)S(1)}, bf16[32,5120]{1,0:T(8,128)(2,1)S(1)}, u32[]{:S(2)}, u32[]{:S(2)}) collective-permute-start(bf16[32,5120]{1,0:T(8,128)(2,1)S(1)} %constant_dynamic-update-slice_fusion.34.refs_0_), channel_id=1, source_target_pairs={{0,1},{1,0},{2,3},{3,2},{4,5},{5,4},{6,7},{7,6},{8,9},{9,8},{10,11... | collective-permute-start | bytes 983048 | tf_op jit(solution)/shard_map/ppermute | solution.py:37
  226.3 6.9 %collective-permute-start.91 = (bf16[32,4864]{1,0:T(8,128)(2,1)S(1)}, bf16[32,4864]{1,0:T(8,128)(2,1)S(1)}, u32[]{:S(2)}, u32[]{:S(2)}) collective-permute-start(bf16[32,4864]{1,0:T(8,128)(2,1)S(1)} %constant_dynamic-update-slice_fusion.37.refs_3_), channel_id=1, source_target_pairs={{0,2},{1,3},{2,0},{3,1},{4,6},{5,7},{6,4},{7,5},{8,10},{9,11},{10,... | collective-permute-start | bytes 933896 | tf_op jit(solution)/shard_map/ppermute | solution.py:37
  (64 other events, 295.1 us)

commit v4 on v3

--- a/solution.py
+++ b/solution.py
@@ -13,7 +13,7 @@
 THRESHOLD = 0.2
 EPSILON = 1e-06
 GROUP = 8
-SHARES = (20, 19, 17)
+SHARES = (16, 16, 16, 8)
 PARTS = len(SHARES)
 LANES = 128
 VMEM_BYTES = 4 * 1024 * 1024
@@ -59,7 +59,9 @@
         edges = [self.unit * round(units * m / marks[-1]) for m in marks]
         self.spans = list(zip(edges[:-1], edges[1:]))
         self.widths = [b - a for a, b in self.spans]
-        self.orders = [[(p + s) % self.rows_bits for s in range(self.rows_bits)] for p in range(PARTS)]
+        levels = range(self.rows_bits)
+        self.scatter = [[(p + s) % self.rows_bits for s in levels] for p in range(PARTS)]
+        self.gather = [[(p + s) % self.rows_bits for s in levels] for p in range(PARTS)]
 
     def blocks(self, p):
         a, b = self.spans[p]
@@ -68,9 +70,9 @@
     def bit_value(self, level):
         return self.places >> (level + 1)
 
-    def arrangement(self, p):
+    def arrangement(self, levels):
         result = [0]
-        for level in reversed(self.orders[p]):
+        for level in levels:
             result = result + [g + self.bit_value(level) for g in result]
         return result
 
@@ -83,10 +85,10 @@
         return jnp.concatenate([x[h * g : h * (g + 1)] for g in places], 0)
 
     def to_part(self, p, x):
-        return self.rearranged(x, self.arrangement(p))
+        return self.rearranged(x, self.arrangement(self.scatter[p][::-1]))
 
     def from_part(self, p, x):
-        order = self.arrangement(p)
+        order = self.arrangement(self.gather[p])
         return self.rearranged(x, [order.index(g) for g in range(self.places)])
 
 
@@ -109,22 +111,28 @@
     )(*args)
 
 
-def first_kernel(plan, mask_ref, dense_ref, targets_ref, act_ref, *refs):
-    *start_refs, wanted_ref, product_ref = refs
+def order_kernel(plan, mask_ref, targets_ref, wanted_ref):
     h = plan.height
     for g in range(plan.places):
         rows = pl.ds(pl.multiple_of((g ^ mask_ref[0]) * h, h), h)
         wanted_ref[g * h : (g + 1) * h] = targets_ref[rows, :]
+
+
+def start_kernel(plan, mask_ref, dense_ref, *start_refs):
+    h = plan.height
+    for p in range(PARTS):
+        for g in range(plan.places):
+            rows = pl.ds(pl.multiple_of((g ^ mask_ref[0]) * h, h), h)
+            for here, there in plan.blocks(p):
+                start_refs[p][g * h : (g + 1) * h, here] = dense_ref[rows, there]
+
+
+def first_kernel(plan, *refs):
+    *start_refs, act_ref, product_ref = refs
     total = jnp.zeros(product_ref.shape, f32)
-    for p, (a, b) in enumerate(plan.spans):
-        for start in range(a, b, plan.unit):
-            groups = []
-            for g in range(plan.places):
-                rows = pl.ds(pl.multiple_of((g ^ mask_ref[0]) * h, h), h)
-                groups.append(dense_ref[rows, start : start + plan.unit])
-            block = jnp.concatenate(groups, 0)
-            start_refs[p][:, start - a : start - a + plan.unit] = block
-            total = total + dot_nt(block.astype(bf16), act_ref[:, start : start + plan.unit])
+    for p in range(PARTS):
+        for here, there in plan.blocks(p):
+            total = total + dot_nt(start_refs[p][:, here].astype(bf16), act_ref[:, there])
     product_ref[...] = total
 
 
@@ -224,7 +232,7 @@
     current = [kept for kept, _ in pieces]
     sends = [sent for _, sent in pieces]
     for stage in range(plan.rows_bits):
-        came = [swap(sends[p], "tok", plan.orders[p][stage]) for p in range(PARTS)]
+        came = [swap(sends[p], "tok", plan.scatter[p][stage]) for p in range(PARTS)]
         for p in range(PARTS):
             arrived = after(came[p], sends[:p]) if p else came[p]
             whole = current[p] + arrived.astype(f32)
@@ -243,9 +251,9 @@
         current[p], *square = run(
             functools.partial(combine_kernel, plan, p), "combine", outs, [VMEM] * (2 + len(square)), (sends[p], came[p], *square)
         )
-    for stage in reversed(range(plan.rows_bits)):
-        came = [swap(current[p], "tok", plan.orders[p][stage]) for p in range(PARTS)]
-        if stage:
+    for stage in range(plan.rows_bits):
+        came = [swap(current[p], "tok", plan.gather[p][stage]) for p in range(PARTS)]
+        if stage + 1 < plan.rows_bits:
             for p in range(PARTS):
                 rows, width = current[p].shape
                 arrived = after(came[p], current[:p]) if p else came[p]
@@ -274,13 +282,12 @@
     states = [((rows, width), f32) for width in plan.widths]
     small = ((rows, tokens), f32)
 
-    *ahead, wanted, product = run(
-        functools.partial(first_kernel, plan),
-        "first",
-        states + [small, small],
-        [SMEM, VMEM, VMEM, VMEM],
-        (mask, dense_rows, targets.T, activations),
+    ahead = run(functools.partial(start_kernel, plan), "start", states, [SMEM, VMEM], (mask, dense_rows))
+    ahead = list(ahead)
+    (product,) = run(
+        functools.partial(first_kernel, plan), "first", [small], [VMEM] * (PARTS + 1), (*ahead, activations)
     )
+    (wanted,) = run(functools.partial(order_kernel, plan), "order", [small], [SMEM, VMEM], (mask, targets.T))
     weights = list(ahead)
     for iteration in range(ITERS):
         own, other = across_features(product)

time: 236 us -> 228 us (0.966)
  waiting for transfers between devices: 98.5 us -> 61.1 us
  starting transfers between devices: 103 us -> 132 us
    ppermute x92 -> x120, waiting for transfers between devices: 98.5 us -> 61.1 us  [swap(): return lax.ppermute(x, axis, pairs)]
    ppermute x92 -> x120, starting transfers between devices: 103 us -> 132 us  [swap(): return lax.ppermute(x, axis, pairs)]
    pallas_call x43 -> x56, Pallas kernels: 25.3 us -> 27 us  [run(): pl.pallas_call(kernel, out_shape=tuple((jax.ShapeDtypeStruct(shape, dtype...]
    unnamed x24 -> x32, local copies, waits for them, and re-layouts: 6.15 us -> 5.36 us
  transfers between devices with their start and end apart: 92 -> 120, of which waited for: 58 -> 55; matrix products, arithmetic and copies ran while one was open for 1% -> 1% of each run, Pallas kernels for 4% -> 6%
where the time goes in v4:
time: 228 us
  starting transfers between devices  132 us (58%)
  waiting for transfers between devices  61.1 us (27%)
  Pallas kernels  27 us (12%)
  local copies, waits for them, and re-layouts  5.84 us (3%)
    ppermute x120, starting transfers between devices, swap(): return lax.ppermute(x, axis, pairs)  132 us
    ppermute x120, waiting for transfers between devices, swap(): return lax.ppermute(x, axis, pairs)  61.1 us
    pallas_call x56, Pallas kernels, run(): pl.pallas_call(kernel, out_shape=tuple((jax.ShapeDtypeStruct(shape, dtype...  27 us
    unnamed x32, local copies, waits for them, and re-layouts  5.36 us
  transfers between devices with their start and end apart: 120, of which 55 were waited for; matrix products, arithmetic and copies ran while one was open for 1% of the time, Pallas kernels for 6%

profile of v4, /device:TPU:0, one launch (start us, length us, event | category | flops | bytes accessed | tf_op | source)
XLA Modules:
  0.0 228.0 jit_solution(4957090277304694383)
XLA Ops:
  0.0 2.0 copy-done.2
  2.3 3.1 %copy-done = bf16[256,14336]{1,0:T(8,128)(2,1)S(1)} copy-done((bf16[256,14336]{1,0:T(8,128)(2,1)S(1)}, bf16[256,14336]{1,0:T(8,128)(2,1)}, u32[]{:S(2)}) %copy-start) | copy-done | bytes 7340056
  5.4 2.4 %first.1.own_ref = f32[64,256]{1,0:T(8,128)S(1)} custom-call(f32[64,4096]{1,0:T(8,128)S(1)} %get-tuple-element.157.refs_0_.refs_4_.refs_5_, f32[64,4096]{1,0:T(8,128)S(1)} %get-tuple-element.158.refs_1_.refs_4_.refs_5_, f32[64,4096]{1,0:T(8,128)S(1)} %get-tuple-element.159.refs_2_.refs_4_.refs_5_, f32[64,2048]{1,0:T(8,128)S(1)} %get-tuple-element.160.refs_3_.refs_4_.refs_5_, ...), custom_call_target="tpu_custom_call" | custom-call | tf_op jit(solution)/shard_map/first/pallas_call | solution.py:104
  9.6 2.9 %collective-permute-start.2 = (bf16[32,4096]{1,0:T(8,128)(2,1)S(1)}, bf16[32,4096]{1,0:T(8,128)(2,1)S(1)}, u32[]{:S(2)}, u32[]{:S(2)}) collective-permute-start(bf16[32,4096]{1,0:T(8,128)(2,1)S(1)} %get-tuple-element.164), channel_id=1, source_target_pairs={{0,1},{1,0},{2,3},{3,2},{4,5},{5,4},{6,7},{7,6},{8,9},{9,8},{10,11... | collective-permute-start | bytes 786440 | tf_op jit(solution)/shard_map/ppermute | solution.py:37
  15.1 1.6 collective-permute-start.4
  19.3 2.5 %collective-permute-start.6 = (bf16[16,4096]{1,0:T(8,128)(2,1)S(1)}, bf16[16,4096]{1,0:T(8,128)(2,1)S(1)}, u32[]{:S(2)}, u32[]{:S(2)}) collective-permute-start(bf16[16,4096]{1,0:T(8,128)(2,1)S(1)} %slice.507), channel_id=1, source_target_pairs={{0,2},{1,3},{2,0},{3,1},{4,6},{5,7},{6,4},{7,5},{8,10},{9,11},{10,... | collective-permute-start | bytes 393224 | tf_op jit(solution)/shard_map/ppermute | solution.py:37
  22.0 1.6 collective-permute-start.7
  25.9 1.7 collective-permute-start.10
  31.5 2.7 %collective-permute-start.16 = (bf16[8,4096]{1,0:T(8,128)(2,1)S(1)}, bf16[8,4096]{1,0:T(8,128)(2,1)S(1)}, u32[]{:S(2)}, u32[]{:S(2)}) collective-permute-start(bf16[8,4096]{1,0:T(8,128)(2,1)S(1)} %fusion.11.low_ref), channel_id=1, source_target_pairs={{0,8},{1,9},{2,10},{3,11},{4,12},{5,13},{6,14},{7,15},{8,0},{9,1},... | collective-permute-start | bytes 196616 | tf_op jit(solution)/shard_map/ppermute | solution.py:37
  34.8 2.5 %collective-permute-start.14 = (bf16[8,4096]{1,0:T(8,128)(2,1)S(1)}, bf16[8,4096]{1,0:T(8,128)(2,1)S(1)}, u32[]{:S(2)}, u32[]{:S(2)}) collective-permute-start(bf16[8,4096]{1,0:T(8,128)(2,1)S(1)} %fusion.9.low_ref), channel_id=1, source_target_pairs={{0,8},{1,9},{2,10},{3,11},{4,12},{5,13},{6,14},{7,15},{8,0},{9,1},... | collective-permute-start | bytes 196616 | tf_op jit(solution)/shard_map/ppermute | solution.py:37
  40.1 2.2 collective-permute-start.19
  44.8 1.7 collective-permute-start.23
  50.4 2.4 %collective-permute-done.24 = bf16[16,4096]{1,0:T(8,128)(2,1)S(1)} collective-permute-done((bf16[16,4096]{1,0:T(8,128)(2,1)S(1)}, bf16[16,4096]{1,0:T(8,128)(2,1)S(1)}, u32[]{:S(2)}, u32[]{:S(2)}) %collective-permute-start.24) | collective-permute-done | bytes 131104 | tf_op jit(solution)/shard_map/ppermute | solution.py:37
  59.4 1.6 collective-permute-done.29.refs_3_
  71.4 3.9 %collective-permute-done.32 = bf16[32,4096]{1,0:T(8,128)(2,1)S(1)} collective-permute-done((bf16[32,4096]{1,0:T(8,128)(2,1)S(1)}, bf16[32,4096]{1,0:T(8,128)(2,1)S(1)}, u32[]{:S(2)}, u32[]{:S(2)}) %collective-permute-start.32) | collective-permute-done | bytes 262176 | tf_op jit(solution)/shard_map/ppermute | solution.py:37
  85.6 2.3 collective-permute-start.46
  88.7 2.3 collective-permute-start.44
  102.6 2.4 %collective-permute-done.53 = bf16[16,4096]{1,0:T(8,128)(2,1)S(1)} collective-permute-done((bf16[16,4096]{1,0:T(8,128)(2,1)S(1)}, bf16[16,4096]{1,0:T(8,128)(2,1)S(1)}, u32[]{:S(2)}, u32[]{:S(2)}) %collective-permute-start.53) | collective-permute-done | bytes 131104 | tf_op jit(solution)/shard_map/ppermute | solution.py:37
  112.8 1.6 collective-permute-done.59.refs_3_
  125.2 3.5 %collective-permute-done.62 = bf16[32,4096]{1,0:T(8,128)(2,1)S(1)} collective-permute-done((bf16[32,4096]{1,0:T(8,128)(2,1)S(1)}, bf16[32,4096]{1,0:T(8,128)(2,1)S(1)}, u32[]{:S(2)}, u32[]{:S(2)}) %collective-permute-start.62) | collective-permute-done | bytes 262176 | tf_op jit(solution)/shard_map/ppermute | solution.py:37
  140.5 1.9 collective-permute-start.75
  143.6 1.9 collective-permute-start.73
  155.6 2.7 %collective-permute-done.83 = bf16[16,4096]{1,0:T(8,128)(2,1)S(1)} collective-permute-done((bf16[16,4096]{1,0:T(8,128)(2,1)S(1)}, bf16[16,4096]{1,0:T(8,128)(2,1)S(1)}, u32[]{:S(2)}, u32[]{:S(2)}) %collective-permute-start.83) | collective-permute-done | bytes 131104 | tf_op jit(solution)/shard_map/ppermute | solution.py:37
  167.5 1.7 update.20
  169.2 1.7 update.21
  170.9 1.7 update.22
  180.8 3.9 %collective-permute-done.92 = bf16[32,4096]{1,0:T(8,128)(2,1)S(1)} collective-permute-done((bf16[32,4096]{1,0:T(8,128)(2,1)S(1)}, bf16[32,4096]{1,0:T(8,128)(2,1)S(1)}, u32[]{:S(2)}, u32[]{:S(2)}) %collective-permute-start.92) | collective-permute-done | bytes 262176 | tf_op jit(solution)/shard_map/ppermute | solution.py:37
  195.2 2.3 collective-permute-start.106
  198.3 2.3 collective-permute-start.104
  212.2 2.8 %collective-permute-done.113 = bf16[16,4096]{1,0:T(8,128)(2,1)S(1)} collective-permute-done((bf16[16,4096]{1,0:T(8,128)(2,1)S(1)}, bf16[16,4096]{1,0:T(8,128)(2,1)S(1)}, u32[]{:S(2)}, u32[]{:S(2)}) %collective-permute-start.113) | collective-permute-done | bytes 131104 | tf_op jit(solution)/shard_map/ppermute | solution.py:37
  222.1 1.6 collective-permute-done.119.refs_7_
  225.2 2.7 %last.1 = f32[64,14336]{1,0:T(8,128)} custom-call(s32[1]{0:T(128)} %bitcast.mask_ref, f32[8,128]{1,0:T(8,128)S(1)} %convert_add_fusion.16.own_ref, f32[8,128]{1,0:T(8,128)S(1)} %collective-permute-done.116.other_ref, bf16[32,4096]{1,0:T(8,128)(2,1)S(1)} %constant_dynamic-update-slice_fusion.51.refs_0_, ...), custom_call_target="tpu_custom_call" | custom-call | tf_op jit(solution)/shard_map/last/pallas_call | solution.py:104
  (392 shorter events, 153.0 us)
Async XLA Ops:
  9.6 9.6 %collective-permute-start.2 = (bf16[32,4096]{1,0:T(8,128)(2,1)S(1)}, bf16[32,4096]{1,0:T(8,128)(2,1)S(1)}, u32[]{:S(2)}, u32[]{:S(2)}) collective-permute-start(bf16[32,4096]{1,0:T(8,128)(2,1)S(1)} %get-tuple-element.164), channel_id=1, source_target_pairs={{0,1},{1,0},{2,3},{3,2},{4,5},{5,4},{6,7},{7,6},{8,9},{9,8},{10,11... | collective-permute-start | bytes 786440 | tf_op jit(solution)/shard_map/ppermute | solution.py:37
  13.0 8.8 %collective-permute-start.3 = (bf16[32,4096]{1,0:T(8,128)(2,1)S(1)}, bf16[32,4096]{1,0:T(8,128)(2,1)S(1)}, u32[]{:S(2)}, u32[]{:S(2)}) collective-permute-start(bf16[32,4096]{1,0:T(8,128)(2,1)S(1)} %get-tuple-element.166), channel_id=1, source_target_pairs={{0,2},{1,3},{2,0},{3,1},{4,6},{5,7},{6,4},{7,5},{8,10},{9,11},{10,... | collective-permute-start | bytes 786440 | tf_op jit(solution)/shard_map/ppermute | solution.py:37
  15.1 8.5 %collective-permute-start.4 = (bf16[32,4096]{1,0:T(8,128)(2,1)S(1)}, bf16[32,4096]{1,0:T(8,128)(2,1)S(1)}, u32[]{:S(2)}, u32[]{:S(2)}) collective-permute-start(bf16[32,4096]{1,0:T(8,128)(2,1)S(1)} %get-tuple-element.169), channel_id=1, source_target_pairs={{0,4},{1,5},{2,6},{3,7},{4,0},{5,1},{6,2},{7,3},{8,12},{9,13},{10,... | collective-permute-start | bytes 786440 | tf_op jit(solution)/shard_map/ppermute | solution.py:37
  17.1 8.2 %collective-permute-start.1 = (bf16[32,2048]{1,0:T(8,128)(2,1)S(1)}, bf16[32,2048]{1,0:T(8,128)(2,1)S(1)}, u32[]{:S(2)}, u32[]{:S(2)}) collective-permute-start(bf16[32,2048]{1,0:T(8,128)(2,1)S(1)} %get-tuple-element.162), channel_id=1, source_target_pairs={{0,1},{1,0},{2,3},{3,2},{4,5},{5,4},{6,7},{7,6},{8,9},{9,8},{10,11... | collective-permute-start | bytes 393224 | tf_op jit(solution)/shard_map/ppermute | solution.py:37
  19.3 6.5 %collective-permute-start.6 = (bf16[16,4096]{1,0:T(8,128)(2,1)S(1)}, bf16[16,4096]{1,0:T(8,128)(2,1)S(1)}, u32[]{:S(2)}, u32[]{:S(2)}) collective-permute-start(bf16[16,4096]{1,0:T(8,128)(2,1)S(1)} %slice.507), channel_id=1, source_target_pairs={{0,2},{1,3},{2,0},{3,1},{4,6},{5,7},{6,4},{7,5},{8,10},{9,11},{10,... | collective-permute-start | bytes 393224 | tf_op jit(solution)/shard_map/ppermute | solution.py:37
  31.5 7.2 %collective-permute-start.16 = (bf16[8,4096]{1,0:T(8,128)(2,1)S(1)}, bf16[8,4096]{1,0:T(8,128)(2,1)S(1)}, u32[]{:S(2)}, u32[]{:S(2)}) collective-permute-start(bf16[8,4096]{1,0:T(8,128)(2,1)S(1)} %fusion.11.low_ref), channel_id=1, source_target_pairs={{0,8},{1,9},{2,10},{3,11},{4,12},{5,13},{6,14},{7,15},{8,0},{9,1},... | collective-permute-start | bytes 196616 | tf_op jit(solution)/shard_map/ppermute | solution.py:37
  34.8 7.6 %collective-permute-start.14 = (bf16[8,4096]{1,0:T(8,128)(2,1)S(1)}, bf16[8,4096]{1,0:T(8,128)(2,1)S(1)}, u32[]{:S(2)}, u32[]{:S(2)}) collective-permute-start(bf16[8,4096]{1,0:T(8,128)(2,1)S(1)} %fusion.9.low_ref), channel_id=1, source_target_pairs={{0,8},{1,9},{2,10},{3,11},{4,12},{5,13},{6,14},{7,15},{8,0},{9,1},... | collective-permute-start | bytes 196616 | tf_op jit(solution)/shard_map/ppermute | solution.py:37
  54.1 6.9 %collective-permute-start.29 = (bf16[32,4096]{1,0:T(8,128)(2,1)S(1)}, bf16[32,4096]{1,0:T(8,128)(2,1)S(1)}, u32[]{:S(2)}, u32[]{:S(2)}) collective-permute-start(bf16[32,4096]{1,0:T(8,128)(2,1)S(1)} %constant_dynamic-update-slice_fusion.6.refs_2_), channel_id=1, source_target_pairs={{0,4},{1,5},{2,6},{3,7},{4,0},{5,1},{6,2},{7,3},{8,12},{9,13},{10,... | collective-permute-start | bytes 786440 | tf_op jit(solution)/shard_map/ppermute | solution.py:37
  55.2 6.7 %collective-permute-start.28 = (bf16[32,4096]{1,0:T(8,128)(2,1)S(1)}, bf16[32,4096]{1,0:T(8,128)(2,1)S(1)}, u32[]{:S(2)}, u32[]{:S(2)}) collective-permute-start(bf16[32,4096]{1,0:T(8,128)(2,1)S(1)} %constant_dynamic-update-slice_fusion.9.refs_2_), channel_id=1, source_target_pairs={{0,1},{1,0},{2,3},{3,2},{4,5},{5,4},{6,7},{7,6},{8,9},{9,8},{10,11... | collective-permute-start | bytes 786440 | tf_op jit(solution)/shard_map/ppermute | solution.py:37
  56.3 6.4 %collective-permute-start.27 = (bf16[32,4096]{1,0:T(8,128)(2,1)S(1)}, bf16[32,4096]{1,0:T(8,128)(2,1)S(1)}, u32[]{:S(2)}, u32[]{:S(2)}) collective-permute-start(bf16[32,4096]{1,0:T(8,128)(2,1)S(1)} %constant_dynamic-update-slice_fusion.12.refs_2_), channel_id=1, source_target_pairs={{0,2},{1,3},{2,0},{3,1},{4,6},{5,7},{6,4},{7,5},{8,10},{9,11},{10,... | collective-permute-start | bytes 786440 | tf_op jit(solution)/shard_map/ppermute | solution.py:37
  66.0 9.2 %collective-permute-start.32 = (bf16[32,4096]{1,0:T(8,128)(2,1)S(1)}, bf16[32,4096]{1,0:T(8,128)(2,1)S(1)}, u32[]{:S(2)}, u32[]{:S(2)}) collective-permute-start(bf16[32,4096]{1,0:T(8,128)(2,1)S(1)} %get-tuple-element.197), channel_id=1, source_target_pairs={{0,1},{1,0},{2,3},{3,2},{4,5},{5,4},{6,7},{7,6},{8,9},{9,8},{10,11... | collective-permute-start | bytes 786440 | tf_op jit(solution)/shard_map/ppermute | solution.py:37
  67.8 8.7 %collective-permute-start.33 = (bf16[32,4096]{1,0:T(8,128)(2,1)S(1)}, bf16[32,4096]{1,0:T(8,128)(2,1)S(1)}, u32[]{:S(2)}, u32[]{:S(2)}) collective-permute-start(bf16[32,4096]{1,0:T(8,128)(2,1)S(1)} %get-tuple-element.199), channel_id=1, source_target_pairs={{0,2},{1,3},{2,0},{3,1},{4,6},{5,7},{6,4},{7,5},{8,10},{9,11},{10,... | collective-permute-start | bytes 786440 | tf_op jit(solution)/shard_map/ppermute | solution.py:37
  69.0 8.3 %collective-permute-start.34 = (bf16[32,4096]{1,0:T(8,128)(2,1)S(1)}, bf16[32,4096]{1,0:T(8,128)(2,1)S(1)}, u32[]{:S(2)}, u32[]{:S(2)}) collective-permute-start(bf16[32,4096]{1,0:T(8,128)(2,1)S(1)} %get-tuple-element.202), channel_id=1, source_target_pairs={{0,4},{1,5},{2,6},{3,7},{4,0},{5,1},{6,2},{7,3},{8,12},{9,13},{10,... | collective-permute-start | bytes 786440 | tf_op jit(solution)/shard_map/ppermute | solution.py:37
  70.6 8.2 %collective-permute-start.31 = (bf16[32,2048]{1,0:T(8,128)(2,1)S(1)}, bf16[32,2048]{1,0:T(8,128)(2,1)S(1)}, u32[]{:S(2)}, u32[]{:S(2)}) collective-permute-start(bf16[32,2048]{1,0:T(8,128)(2,1)S(1)} %get-tuple-element.195), channel_id=1, source_target_pairs={{0,1},{1,0},{2,3},{3,2},{4,5},{5,4},{6,7},{7,6},{8,9},{9,8},{10,11... | collective-permute-start | bytes 393224 | tf_op jit(solution)/shard_map/ppermute | solution.py:37
  88.7 6.5 %collective-permute-start.44 = (bf16[8,4096]{1,0:T(8,128)(2,1)S(1)}, bf16[8,4096]{1,0:T(8,128)(2,1)S(1)}, u32[]{:S(2)}, u32[]{:S(2)}) collective-permute-start(bf16[8,4096]{1,0:T(8,128)(2,1)S(1)} %fusion.6.low_ref), channel_id=1, source_target_pairs={{0,8},{1,9},{2,10},{3,11},{4,12},{5,13},{6,14},{7,15},{8,0},{9,1},... | collective-permute-start | bytes 196616 | tf_op jit(solution)/shard_map/ppermute | solution.py:37
  98.5 6.4 %collective-permute-start.53 = (bf16[16,4096]{1,0:T(8,128)(2,1)S(1)}, bf16[16,4096]{1,0:T(8,128)(2,1)S(1)}, u32[]{:S(2)}, u32[]{:S(2)}) collective-permute-start(bf16[16,4096]{1,0:T(8,128)(2,1)S(1)} %get-tuple-element.338), channel_id=1, source_target_pairs={{0,4},{1,5},{2,6},{3,7},{4,0},{5,1},{6,2},{7,3},{8,12},{9,13},{10,... | collective-permute-start | bytes 393224 | tf_op jit(solution)/shard_map/ppermute | solution.py:37
  107.8 6.6 %collective-permute-start.59 = (bf16[32,4096]{1,0:T(8,128)(2,1)S(1)}, bf16[32,4096]{1,0:T(8,128)(2,1)S(1)}, u32[]{:S(2)}, u32[]{:S(2)}) collective-permute-start(bf16[32,4096]{1,0:T(8,128)(2,1)S(1)} %constant_dynamic-update-slice_fusion.21.refs_2_), channel_id=1, source_target_pairs={{0,4},{1,5},{2,6},{3,7},{4,0},{5,1},{6,2},{7,3},{8,12},{9,13},{10,... | collective-permute-start | bytes 786440 | tf_op jit(solution)/shard_map/ppermute | solution.py:37
  108.6 6.7 %collective-permute-start.58 = (bf16[32,4096]{1,0:T(8,128)(2,1)S(1)}, bf16[32,4096]{1,0:T(8,128)(2,1)S(1)}, u32[]{:S(2)}, u32[]{:S(2)}) collective-permute-start(bf16[32,4096]{1,0:T(8,128)(2,1)S(1)} %constant_dynamic-update-slice_fusion.24.refs_2_), channel_id=1, source_target_pairs={{0,1},{1,0},{2,3},{3,2},{4,5},{5,4},{6,7},{7,6},{8,9},{9,8},{10,11... | collective-permute-start | bytes 786440 | tf_op jit(solution)/shard_map/ppermute | solution.py:37
  109.5 6.6 %collective-permute-start.57 = (bf16[32,4096]{1,0:T(8,128)(2,1)S(1)}, bf16[32,4096]{1,0:T(8,128)(2,1)S(1)}, u32[]{:S(2)}, u32[]{:S(2)}) collective-permute-start(bf16[32,4096]{1,0:T(8,128)(2,1)S(1)} %constant_dynamic-update-slice_fusion.27.refs_2_), channel_id=1, source_target_pairs={{0,2},{1,3},{2,0},{3,1},{4,6},{5,7},{6,4},{7,5},{8,10},{9,11},{10,... | collective-permute-start | bytes 786440 | tf_op jit(solution)/shard_map/ppermute | solution.py:37
  119.4 9.2 %collective-permute-start.62 = (bf16[32,4096]{1,0:T(8,128)(2,1)S(1)}, bf16[32,4096]{1,0:T(8,128)(2,1)S(1)}, u32[]{:S(2)}, u32[]{:S(2)}) collective-permute-start(bf16[32,4096]{1,0:T(8,128)(2,1)S(1)} %get-tuple-element.238), channel_id=1, source_target_pairs={{0,1},{1,0},{2,3},{3,2},{4,5},{5,4},{6,7},{7,6},{8,9},{9,8},{10,11... | collective-permute-start | bytes 786440 | tf_op jit(solution)/shard_map/ppermute | solution.py:37
  120.9 8.9 %collective-permute-start.63 = (bf16[32,4096]{1,0:T(8,128)(2,1)S(1)}, bf16[32,4096]{1,0:T(8,128)(2,1)S(1)}, u32[]{:S(2)}, u32[]{:S(2)}) collective-permute-start(bf16[32,4096]{1,0:T(8,128)(2,1)S(1)} %get-tuple-element.240), channel_id=1, source_target_pairs={{0,2},{1,3},{2,0},{3,1},{4,6},{5,7},{6,4},{7,5},{8,10},{9,11},{10,... | collective-permute-start | bytes 786440 | tf_op jit(solution)/shard_map/ppermute | solution.py:37
  122.7 8.5 %collective-permute-start.64 = (bf16[32,4096]{1,0:T(8,128)(2,1)S(1)}, bf16[32,4096]{1,0:T(8,128)(2,1)S(1)}, u32[]{:S(2)}, u32[]{:S(2)}) collective-permute-start(bf16[32,4096]{1,0:T(8,128)(2,1)S(1)} %get-tuple-element.243), channel_id=1, source_target_pairs={{0,4},{1,5},{2,6},{3,7},{4,0},{5,1},{6,2},{7,3},{8,12},{9,13},{10,... | collective-permute-start | bytes 786440 | tf_op jit(solution)/shard_map/ppermute | solution.py:37
  124.1 8.2 %collective-permute-start.61 = (bf16[32,2048]{1,0:T(8,128)(2,1)S(1)}, bf16[32,2048]{1,0:T(8,128)(2,1)S(1)}, u32[]{:S(2)}, u32[]{:S(2)}) collective-permute-start(bf16[32,2048]{1,0:T(8,128)(2,1)S(1)} %get-tuple-element.236), channel_id=1, source_target_pairs={{0,1},{1,0},{2,3},{3,2},{4,5},{5,4},{6,7},{7,6},{8,9},{9,8},{10,11... | collective-permute-start | bytes 393224 | tf_op jit(solution)/shard_map/ppermute | solution.py:37
  160.7 6.9 %collective-permute-start.89 = (bf16[32,4096]{1,0:T(8,128)(2,1)S(1)}, bf16[32,4096]{1,0:T(8,128)(2,1)S(1)}, u32[]{:S(2)}, u32[]{:S(2)}) collective-permute-start(bf16[32,4096]{1,0:T(8,128)(2,1)S(1)} %constant_dynamic-update-slice_fusion.36.refs_2_), channel_id=1, source_target_pairs={{0,4},{1,5},{2,6},{3,7},{4,0},{5,1},{6,2},{7,3},{8,12},{9,13},{10,... | collective-permute-start | bytes 786440 | tf_op jit(solution)/shard_map/ppermute | solution.py:37
  161.7 7.5 %collective-permute-start.88 = (bf16[32,4096]{1,0:T(8,128)(2,1)S(1)}, bf16[32,4096]{1,0:T(8,128)(2,1)S(1)}, u32[]{:S(2)}, u32[]{:S(2)}) collective-permute-start(bf16[32,4096]{1,0:T(8,128)(2,1)S(1)} %constant_dynamic-update-slice_fusion.39.refs_2_), channel_id=1, source_target_pairs={{0,1},{1,0},{2,3},{3,2},{4,5},{5,4},{6,7},{7,6},{8,9},{9,8},{10,11... | collective-permute-start | bytes 786440 | tf_op jit(solution)/shard_map/ppermute | solution.py:37
  162.7 8.3 %collective-permute-start.87 = (bf16[32,4096]{1,0:T(8,128)(2,1)S(1)}, bf16[32,4096]{1,0:T(8,128)(2,1)S(1)}, u32[]{:S(2)}, u32[]{:S(2)}) collective-permute-start(bf16[32,4096]{1,0:T(8,128)(2,1)S(1)} %constant_dynamic-update-slice_fusion.42.refs_2_), channel_id=1, source_target_pairs={{0,2},{1,3},{2,0},{3,1},{4,6},{5,7},{6,4},{7,5},{8,10},{9,11},{10,... | collective-permute-start | bytes 786440 | tf_op jit(solution)/shard_map/ppermute | solution.py:37
  175.5 9.2 %collective-permute-start.92 = (bf16[32,4096]{1,0:T(8,128)(2,1)S(1)}, bf16[32,4096]{1,0:T(8,128)(2,1)S(1)}, u32[]{:S(2)}, u32[]{:S(2)}) collective-permute-start(bf16[32,4096]{1,0:T(8,128)(2,1)S(1)} %get-tuple-element.279), channel_id=1, source_target_pairs={{0,1},{1,0},{2,3},{3,2},{4,5},{5,4},{6,7},{7,6},{8,9},{9,8},{10,11... | collective-permute-start | bytes 786440 | tf_op jit(solution)/shard_map/ppermute | solution.py:37
  177.0 9.1 %collective-permute-start.93 = (bf16[32,4096]{1,0:T(8,128)(2,1)S(1)}, bf16[32,4096]{1,0:T(8,128)(2,1)S(1)}, u32[]{:S(2)}, u32[]{:S(2)}) collective-permute-start(bf16[32,4096]{1,0:T(8,128)(2,1)S(1)} %get-tuple-element.281), channel_id=1, source_target_pairs={{0,2},{1,3},{2,0},{3,1},{4,6},{5,7},{6,4},{7,5},{8,10},{9,11},{10,... | collective-permute-start | bytes 786440 | tf_op jit(solution)/shard_map/ppermute | solution.py:37
  178.7 8.1 %collective-permute-start.94 = (bf16[32,4096]{1,0:T(8,128)(2,1)S(1)}, bf16[32,4096]{1,0:T(8,128)(2,1)S(1)}, u32[]{:S(2)}, u32[]{:S(2)}) collective-permute-start(bf16[32,4096]{1,0:T(8,128)(2,1)S(1)} %get-tuple-element.284), channel_id=1, source_target_pairs={{0,4},{1,5},{2,6},{3,7},{4,0},{5,1},{6,2},{7,3},{8,12},{9,13},{10,... | collective-permute-start | bytes 786440 | tf_op jit(solution)/shard_map/ppermute | solution.py:37
  179.8 8.2 %collective-permute-start.91 = (bf16[32,2048]{1,0:T(8,128)(2,1)S(1)}, bf16[32,2048]{1,0:T(8,128)(2,1)S(1)}, u32[]{:S(2)}, u32[]{:S(2)}) collective-permute-start(bf16[32,2048]{1,0:T(8,128)(2,1)S(1)} %get-tuple-element.277), channel_id=1, source_target_pairs={{0,1},{1,0},{2,3},{3,2},{4,5},{5,4},{6,7},{7,6},{8,9},{9,8},{10,11... | collective-permute-start | bytes 393224 | tf_op jit(solution)/shard_map/ppermute | solution.py:37
  194.0 6.6 %collective-permute-start.99 = (bf16[8,2048]{1,0:T(8,128)(2,1)S(1)}, bf16[8,2048]{1,0:T(8,128)(2,1)S(1)}, u32[]{:S(2)}, u32[]{:S(2)}) collective-permute-start(bf16[8,2048]{1,0:T(8,128)(2,1)S(1)} %slice.524), channel_id=1, source_target_pairs={{0,4},{1,5},{2,6},{3,7},{4,0},{5,1},{6,2},{7,3},{8,12},{9,13},{10,... | collective-permute-start | bytes 98312 | tf_op jit(solution)/shard_map/ppermute | solution.py:37
  198.3 6.5 %collective-permute-start.104 = (bf16[8,4096]{1,0:T(8,128)(2,1)S(1)}, bf16[8,4096]{1,0:T(8,128)(2,1)S(1)}, u32[]{:S(2)}, u32[]{:S(2)}) collective-permute-start(bf16[8,4096]{1,0:T(8,128)(2,1)S(1)} %fusion.low_ref), channel_id=1, source_target_pairs={{0,8},{1,9},{2,10},{3,11},{4,12},{5,13},{6,14},{7,15},{8,0},{9,1},... | collective-permute-start | bytes 196616 | tf_op jit(solution)/shard_map/ppermute | solution.py:37
  (92 other events, 461.5 us)

commit v5 on v4

--- a/solution.py
+++ b/solution.py
@@ -97,16 +97,18 @@
 
 
 VMEM = pl.BlockSpec(memory_space=pltpu.VMEM)
+HBM = pl.BlockSpec(memory_space=pltpu.HBM)
 SMEM = pl.BlockSpec(memory_space=pltpu.SMEM)
 
 
-def run(kernel, name, outs, specs, args):
+def run(kernel, name, outs, specs, args, place=VMEM, scratch=(), limit=VMEM_BYTES):
     return pl.pallas_call(
         kernel,
         out_shape=tuple(jax.ShapeDtypeStruct(shape, dtype) for shape, dtype in outs),
         in_specs=list(specs),
-        out_specs=(VMEM,) * len(outs),
-        compiler_params=pltpu.CompilerParams(vmem_limit_bytes=VMEM_BYTES),
+        out_specs=(place,) * len(outs),
+        scratch_shapes=list(scratch),
+        compiler_params=pltpu.CompilerParams(vmem_limit_bytes=limit),
         name=name,
     )(*args)
 
@@ -212,16 +214,22 @@
 
 
 def last_kernel(plan, mask_ref, own_ref, other_ref, *refs):
-    *refs, out_ref = refs
+    *refs, out_ref, held_ref, sem = refs
     scale = scale_of(plan, own_ref, other_ref)
     h = plan.height
-    for p in range(PARTS):
+    copies = []
+    for p in (PARTS - 1, *range(1, PARTS - 1), 0):
         kept_ref, came_ref, ahead_ref = refs[3 * p : 3 * p + 3]
         for here, there in plan.blocks(p):
             shrunk = shrink(plan, p, scale, kept_ref, came_ref, ahead_ref, here)
             for g in range(plan.places):
                 rows = pl.ds(pl.multiple_of((g ^ mask_ref[0]) * h, h), h)
-                out_ref[rows, there] = shrunk[h * g : h * (g + 1)]
+                held_ref[rows, there] = shrunk[h * g : h * (g + 1)]
+        a, b = plan.spans[p]
+        copies.append(pltpu.make_async_copy(held_ref.at[:, a:b], out_ref.at[:, a:b], sem.at[p]))
+        copies[-1].start()
+    for copy in copies:
+        copy.wait()
 
 
 def after(x, earlier):
@@ -307,7 +315,7 @@
         own, other = across_features(kept[:8, last:].astype(f32) + came[:8, last:].astype(f32))
         if iteration + 1 < ITERS:
             before = ()
-            for p in range(PARTS):
+            for p in (PARTS - 1, *range(1, PARTS - 1), 0):
                 weights[p], ahead[p], product = run(
                     functools.partial(update_kernel, plan, p, momentum[iteration]),
                     "update",
@@ -324,6 +332,9 @@
                 [((rows, columns), f32)],
                 [SMEM] + [VMEM] * (2 + len(args)),
                 (mask, own, other, *args),
+                HBM,
+                [pltpu.VMEM((rows, columns), f32), pltpu.SemaphoreType.DMA((PARTS,))],
+                VMEM_BYTES + 4 * rows * columns,
             )
     return result
 

time: 228 us -> 224 us (0.982)
  waiting for transfers between devices: 61.1 us -> 53.7 us
  starting transfers between devices: 132 us -> 135 us
    ppermute x120, waiting for transfers between devices: 61.1 us -> 53.7 us  [swap(): return lax.ppermute(x, axis, pairs)]
    ppermute x120, starting transfers between devices: 132 us -> 135 us  [swap(): return lax.ppermute(x, axis, pairs)]
  transfers between devices with their start and end apart: 120 -> 120, of which waited for: 55 -> 50; matrix products, arithmetic and copies ran while one was open for 1% -> 1% of each run, Pallas kernels for 6% -> 7%
where the time goes in v5:
time: 224 us
  starting transfers between devices  135 us (60%)
  waiting for transfers between devices  53.7 us (24%)
  Pallas kernels  26.4 us (12%)
  local copies, waits for them, and re-layouts  5.84 us (3%)
    ppermute x120, starting transfers between devices, swap(): return lax.ppermute(x, axis, pairs)  135 us
    ppermute x120, waiting for transfers between devices, swap(): return lax.ppermute(x, axis, pairs)  53.7 us
    pallas_call x56, Pallas kernels, run(): pl.pallas_call(kernel, out_shape=tuple((jax.ShapeDtypeStruct(shape, dtype...  26.4 us
    unnamed x32, local copies, waits for them, and re-layouts  5.36 us
  transfers between devices with their start and end apart: 120, of which 50 were waited for; matrix products, arithmetic and copies ran while one was open for 1% of the time, Pallas kernels for 7%

profile of v5, /device:TPU:0, one launch (start us, length us, event | category | flops | bytes accessed | tf_op | source)
XLA Modules:
  0.0 224.0 jit_solution(12607075411627804320)
XLA Ops:
  0.0 2.0 copy-done.2
  2.3 3.1 %copy-done = bf16[256,14336]{1,0:T(8,128)(2,1)S(1)} copy-done((bf16[256,14336]{1,0:T(8,128)(2,1)S(1)}, bf16[256,14336]{1,0:T(8,128)(2,1)}, u32[]{:S(2)}) %copy-start) | copy-done | bytes 7340056
  5.4 2.4 %first.1.own_ref = f32[64,256]{1,0:T(8,128)S(1)} custom-call(f32[64,4096]{1,0:T(8,128)S(1)} %get-tuple-element.157.refs_0_.refs_4_.refs_5_, f32[64,4096]{1,0:T(8,128)S(1)} %get-tuple-element.158.refs_1_.refs_4_.refs_5_, f32[64,4096]{1,0:T(8,128)S(1)} %get-tuple-element.159.refs_2_.refs_4_.refs_5_, f32[64,2048]{1,0:T(8,128)S(1)} %get-tuple-element.160.refs_3_.refs_4_.refs_5_, ...), custom_call_target="tpu_custom_call" | custom-call | tf_op jit(solution)/shard_map/first/pallas_call | solution.py:105
  9.6 2.9 %collective-permute-start.2 = (bf16[32,4096]{1,0:T(8,128)(2,1)S(1)}, bf16[32,4096]{1,0:T(8,128)(2,1)S(1)}, u32[]{:S(2)}, u32[]{:S(2)}) collective-permute-start(bf16[32,4096]{1,0:T(8,128)(2,1)S(1)} %get-tuple-element.164), channel_id=1, source_target_pairs={{0,1},{1,0},{2,3},{3,2},{4,5},{5,4},{6,7},{7,6},{8,9},{9,8},{10,11... | collective-permute-start | bytes 786440 | tf_op jit(solution)/shard_map/ppermute | solution.py:37
  13.0 1.6 collective-permute-start.3
  15.1 1.6 collective-permute-start.4
  17.7 1.6 collective-permute-done.2
  19.3 2.5 %collective-permute-start.6 = (bf16[16,4096]{1,0:T(8,128)(2,1)S(1)}, bf16[16,4096]{1,0:T(8,128)(2,1)S(1)}, u32[]{:S(2)}, u32[]{:S(2)}) collective-permute-start(bf16[16,4096]{1,0:T(8,128)(2,1)S(1)} %slice.507), channel_id=1, source_target_pairs={{0,2},{1,3},{2,0},{3,1},{4,6},{5,7},{6,4},{7,5},{8,10},{9,11},{10,... | collective-permute-start | bytes 393224 | tf_op jit(solution)/shard_map/ppermute | solution.py:37
  22.0 1.6 collective-permute-start.7
  25.9 1.7 collective-permute-start.10
  29.4 1.6 collective-permute-start.12
  31.5 2.7 %collective-permute-start.16 = (bf16[8,4096]{1,0:T(8,128)(2,1)S(1)}, bf16[8,4096]{1,0:T(8,128)(2,1)S(1)}, u32[]{:S(2)}, u32[]{:S(2)}) collective-permute-start(bf16[8,4096]{1,0:T(8,128)(2,1)S(1)} %fusion.11.low_ref), channel_id=1, source_target_pairs={{0,8},{1,9},{2,10},{3,11},{4,12},{5,13},{6,14},{7,15},{8,0},{9,1},... | collective-permute-start | bytes 196616 | tf_op jit(solution)/shard_map/ppermute | solution.py:37
  34.8 2.5 %collective-permute-start.14 = (bf16[8,4096]{1,0:T(8,128)(2,1)S(1)}, bf16[8,4096]{1,0:T(8,128)(2,1)S(1)}, u32[]{:S(2)}, u32[]{:S(2)}) collective-permute-start(bf16[8,4096]{1,0:T(8,128)(2,1)S(1)} %fusion.9.low_ref), channel_id=1, source_target_pairs={{0,8},{1,9},{2,10},{3,11},{4,12},{5,13},{6,14},{7,15},{8,0},{9,1},... | collective-permute-start | bytes 196616 | tf_op jit(solution)/shard_map/ppermute | solution.py:37
  40.1 2.2 collective-permute-start.19
  44.8 1.7 collective-permute-start.23
  50.4 2.8 %collective-permute-done.24 = bf16[16,4096]{1,0:T(8,128)(2,1)S(1)} collective-permute-done((bf16[16,4096]{1,0:T(8,128)(2,1)S(1)}, bf16[16,4096]{1,0:T(8,128)(2,1)S(1)}, u32[]{:S(2)}, u32[]{:S(2)}) %collective-permute-start.24) | collective-permute-done | bytes 131104 | tf_op jit(solution)/shard_map/ppermute | solution.py:37
  71.2 3.4 %collective-permute-done.32 = bf16[32,4096]{1,0:T(8,128)(2,1)S(1)} collective-permute-done((bf16[32,4096]{1,0:T(8,128)(2,1)S(1)}, bf16[32,4096]{1,0:T(8,128)(2,1)S(1)}, u32[]{:S(2)}, u32[]{:S(2)}) %collective-permute-start.32) | collective-permute-done | bytes 262176 | tf_op jit(solution)/shard_map/ppermute | solution.py:37
  85.2 2.1 collective-permute-start.46
  88.3 2.1 collective-permute-start.44
  101.9 2.1 collective-permute-done.53
  123.6 3.6 %collective-permute-done.62 = bf16[32,4096]{1,0:T(8,128)(2,1)S(1)} collective-permute-done((bf16[32,4096]{1,0:T(8,128)(2,1)S(1)}, bf16[32,4096]{1,0:T(8,128)(2,1)S(1)}, u32[]{:S(2)}, u32[]{:S(2)}) %collective-permute-start.62) | collective-permute-done | bytes 262176 | tf_op jit(solution)/shard_map/ppermute | solution.py:37
  137.7 1.7 collective-permute-start.76
  140.8 1.7 collective-permute-start.74
  154.1 2.8 %collective-permute-done.83 = bf16[16,4096]{1,0:T(8,128)(2,1)S(1)} collective-permute-done((bf16[16,4096]{1,0:T(8,128)(2,1)S(1)}, bf16[16,4096]{1,0:T(8,128)(2,1)S(1)}, u32[]{:S(2)}, u32[]{:S(2)}) %collective-permute-start.83) | collective-permute-done | bytes 131104 | tf_op jit(solution)/shard_map/ppermute | solution.py:37
  165.6 1.7 update.21
  167.3 1.7 update.22
  168.9 1.7 update.23
  177.8 3.7 %collective-permute-done.92 = bf16[32,4096]{1,0:T(8,128)(2,1)S(1)} collective-permute-done((bf16[32,4096]{1,0:T(8,128)(2,1)S(1)}, bf16[32,4096]{1,0:T(8,128)(2,1)S(1)}, u32[]{:S(2)}, u32[]{:S(2)}) %collective-permute-start.92) | collective-permute-done | bytes 262176 | tf_op jit(solution)/shard_map/ppermute | solution.py:37
  193.4 1.6 collective-permute-start.105
  196.5 1.6 collective-permute-start.103
  208.1 2.7 %collective-permute-done.113 = bf16[16,4096]{1,0:T(8,128)(2,1)S(1)} collective-permute-done((bf16[16,4096]{1,0:T(8,128)(2,1)S(1)}, bf16[16,4096]{1,0:T(8,128)(2,1)S(1)}, u32[]{:S(2)}, u32[]{:S(2)}) %collective-permute-start.113) | collective-permute-done | bytes 131104 | tf_op jit(solution)/shard_map/ppermute | solution.py:37
  221.7 2.2 last.1
  (392 shorter events, 152.1 us)
Async XLA Ops:
  9.6 9.6 %collective-permute-start.2 = (bf16[32,4096]{1,0:T(8,128)(2,1)S(1)}, bf16[32,4096]{1,0:T(8,128)(2,1)S(1)}, u32[]{:S(2)}, u32[]{:S(2)}) collective-permute-start(bf16[32,4096]{1,0:T(8,128)(2,1)S(1)} %get-tuple-element.164), channel_id=1, source_target_pairs={{0,1},{1,0},{2,3},{3,2},{4,5},{5,4},{6,7},{7,6},{8,9},{9,8},{10,11... | collective-permute-start | bytes 786440 | tf_op jit(solution)/shard_map/ppermute | solution.py:37
  13.0 8.8 %collective-permute-start.3 = (bf16[32,4096]{1,0:T(8,128)(2,1)S(1)}, bf16[32,4096]{1,0:T(8,128)(2,1)S(1)}, u32[]{:S(2)}, u32[]{:S(2)}) collective-permute-start(bf16[32,4096]{1,0:T(8,128)(2,1)S(1)} %get-tuple-element.166), channel_id=1, source_target_pairs={{0,2},{1,3},{2,0},{3,1},{4,6},{5,7},{6,4},{7,5},{8,10},{9,11},{10,... | collective-permute-start | bytes 786440 | tf_op jit(solution)/shard_map/ppermute | solution.py:37
  15.1 8.5 %collective-permute-start.4 = (bf16[32,4096]{1,0:T(8,128)(2,1)S(1)}, bf16[32,4096]{1,0:T(8,128)(2,1)S(1)}, u32[]{:S(2)}, u32[]{:S(2)}) collective-permute-start(bf16[32,4096]{1,0:T(8,128)(2,1)S(1)} %get-tuple-element.169), channel_id=1, source_target_pairs={{0,4},{1,5},{2,6},{3,7},{4,0},{5,1},{6,2},{7,3},{8,12},{9,13},{10,... | collective-permute-start | bytes 786440 | tf_op jit(solution)/shard_map/ppermute | solution.py:37
  17.1 8.2 %collective-permute-start.1 = (bf16[32,2048]{1,0:T(8,128)(2,1)S(1)}, bf16[32,2048]{1,0:T(8,128)(2,1)S(1)}, u32[]{:S(2)}, u32[]{:S(2)}) collective-permute-start(bf16[32,2048]{1,0:T(8,128)(2,1)S(1)} %get-tuple-element.162), channel_id=1, source_target_pairs={{0,1},{1,0},{2,3},{3,2},{4,5},{5,4},{6,7},{7,6},{8,9},{9,8},{10,11... | collective-permute-start | bytes 393224 | tf_op jit(solution)/shard_map/ppermute | solution.py:37
  19.3 6.5 %collective-permute-start.6 = (bf16[16,4096]{1,0:T(8,128)(2,1)S(1)}, bf16[16,4096]{1,0:T(8,128)(2,1)S(1)}, u32[]{:S(2)}, u32[]{:S(2)}) collective-permute-start(bf16[16,4096]{1,0:T(8,128)(2,1)S(1)} %slice.507), channel_id=1, source_target_pairs={{0,2},{1,3},{2,0},{3,1},{4,6},{5,7},{6,4},{7,5},{8,10},{9,11},{10,... | collective-permute-start | bytes 393224 | tf_op jit(solution)/shard_map/ppermute | solution.py:37
  27.8 6.4 %collective-permute-start.11 = (bf16[8,4096]{1,0:T(8,128)(2,1)S(1)}, bf16[8,4096]{1,0:T(8,128)(2,1)S(1)}, u32[]{:S(2)}, u32[]{:S(2)}) collective-permute-start(bf16[8,4096]{1,0:T(8,128)(2,1)S(1)} %slice.521), channel_id=1, source_target_pairs={{0,1},{1,0},{2,3},{3,2},{4,5},{5,4},{6,7},{7,6},{8,9},{9,8},{10,11... | collective-permute-start | bytes 196616 | tf_op jit(solution)/shard_map/ppermute | solution.py:37
  31.5 7.2 %collective-permute-start.16 = (bf16[8,4096]{1,0:T(8,128)(2,1)S(1)}, bf16[8,4096]{1,0:T(8,128)(2,1)S(1)}, u32[]{:S(2)}, u32[]{:S(2)}) collective-permute-start(bf16[8,4096]{1,0:T(8,128)(2,1)S(1)} %fusion.11.low_ref), channel_id=1, source_target_pairs={{0,8},{1,9},{2,10},{3,11},{4,12},{5,13},{6,14},{7,15},{8,0},{9,1},... | collective-permute-start | bytes 196616 | tf_op jit(solution)/shard_map/ppermute | solution.py:37
  34.8 7.6 %collective-permute-start.14 = (bf16[8,4096]{1,0:T(8,128)(2,1)S(1)}, bf16[8,4096]{1,0:T(8,128)(2,1)S(1)}, u32[]{:S(2)}, u32[]{:S(2)}) collective-permute-start(bf16[8,4096]{1,0:T(8,128)(2,1)S(1)} %fusion.9.low_ref), channel_id=1, source_target_pairs={{0,8},{1,9},{2,10},{3,11},{4,12},{5,13},{6,14},{7,15},{8,0},{9,1},... | collective-permute-start | bytes 196616 | tf_op jit(solution)/shard_map/ppermute | solution.py:37
  46.8 6.4 %collective-permute-start.24 = (bf16[16,4096]{1,0:T(8,128)(2,1)S(1)}, bf16[16,4096]{1,0:T(8,128)(2,1)S(1)}, u32[]{:S(2)}, u32[]{:S(2)}) collective-permute-start(bf16[16,4096]{1,0:T(8,128)(2,1)S(1)} %get-tuple-element.346), channel_id=1, source_target_pairs={{0,1},{1,0},{2,3},{3,2},{4,5},{5,4},{6,7},{7,6},{8,9},{9,8},{10,11... | collective-permute-start | bytes 393224 | tf_op jit(solution)/shard_map/ppermute | solution.py:37
  54.1 6.4 %collective-permute-start.29 = (bf16[32,4096]{1,0:T(8,128)(2,1)S(1)}, bf16[32,4096]{1,0:T(8,128)(2,1)S(1)}, u32[]{:S(2)}, u32[]{:S(2)}) collective-permute-start(bf16[32,4096]{1,0:T(8,128)(2,1)S(1)} %constant_dynamic-update-slice_fusion.9.refs_2_), channel_id=1, source_target_pairs={{0,1},{1,0},{2,3},{3,2},{4,5},{5,4},{6,7},{7,6},{8,9},{9,8},{10,11... | collective-permute-start | bytes 786440 | tf_op jit(solution)/shard_map/ppermute | solution.py:37
  55.0 6.4 %collective-permute-start.28 = (bf16[32,4096]{1,0:T(8,128)(2,1)S(1)}, bf16[32,4096]{1,0:T(8,128)(2,1)S(1)}, u32[]{:S(2)}, u32[]{:S(2)}) collective-permute-start(bf16[32,4096]{1,0:T(8,128)(2,1)S(1)} %constant_dynamic-update-slice_fusion.12.refs_2_), channel_id=1, source_target_pairs={{0,2},{1,3},{2,0},{3,1},{4,6},{5,7},{6,4},{7,5},{8,10},{9,11},{10,... | collective-permute-start | bytes 786440 | tf_op jit(solution)/shard_map/ppermute | solution.py:37
  56.3 6.4 %collective-permute-start.27 = (bf16[32,4096]{1,0:T(8,128)(2,1)S(1)}, bf16[32,4096]{1,0:T(8,128)(2,1)S(1)}, u32[]{:S(2)}, u32[]{:S(2)}) collective-permute-start(bf16[32,4096]{1,0:T(8,128)(2,1)S(1)} %constant_dynamic-update-slice_fusion.6.refs_2_), channel_id=1, source_target_pairs={{0,4},{1,5},{2,6},{3,7},{4,0},{5,1},{6,2},{7,3},{8,12},{9,13},{10,... | collective-permute-start | bytes 786440 | tf_op jit(solution)/shard_map/ppermute | solution.py:37
  65.4 9.2 %collective-permute-start.32 = (bf16[32,4096]{1,0:T(8,128)(2,1)S(1)}, bf16[32,4096]{1,0:T(8,128)(2,1)S(1)}, u32[]{:S(2)}, u32[]{:S(2)}) collective-permute-start(bf16[32,4096]{1,0:T(8,128)(2,1)S(1)} %get-tuple-element.197), channel_id=1, source_target_pairs={{0,1},{1,0},{2,3},{3,2},{4,5},{5,4},{6,7},{7,6},{8,9},{9,8},{10,11... | collective-permute-start | bytes 786440 | tf_op jit(solution)/shard_map/ppermute | solution.py:37
  66.6 9.0 %collective-permute-start.33 = (bf16[32,4096]{1,0:T(8,128)(2,1)S(1)}, bf16[32,4096]{1,0:T(8,128)(2,1)S(1)}, u32[]{:S(2)}, u32[]{:S(2)}) collective-permute-start(bf16[32,4096]{1,0:T(8,128)(2,1)S(1)} %get-tuple-element.199), channel_id=1, source_target_pairs={{0,2},{1,3},{2,0},{3,1},{4,6},{5,7},{6,4},{7,5},{8,10},{9,11},{10,... | collective-permute-start | bytes 786440 | tf_op jit(solution)/shard_map/ppermute | solution.py:37
  68.3 8.8 %collective-permute-start.34 = (bf16[32,4096]{1,0:T(8,128)(2,1)S(1)}, bf16[32,4096]{1,0:T(8,128)(2,1)S(1)}, u32[]{:S(2)}, u32[]{:S(2)}) collective-permute-start(bf16[32,4096]{1,0:T(8,128)(2,1)S(1)} %get-tuple-element.202), channel_id=1, source_target_pairs={{0,4},{1,5},{2,6},{3,7},{4,0},{5,1},{6,2},{7,3},{8,12},{9,13},{10,... | collective-permute-start | bytes 786440 | tf_op jit(solution)/shard_map/ppermute | solution.py:37
  70.0 8.2 %collective-permute-start.31 = (bf16[32,2048]{1,0:T(8,128)(2,1)S(1)}, bf16[32,2048]{1,0:T(8,128)(2,1)S(1)}, u32[]{:S(2)}, u32[]{:S(2)}) collective-permute-start(bf16[32,2048]{1,0:T(8,128)(2,1)S(1)} %get-tuple-element.195), channel_id=1, source_target_pairs={{0,1},{1,0},{2,3},{3,2},{4,5},{5,4},{6,7},{7,6},{8,9},{9,8},{10,11... | collective-permute-start | bytes 393224 | tf_op jit(solution)/shard_map/ppermute | solution.py:37
  85.2 6.4 %collective-permute-start.46 = (bf16[8,4096]{1,0:T(8,128)(2,1)S(1)}, bf16[8,4096]{1,0:T(8,128)(2,1)S(1)}, u32[]{:S(2)}, u32[]{:S(2)}) collective-permute-start(bf16[8,4096]{1,0:T(8,128)(2,1)S(1)} %fusion.8.low_ref), channel_id=1, source_target_pairs={{0,8},{1,9},{2,10},{3,11},{4,12},{5,13},{6,14},{7,15},{8,0},{9,1},... | collective-permute-start | bytes 196616 | tf_op jit(solution)/shard_map/ppermute | solution.py:37
  106.7 6.4 %collective-permute-start.59 = (bf16[32,4096]{1,0:T(8,128)(2,1)S(1)}, bf16[32,4096]{1,0:T(8,128)(2,1)S(1)}, u32[]{:S(2)}, u32[]{:S(2)}) collective-permute-start(bf16[32,4096]{1,0:T(8,128)(2,1)S(1)} %constant_dynamic-update-slice_fusion.24.refs_2_), channel_id=1, source_target_pairs={{0,1},{1,0},{2,3},{3,2},{4,5},{5,4},{6,7},{7,6},{8,9},{9,8},{10,11... | collective-permute-start | bytes 786440 | tf_op jit(solution)/shard_map/ppermute | solution.py:37
  107.7 6.4 %collective-permute-start.58 = (bf16[32,4096]{1,0:T(8,128)(2,1)S(1)}, bf16[32,4096]{1,0:T(8,128)(2,1)S(1)}, u32[]{:S(2)}, u32[]{:S(2)}) collective-permute-start(bf16[32,4096]{1,0:T(8,128)(2,1)S(1)} %constant_dynamic-update-slice_fusion.27.refs_2_), channel_id=1, source_target_pairs={{0,2},{1,3},{2,0},{3,1},{4,6},{5,7},{6,4},{7,5},{8,10},{9,11},{10,... | collective-permute-start | bytes 786440 | tf_op jit(solution)/shard_map/ppermute | solution.py:37
  118.0 9.2 %collective-permute-start.62 = (bf16[32,4096]{1,0:T(8,128)(2,1)S(1)}, bf16[32,4096]{1,0:T(8,128)(2,1)S(1)}, u32[]{:S(2)}, u32[]{:S(2)}) collective-permute-start(bf16[32,4096]{1,0:T(8,128)(2,1)S(1)} %get-tuple-element.238), channel_id=1, source_target_pairs={{0,1},{1,0},{2,3},{3,2},{4,5},{5,4},{6,7},{7,6},{8,9},{9,8},{10,11... | collective-permute-start | bytes 786440 | tf_op jit(solution)/shard_map/ppermute | solution.py:37
  119.5 8.7 %collective-permute-start.63 = (bf16[32,4096]{1,0:T(8,128)(2,1)S(1)}, bf16[32,4096]{1,0:T(8,128)(2,1)S(1)}, u32[]{:S(2)}, u32[]{:S(2)}) collective-permute-start(bf16[32,4096]{1,0:T(8,128)(2,1)S(1)} %get-tuple-element.240), channel_id=1, source_target_pairs={{0,2},{1,3},{2,0},{3,1},{4,6},{5,7},{6,4},{7,5},{8,10},{9,11},{10,... | collective-permute-start | bytes 786440 | tf_op jit(solution)/shard_map/ppermute | solution.py:37
  120.9 8.6 %collective-permute-start.64 = (bf16[32,4096]{1,0:T(8,128)(2,1)S(1)}, bf16[32,4096]{1,0:T(8,128)(2,1)S(1)}, u32[]{:S(2)}, u32[]{:S(2)}) collective-permute-start(bf16[32,4096]{1,0:T(8,128)(2,1)S(1)} %get-tuple-element.243), channel_id=1, source_target_pairs={{0,4},{1,5},{2,6},{3,7},{4,0},{5,1},{6,2},{7,3},{8,12},{9,13},{10,... | collective-permute-start | bytes 786440 | tf_op jit(solution)/shard_map/ppermute | solution.py:37
  122.4 8.2 %collective-permute-start.61 = (bf16[32,2048]{1,0:T(8,128)(2,1)S(1)}, bf16[32,2048]{1,0:T(8,128)(2,1)S(1)}, u32[]{:S(2)}, u32[]{:S(2)}) collective-permute-start(bf16[32,2048]{1,0:T(8,128)(2,1)S(1)} %get-tuple-element.236), channel_id=1, source_target_pairs={{0,1},{1,0},{2,3},{3,2},{4,5},{5,4},{6,7},{7,6},{8,9},{9,8},{10,11... | collective-permute-start | bytes 393224 | tf_op jit(solution)/shard_map/ppermute | solution.py:37
  150.4 6.4 %collective-permute-start.83 = (bf16[16,4096]{1,0:T(8,128)(2,1)S(1)}, bf16[16,4096]{1,0:T(8,128)(2,1)S(1)}, u32[]{:S(2)}, u32[]{:S(2)}) collective-permute-start(bf16[16,4096]{1,0:T(8,128)(2,1)S(1)} %get-tuple-element.326), channel_id=1, source_target_pairs={{0,4},{1,5},{2,6},{3,7},{4,0},{5,1},{6,2},{7,3},{8,12},{9,13},{10,... | collective-permute-start | bytes 393224 | tf_op jit(solution)/shard_map/ppermute | solution.py:37
  151.5 6.4 %collective-permute-start.84 = (bf16[16,4096]{1,0:T(8,128)(2,1)S(1)}, bf16[16,4096]{1,0:T(8,128)(2,1)S(1)}, u32[]{:S(2)}, u32[]{:S(2)}) collective-permute-start(bf16[16,4096]{1,0:T(8,128)(2,1)S(1)} %get-tuple-element.322), channel_id=1, source_target_pairs={{0,1},{1,0},{2,3},{3,2},{4,5},{5,4},{6,7},{7,6},{8,9},{9,8},{10,11... | collective-permute-start | bytes 393224 | tf_op jit(solution)/shard_map/ppermute | solution.py:37
  159.1 6.5 %collective-permute-start.89 = (bf16[32,4096]{1,0:T(8,128)(2,1)S(1)}, bf16[32,4096]{1,0:T(8,128)(2,1)S(1)}, u32[]{:S(2)}, u32[]{:S(2)}) collective-permute-start(bf16[32,4096]{1,0:T(8,128)(2,1)S(1)} %constant_dynamic-update-slice_fusion.39.refs_2_), channel_id=1, source_target_pairs={{0,1},{1,0},{2,3},{3,2},{4,5},{5,4},{6,7},{7,6},{8,9},{9,8},{10,11... | collective-permute-start | bytes 786440 | tf_op jit(solution)/shard_map/ppermute | solution.py:37
  160.0 7.2 %collective-permute-start.88 = (bf16[32,4096]{1,0:T(8,128)(2,1)S(1)}, bf16[32,4096]{1,0:T(8,128)(2,1)S(1)}, u32[]{:S(2)}, u32[]{:S(2)}) collective-permute-start(bf16[32,4096]{1,0:T(8,128)(2,1)S(1)} %constant_dynamic-update-slice_fusion.42.refs_2_), channel_id=1, source_target_pairs={{0,2},{1,3},{2,0},{3,1},{4,6},{5,7},{6,4},{7,5},{8,10},{9,11},{10,... | collective-permute-start | bytes 786440 | tf_op jit(solution)/shard_map/ppermute | solution.py:37
  160.8 8.2 %collective-permute-start.87 = (bf16[32,4096]{1,0:T(8,128)(2,1)S(1)}, bf16[32,4096]{1,0:T(8,128)(2,1)S(1)}, u32[]{:S(2)}, u32[]{:S(2)}) collective-permute-start(bf16[32,4096]{1,0:T(8,128)(2,1)S(1)} %constant_dynamic-update-slice_fusion.36.refs_2_), channel_id=1, source_target_pairs={{0,4},{1,5},{2,6},{3,7},{4,0},{5,1},{6,2},{7,3},{8,12},{9,13},{10,... | collective-permute-start | bytes 786440 | tf_op jit(solution)/shard_map/ppermute | solution.py:37
  172.4 9.2 %collective-permute-start.92 = (bf16[32,4096]{1,0:T(8,128)(2,1)S(1)}, bf16[32,4096]{1,0:T(8,128)(2,1)S(1)}, u32[]{:S(2)}, u32[]{:S(2)}) collective-permute-start(bf16[32,4096]{1,0:T(8,128)(2,1)S(1)} %get-tuple-element.279), channel_id=1, source_target_pairs={{0,1},{1,0},{2,3},{3,2},{4,5},{5,4},{6,7},{7,6},{8,9},{9,8},{10,11... | collective-permute-start | bytes 786440 | tf_op jit(solution)/shard_map/ppermute | solution.py:37
  173.9 8.8 %collective-permute-start.93 = (bf16[32,4096]{1,0:T(8,128)(2,1)S(1)}, bf16[32,4096]{1,0:T(8,128)(2,1)S(1)}, u32[]{:S(2)}, u32[]{:S(2)}) collective-permute-start(bf16[32,4096]{1,0:T(8,128)(2,1)S(1)} %get-tuple-element.281), channel_id=1, source_target_pairs={{0,2},{1,3},{2,0},{3,1},{4,6},{5,7},{6,4},{7,5},{8,10},{9,11},{10,... | collective-permute-start | bytes 786440 | tf_op jit(solution)/shard_map/ppermute | solution.py:37
  175.3 8.5 %collective-permute-start.94 = (bf16[32,4096]{1,0:T(8,128)(2,1)S(1)}, bf16[32,4096]{1,0:T(8,128)(2,1)S(1)}, u32[]{:S(2)}, u32[]{:S(2)}) collective-permute-start(bf16[32,4096]{1,0:T(8,128)(2,1)S(1)} %get-tuple-element.284), channel_id=1, source_target_pairs={{0,4},{1,5},{2,6},{3,7},{4,0},{5,1},{6,2},{7,3},{8,12},{9,13},{10,... | collective-permute-start | bytes 786440 | tf_op jit(solution)/shard_map/ppermute | solution.py:37
  176.7 8.2 %collective-permute-start.91 = (bf16[32,2048]{1,0:T(8,128)(2,1)S(1)}, bf16[32,2048]{1,0:T(8,128)(2,1)S(1)}, u32[]{:S(2)}, u32[]{:S(2)}) collective-permute-start(bf16[32,2048]{1,0:T(8,128)(2,1)S(1)} %get-tuple-element.277), channel_id=1, source_target_pairs={{0,1},{1,0},{2,3},{3,2},{4,5},{5,4},{6,7},{7,6},{8,9},{9,8},{10,11... | collective-permute-start | bytes 393224 | tf_op jit(solution)/shard_map/ppermute | solution.py:37
  (92 other events, 458.5 us)

commit v6 on v5

--- a/solution.py
+++ b/solution.py
@@ -251,7 +251,7 @@
     for bit in range(plan.rows_bits, bits_of("tok")):
         if bit > plan.rows_bits:
             sends = [(a.astype(f32) + b.astype(f32)).astype(bf16) for a, b in zip(sends, came)]
-        came = [swap(x, "tok", bit) for x in sends]
+        came = [swap(after(x, sends[:p]) if p else x, "tok", bit) for p, x in enumerate(sends)]
     square = ()
     for p, width in enumerate(plan.widths):
         last = p + 1 == PARTS

time: 224 us -> 224 us (level)
  no operation moved by 1% of the time
where the time goes in v6:
time: 224 us
  starting transfers between devices  135 us (60%)
  waiting for transfers between devices  53.7 us (24%)
  Pallas kernels  26.4 us (12%)
  local copies, waits for them, and re-layouts  5.84 us (3%)
    ppermute x120, starting transfers between devices, swap(): return lax.ppermute(x, axis, pairs)  135 us
    ppermute x120, waiting for transfers between devices, swap(): return lax.ppermute(x, axis, pairs)  53.7 us
    pallas_call x56, Pallas kernels, run(): pl.pallas_call(kernel, out_shape=tuple((jax.ShapeDtypeStruct(shape, dtype...  26.4 us
    unnamed x32, local copies, waits for them, and re-layouts  5.36 us
  transfers between devices with their start and end apart: 120, of which 50 were waited for; matrix products, arithmetic and copies ran while one was open for 1% of the time, Pallas kernels for 7%

profile of v6, /device:TPU:0, one launch (start us, length us, event | category | flops | bytes accessed | tf_op | source)
XLA Modules:
  0.0 224.0 jit_solution(12607075411627804320)
XLA Ops:
  0.0 2.0 copy-done.2
  2.3 3.1 %copy-done = bf16[256,14336]{1,0:T(8,128)(2,1)S(1)} copy-done((bf16[256,14336]{1,0:T(8,128)(2,1)S(1)}, bf16[256,14336]{1,0:T(8,128)(2,1)}, u32[]{:S(2)}) %copy-start) | copy-done | bytes 7340056
  5.4 2.4 %first.1.own_ref = f32[64,256]{1,0:T(8,128)S(1)} custom-call(f32[64,4096]{1,0:T(8,128)S(1)} %get-tuple-element.169.refs_0_.refs_4_.refs_5_, f32[64,4096]{1,0:T(8,128)S(1)} %get-tuple-element.170.refs_1_.refs_4_.refs_5_, f32[64,4096]{1,0:T(8,128)S(1)} %get-tuple-element.171.refs_2_.refs_4_.refs_5_, f32[64,2048]{1,0:T(8,128)S(1)} %get-tuple-element.172.refs_3_.refs_4_.refs_5_, ...), custom_call_target="tpu_custom_call" | custom-call | tf_op jit(solution)/shard_map/first/pallas_call | solution.py:105
  9.6 2.9 %collective-permute-start.2 = (bf16[32,4096]{1,0:T(8,128)(2,1)S(1)}, bf16[32,4096]{1,0:T(8,128)(2,1)S(1)}, u32[]{:S(2)}, u32[]{:S(2)}) collective-permute-start(bf16[32,4096]{1,0:T(8,128)(2,1)S(1)} %get-tuple-element.176), channel_id=1, source_target_pairs={{0,1},{1,0},{2,3},{3,2},{4,5},{5,4},{6,7},{7,6},{8,9},{9,8},{10,11... | collective-permute-start | bytes 786440 | tf_op jit(solution)/shard_map/ppermute | solution.py:37
  13.0 1.6 collective-permute-start.3
  15.1 1.6 collective-permute-start.4
  17.7 1.6 collective-permute-done.2
  19.3 2.5 %collective-permute-start.6 = (bf16[16,4096]{1,0:T(8,128)(2,1)S(1)}, bf16[16,4096]{1,0:T(8,128)(2,1)S(1)}, u32[]{:S(2)}, u32[]{:S(2)}) collective-permute-start(bf16[16,4096]{1,0:T(8,128)(2,1)S(1)} %slice.507), channel_id=1, source_target_pairs={{0,2},{1,3},{2,0},{3,1},{4,6},{5,7},{6,4},{7,5},{8,10},{9,11},{10,... | collective-permute-start | bytes 393224 | tf_op jit(solution)/shard_map/ppermute | solution.py:37
  22.0 1.6 collective-permute-start.7
  25.9 1.7 collective-permute-start.10
  29.4 1.6 collective-permute-start.12
  31.5 2.7 %collective-permute-start.16 = (bf16[8,4096]{1,0:T(8,128)(2,1)S(1)}, bf16[8,4096]{1,0:T(8,128)(2,1)S(1)}, u32[]{:S(2)}, u32[]{:S(2)}) collective-permute-start(bf16[8,4096]{1,0:T(8,128)(2,1)S(1)} %fusion.11.low_ref), channel_id=1, source_target_pairs={{0,8},{1,9},{2,10},{3,11},{4,12},{5,13},{6,14},{7,15},{8,0},{9,1},... | collective-permute-start | bytes 196616 | tf_op jit(solution)/shard_map/ppermute | solution.py:37
  34.8 2.5 %collective-permute-start.14 = (bf16[8,4096]{1,0:T(8,128)(2,1)S(1)}, bf16[8,4096]{1,0:T(8,128)(2,1)S(1)}, u32[]{:S(2)}, u32[]{:S(2)}) collective-permute-start(bf16[8,4096]{1,0:T(8,128)(2,1)S(1)} %fusion.9.low_ref), channel_id=1, source_target_pairs={{0,8},{1,9},{2,10},{3,11},{4,12},{5,13},{6,14},{7,15},{8,0},{9,1},... | collective-permute-start | bytes 196616 | tf_op jit(solution)/shard_map/ppermute | solution.py:37
  40.1 2.2 collective-permute-start.19
  44.8 1.7 collective-permute-start.23
  50.4 2.8 %collective-permute-done.24 = bf16[16,4096]{1,0:T(8,128)(2,1)S(1)} collective-permute-done((bf16[16,4096]{1,0:T(8,128)(2,1)S(1)}, bf16[16,4096]{1,0:T(8,128)(2,1)S(1)}, u32[]{:S(2)}, u32[]{:S(2)}) %collective-permute-start.24) | collective-permute-done | bytes 131104 | tf_op jit(solution)/shard_map/ppermute | solution.py:37
  71.2 3.4 %collective-permute-done.32 = bf16[32,4096]{1,0:T(8,128)(2,1)S(1)} collective-permute-done((bf16[32,4096]{1,0:T(8,128)(2,1)S(1)}, bf16[32,4096]{1,0:T(8,128)(2,1)S(1)}, u32[]{:S(2)}, u32[]{:S(2)}) %collective-permute-start.32) | collective-permute-done | bytes 262176 | tf_op jit(solution)/shard_map/ppermute | solution.py:37
  85.2 2.1 collective-permute-start.46
  88.3 2.1 collective-permute-start.44
  101.9 2.1 collective-permute-done.53
  123.6 3.6 %collective-permute-done.62 = bf16[32,4096]{1,0:T(8,128)(2,1)S(1)} collective-permute-done((bf16[32,4096]{1,0:T(8,128)(2,1)S(1)}, bf16[32,4096]{1,0:T(8,128)(2,1)S(1)}, u32[]{:S(2)}, u32[]{:S(2)}) %collective-permute-start.62) | collective-permute-done | bytes 262176 | tf_op jit(solution)/shard_map/ppermute | solution.py:37
  137.7 1.7 collective-permute-start.76
  140.8 1.7 collective-permute-start.74
  154.1 2.8 %collective-permute-done.83 = bf16[16,4096]{1,0:T(8,128)(2,1)S(1)} collective-permute-done((bf16[16,4096]{1,0:T(8,128)(2,1)S(1)}, bf16[16,4096]{1,0:T(8,128)(2,1)S(1)}, u32[]{:S(2)}, u32[]{:S(2)}) %collective-permute-start.83) | collective-permute-done | bytes 131104 | tf_op jit(solution)/shard_map/ppermute | solution.py:37
  165.6 1.7 update.21
  167.3 1.7 update.22
  168.9 1.7 update.23
  177.8 3.7 %collective-permute-done.92 = bf16[32,4096]{1,0:T(8,128)(2,1)S(1)} collective-permute-done((bf16[32,4096]{1,0:T(8,128)(2,1)S(1)}, bf16[32,4096]{1,0:T(8,128)(2,1)S(1)}, u32[]{:S(2)}, u32[]{:S(2)}) %collective-permute-start.92) | collective-permute-done | bytes 262176 | tf_op jit(solution)/shard_map/ppermute | solution.py:37
  193.4 1.6 collective-permute-start.105
  196.5 1.6 collective-permute-start.103
  208.1 2.7 %collective-permute-done.113 = bf16[16,4096]{1,0:T(8,128)(2,1)S(1)} collective-permute-done((bf16[16,4096]{1,0:T(8,128)(2,1)S(1)}, bf16[16,4096]{1,0:T(8,128)(2,1)S(1)}, u32[]{:S(2)}, u32[]{:S(2)}) %collective-permute-start.113) | collective-permute-done | bytes 131104 | tf_op jit(solution)/shard_map/ppermute | solution.py:37
  221.7 2.2 last.1
  (392 shorter events, 152.1 us)
Async XLA Ops:
  9.6 9.6 %collective-permute-start.2 = (bf16[32,4096]{1,0:T(8,128)(2,1)S(1)}, bf16[32,4096]{1,0:T(8,128)(2,1)S(1)}, u32[]{:S(2)}, u32[]{:S(2)}) collective-permute-start(bf16[32,4096]{1,0:T(8,128)(2,1)S(1)} %get-tuple-element.176), channel_id=1, source_target_pairs={{0,1},{1,0},{2,3},{3,2},{4,5},{5,4},{6,7},{7,6},{8,9},{9,8},{10,11... | collective-permute-start | bytes 786440 | tf_op jit(solution)/shard_map/ppermute | solution.py:37
  13.0 8.8 %collective-permute-start.3 = (bf16[32,4096]{1,0:T(8,128)(2,1)S(1)}, bf16[32,4096]{1,0:T(8,128)(2,1)S(1)}, u32[]{:S(2)}, u32[]{:S(2)}) collective-permute-start(bf16[32,4096]{1,0:T(8,128)(2,1)S(1)} %get-tuple-element.178), channel_id=1, source_target_pairs={{0,2},{1,3},{2,0},{3,1},{4,6},{5,7},{6,4},{7,5},{8,10},{9,11},{10,... | collective-permute-start | bytes 786440 | tf_op jit(solution)/shard_map/ppermute | solution.py:37
  15.1 8.5 %collective-permute-start.4 = (bf16[32,4096]{1,0:T(8,128)(2,1)S(1)}, bf16[32,4096]{1,0:T(8,128)(2,1)S(1)}, u32[]{:S(2)}, u32[]{:S(2)}) collective-permute-start(bf16[32,4096]{1,0:T(8,128)(2,1)S(1)} %get-tuple-element.181), channel_id=1, source_target_pairs={{0,4},{1,5},{2,6},{3,7},{4,0},{5,1},{6,2},{7,3},{8,12},{9,13},{10,... | collective-permute-start | bytes 786440 | tf_op jit(solution)/shard_map/ppermute | solution.py:37
  17.1 8.2 %collective-permute-start.1 = (bf16[32,2048]{1,0:T(8,128)(2,1)S(1)}, bf16[32,2048]{1,0:T(8,128)(2,1)S(1)}, u32[]{:S(2)}, u32[]{:S(2)}) collective-permute-start(bf16[32,2048]{1,0:T(8,128)(2,1)S(1)} %get-tuple-element.174), channel_id=1, source_target_pairs={{0,1},{1,0},{2,3},{3,2},{4,5},{5,4},{6,7},{7,6},{8,9},{9,8},{10,11... | collective-permute-start | bytes 393224 | tf_op jit(solution)/shard_map/ppermute | solution.py:37
  19.3 6.5 %collective-permute-start.6 = (bf16[16,4096]{1,0:T(8,128)(2,1)S(1)}, bf16[16,4096]{1,0:T(8,128)(2,1)S(1)}, u32[]{:S(2)}, u32[]{:S(2)}) collective-permute-start(bf16[16,4096]{1,0:T(8,128)(2,1)S(1)} %slice.507), channel_id=1, source_target_pairs={{0,2},{1,3},{2,0},{3,1},{4,6},{5,7},{6,4},{7,5},{8,10},{9,11},{10,... | collective-permute-start | bytes 393224 | tf_op jit(solution)/shard_map/ppermute | solution.py:37
  27.8 6.4 %collective-permute-start.11 = (bf16[8,4096]{1,0:T(8,128)(2,1)S(1)}, bf16[8,4096]{1,0:T(8,128)(2,1)S(1)}, u32[]{:S(2)}, u32[]{:S(2)}) collective-permute-start(bf16[8,4096]{1,0:T(8,128)(2,1)S(1)} %slice.521), channel_id=1, source_target_pairs={{0,1},{1,0},{2,3},{3,2},{4,5},{5,4},{6,7},{7,6},{8,9},{9,8},{10,11... | collective-permute-start | bytes 196616 | tf_op jit(solution)/shard_map/ppermute | solution.py:37
  31.5 7.2 %collective-permute-start.16 = (bf16[8,4096]{1,0:T(8,128)(2,1)S(1)}, bf16[8,4096]{1,0:T(8,128)(2,1)S(1)}, u32[]{:S(2)}, u32[]{:S(2)}) collective-permute-start(bf16[8,4096]{1,0:T(8,128)(2,1)S(1)} %fusion.11.low_ref), channel_id=1, source_target_pairs={{0,8},{1,9},{2,10},{3,11},{4,12},{5,13},{6,14},{7,15},{8,0},{9,1},... | collective-permute-start | bytes 196616 | tf_op jit(solution)/shard_map/ppermute | solution.py:37
  34.8 7.6 %collective-permute-start.14 = (bf16[8,4096]{1,0:T(8,128)(2,1)S(1)}, bf16[8,4096]{1,0:T(8,128)(2,1)S(1)}, u32[]{:S(2)}, u32[]{:S(2)}) collective-permute-start(bf16[8,4096]{1,0:T(8,128)(2,1)S(1)} %fusion.9.low_ref), channel_id=1, source_target_pairs={{0,8},{1,9},{2,10},{3,11},{4,12},{5,13},{6,14},{7,15},{8,0},{9,1},... | collective-permute-start | bytes 196616 | tf_op jit(solution)/shard_map/ppermute | solution.py:37
  46.8 6.4 %collective-permute-start.24 = (bf16[16,4096]{1,0:T(8,128)(2,1)S(1)}, bf16[16,4096]{1,0:T(8,128)(2,1)S(1)}, u32[]{:S(2)}, u32[]{:S(2)}) collective-permute-start(bf16[16,4096]{1,0:T(8,128)(2,1)S(1)} %get-tuple-element.370), channel_id=1, source_target_pairs={{0,1},{1,0},{2,3},{3,2},{4,5},{5,4},{6,7},{7,6},{8,9},{9,8},{10,11... | collective-permute-start | bytes 393224 | tf_op jit(solution)/shard_map/ppermute | solution.py:37
  54.1 6.4 %collective-permute-start.29 = (bf16[32,4096]{1,0:T(8,128)(2,1)S(1)}, bf16[32,4096]{1,0:T(8,128)(2,1)S(1)}, u32[]{:S(2)}, u32[]{:S(2)}) collective-permute-start(bf16[32,4096]{1,0:T(8,128)(2,1)S(1)} %constant_dynamic-update-slice_fusion.9.refs_2_), channel_id=1, source_target_pairs={{0,1},{1,0},{2,3},{3,2},{4,5},{5,4},{6,7},{7,6},{8,9},{9,8},{10,11... | collective-permute-start | bytes 786440 | tf_op jit(solution)/shard_map/ppermute | solution.py:37
  55.0 6.4 %collective-permute-start.28 = (bf16[32,4096]{1,0:T(8,128)(2,1)S(1)}, bf16[32,4096]{1,0:T(8,128)(2,1)S(1)}, u32[]{:S(2)}, u32[]{:S(2)}) collective-permute-start(bf16[32,4096]{1,0:T(8,128)(2,1)S(1)} %constant_dynamic-update-slice_fusion.12.refs_2_), channel_id=1, source_target_pairs={{0,2},{1,3},{2,0},{3,1},{4,6},{5,7},{6,4},{7,5},{8,10},{9,11},{10,... | collective-permute-start | bytes 786440 | tf_op jit(solution)/shard_map/ppermute | solution.py:37
  56.3 6.4 %collective-permute-start.27 = (bf16[32,4096]{1,0:T(8,128)(2,1)S(1)}, bf16[32,4096]{1,0:T(8,128)(2,1)S(1)}, u32[]{:S(2)}, u32[]{:S(2)}) collective-permute-start(bf16[32,4096]{1,0:T(8,128)(2,1)S(1)} %constant_dynamic-update-slice_fusion.6.refs_2_), channel_id=1, source_target_pairs={{0,4},{1,5},{2,6},{3,7},{4,0},{5,1},{6,2},{7,3},{8,12},{9,13},{10,... | collective-permute-start | bytes 786440 | tf_op jit(solution)/shard_map/ppermute | solution.py:37
  65.4 9.2 %collective-permute-start.32 = (bf16[32,4096]{1,0:T(8,128)(2,1)S(1)}, bf16[32,4096]{1,0:T(8,128)(2,1)S(1)}, u32[]{:S(2)}, u32[]{:S(2)}) collective-permute-start(bf16[32,4096]{1,0:T(8,128)(2,1)S(1)} %get-tuple-element.212), channel_id=1, source_target_pairs={{0,1},{1,0},{2,3},{3,2},{4,5},{5,4},{6,7},{7,6},{8,9},{9,8},{10,11... | collective-permute-start | bytes 786440 | tf_op jit(solution)/shard_map/ppermute | solution.py:37
  66.6 9.0 %collective-permute-start.33 = (bf16[32,4096]{1,0:T(8,128)(2,1)S(1)}, bf16[32,4096]{1,0:T(8,128)(2,1)S(1)}, u32[]{:S(2)}, u32[]{:S(2)}) collective-permute-start(bf16[32,4096]{1,0:T(8,128)(2,1)S(1)} %get-tuple-element.214), channel_id=1, source_target_pairs={{0,2},{1,3},{2,0},{3,1},{4,6},{5,7},{6,4},{7,5},{8,10},{9,11},{10,... | collective-permute-start | bytes 786440 | tf_op jit(solution)/shard_map/ppermute | solution.py:37
  68.3 8.8 %collective-permute-start.34 = (bf16[32,4096]{1,0:T(8,128)(2,1)S(1)}, bf16[32,4096]{1,0:T(8,128)(2,1)S(1)}, u32[]{:S(2)}, u32[]{:S(2)}) collective-permute-start(bf16[32,4096]{1,0:T(8,128)(2,1)S(1)} %get-tuple-element.217), channel_id=1, source_target_pairs={{0,4},{1,5},{2,6},{3,7},{4,0},{5,1},{6,2},{7,3},{8,12},{9,13},{10,... | collective-permute-start | bytes 786440 | tf_op jit(solution)/shard_map/ppermute | solution.py:37
  70.0 8.2 %collective-permute-start.31 = (bf16[32,2048]{1,0:T(8,128)(2,1)S(1)}, bf16[32,2048]{1,0:T(8,128)(2,1)S(1)}, u32[]{:S(2)}, u32[]{:S(2)}) collective-permute-start(bf16[32,2048]{1,0:T(8,128)(2,1)S(1)} %get-tuple-element.210), channel_id=1, source_target_pairs={{0,1},{1,0},{2,3},{3,2},{4,5},{5,4},{6,7},{7,6},{8,9},{9,8},{10,11... | collective-permute-start | bytes 393224 | tf_op jit(solution)/shard_map/ppermute | solution.py:37
  85.2 6.4 %collective-permute-start.46 = (bf16[8,4096]{1,0:T(8,128)(2,1)S(1)}, bf16[8,4096]{1,0:T(8,128)(2,1)S(1)}, u32[]{:S(2)}, u32[]{:S(2)}) collective-permute-start(bf16[8,4096]{1,0:T(8,128)(2,1)S(1)} %fusion.8.low_ref), channel_id=1, source_target_pairs={{0,8},{1,9},{2,10},{3,11},{4,12},{5,13},{6,14},{7,15},{8,0},{9,1},... | collective-permute-start | bytes 196616 | tf_op jit(solution)/shard_map/ppermute | solution.py:37
  106.7 6.4 %collective-permute-start.59 = (bf16[32,4096]{1,0:T(8,128)(2,1)S(1)}, bf16[32,4096]{1,0:T(8,128)(2,1)S(1)}, u32[]{:S(2)}, u32[]{:S(2)}) collective-permute-start(bf16[32,4096]{1,0:T(8,128)(2,1)S(1)} %constant_dynamic-update-slice_fusion.24.refs_2_), channel_id=1, source_target_pairs={{0,1},{1,0},{2,3},{3,2},{4,5},{5,4},{6,7},{7,6},{8,9},{9,8},{10,11... | collective-permute-start | bytes 786440 | tf_op jit(solution)/shard_map/ppermute | solution.py:37
  107.7 6.4 %collective-permute-start.58 = (bf16[32,4096]{1,0:T(8,128)(2,1)S(1)}, bf16[32,4096]{1,0:T(8,128)(2,1)S(1)}, u32[]{:S(2)}, u32[]{:S(2)}) collective-permute-start(bf16[32,4096]{1,0:T(8,128)(2,1)S(1)} %constant_dynamic-update-slice_fusion.27.refs_2_), channel_id=1, source_target_pairs={{0,2},{1,3},{2,0},{3,1},{4,6},{5,7},{6,4},{7,5},{8,10},{9,11},{10,... | collective-permute-start | bytes 786440 | tf_op jit(solution)/shard_map/ppermute | solution.py:37
  118.0 9.2 %collective-permute-start.62 = (bf16[32,4096]{1,0:T(8,128)(2,1)S(1)}, bf16[32,4096]{1,0:T(8,128)(2,1)S(1)}, u32[]{:S(2)}, u32[]{:S(2)}) collective-permute-start(bf16[32,4096]{1,0:T(8,128)(2,1)S(1)} %get-tuple-element.256), channel_id=1, source_target_pairs={{0,1},{1,0},{2,3},{3,2},{4,5},{5,4},{6,7},{7,6},{8,9},{9,8},{10,11... | collective-permute-start | bytes 786440 | tf_op jit(solution)/shard_map/ppermute | solution.py:37
  119.5 8.7 %collective-permute-start.63 = (bf16[32,4096]{1,0:T(8,128)(2,1)S(1)}, bf16[32,4096]{1,0:T(8,128)(2,1)S(1)}, u32[]{:S(2)}, u32[]{:S(2)}) collective-permute-start(bf16[32,4096]{1,0:T(8,128)(2,1)S(1)} %get-tuple-element.258), channel_id=1, source_target_pairs={{0,2},{1,3},{2,0},{3,1},{4,6},{5,7},{6,4},{7,5},{8,10},{9,11},{10,... | collective-permute-start | bytes 786440 | tf_op jit(solution)/shard_map/ppermute | solution.py:37
  120.9 8.6 %collective-permute-start.64 = (bf16[32,4096]{1,0:T(8,128)(2,1)S(1)}, bf16[32,4096]{1,0:T(8,128)(2,1)S(1)}, u32[]{:S(2)}, u32[]{:S(2)}) collective-permute-start(bf16[32,4096]{1,0:T(8,128)(2,1)S(1)} %get-tuple-element.261), channel_id=1, source_target_pairs={{0,4},{1,5},{2,6},{3,7},{4,0},{5,1},{6,2},{7,3},{8,12},{9,13},{10,... | collective-permute-start | bytes 786440 | tf_op jit(solution)/shard_map/ppermute | solution.py:37
  122.4 8.2 %collective-permute-start.61 = (bf16[32,2048]{1,0:T(8,128)(2,1)S(1)}, bf16[32,2048]{1,0:T(8,128)(2,1)S(1)}, u32[]{:S(2)}, u32[]{:S(2)}) collective-permute-start(bf16[32,2048]{1,0:T(8,128)(2,1)S(1)} %get-tuple-element.254), channel_id=1, source_target_pairs={{0,1},{1,0},{2,3},{3,2},{4,5},{5,4},{6,7},{7,6},{8,9},{9,8},{10,11... | collective-permute-start | bytes 393224 | tf_op jit(solution)/shard_map/ppermute | solution.py:37
  150.4 6.4 %collective-permute-start.83 = (bf16[16,4096]{1,0:T(8,128)(2,1)S(1)}, bf16[16,4096]{1,0:T(8,128)(2,1)S(1)}, u32[]{:S(2)}, u32[]{:S(2)}) collective-permute-start(bf16[16,4096]{1,0:T(8,128)(2,1)S(1)} %get-tuple-element.350), channel_id=1, source_target_pairs={{0,4},{1,5},{2,6},{3,7},{4,0},{5,1},{6,2},{7,3},{8,12},{9,13},{10,... | collective-permute-start | bytes 393224 | tf_op jit(solution)/shard_map/ppermute | solution.py:37
  151.5 6.4 %collective-permute-start.84 = (bf16[16,4096]{1,0:T(8,128)(2,1)S(1)}, bf16[16,4096]{1,0:T(8,128)(2,1)S(1)}, u32[]{:S(2)}, u32[]{:S(2)}) collective-permute-start(bf16[16,4096]{1,0:T(8,128)(2,1)S(1)} %get-tuple-element.346), channel_id=1, source_target_pairs={{0,1},{1,0},{2,3},{3,2},{4,5},{5,4},{6,7},{7,6},{8,9},{9,8},{10,11... | collective-permute-start | bytes 393224 | tf_op jit(solution)/shard_map/ppermute | solution.py:37
  159.1 6.5 %collective-permute-start.89 = (bf16[32,4096]{1,0:T(8,128)(2,1)S(1)}, bf16[32,4096]{1,0:T(8,128)(2,1)S(1)}, u32[]{:S(2)}, u32[]{:S(2)}) collective-permute-start(bf16[32,4096]{1,0:T(8,128)(2,1)S(1)} %constant_dynamic-update-slice_fusion.39.refs_2_), channel_id=1, source_target_pairs={{0,1},{1,0},{2,3},{3,2},{4,5},{5,4},{6,7},{7,6},{8,9},{9,8},{10,11... | collective-permute-start | bytes 786440 | tf_op jit(solution)/shard_map/ppermute | solution.py:37
  160.0 7.2 %collective-permute-start.88 = (bf16[32,4096]{1,0:T(8,128)(2,1)S(1)}, bf16[32,4096]{1,0:T(8,128)(2,1)S(1)}, u32[]{:S(2)}, u32[]{:S(2)}) collective-permute-start(bf16[32,4096]{1,0:T(8,128)(2,1)S(1)} %constant_dynamic-update-slice_fusion.42.refs_2_), channel_id=1, source_target_pairs={{0,2},{1,3},{2,0},{3,1},{4,6},{5,7},{6,4},{7,5},{8,10},{9,11},{10,... | collective-permute-start | bytes 786440 | tf_op jit(solution)/shard_map/ppermute | solution.py:37
  160.8 8.2 %collective-permute-start.87 = (bf16[32,4096]{1,0:T(8,128)(2,1)S(1)}, bf16[32,4096]{1,0:T(8,128)(2,1)S(1)}, u32[]{:S(2)}, u32[]{:S(2)}) collective-permute-start(bf16[32,4096]{1,0:T(8,128)(2,1)S(1)} %constant_dynamic-update-slice_fusion.36.refs_2_), channel_id=1, source_target_pairs={{0,4},{1,5},{2,6},{3,7},{4,0},{5,1},{6,2},{7,3},{8,12},{9,13},{10,... | collective-permute-start | bytes 786440 | tf_op jit(solution)/shard_map/ppermute | solution.py:37
  172.4 9.2 %collective-permute-start.92 = (bf16[32,4096]{1,0:T(8,128)(2,1)S(1)}, bf16[32,4096]{1,0:T(8,128)(2,1)S(1)}, u32[]{:S(2)}, u32[]{:S(2)}) collective-permute-start(bf16[32,4096]{1,0:T(8,128)(2,1)S(1)} %get-tuple-element.300), channel_id=1, source_target_pairs={{0,1},{1,0},{2,3},{3,2},{4,5},{5,4},{6,7},{7,6},{8,9},{9,8},{10,11... | collective-permute-start | bytes 786440 | tf_op jit(solution)/shard_map/ppermute | solution.py:37
  173.9 8.8 %collective-permute-start.93 = (bf16[32,4096]{1,0:T(8,128)(2,1)S(1)}, bf16[32,4096]{1,0:T(8,128)(2,1)S(1)}, u32[]{:S(2)}, u32[]{:S(2)}) collective-permute-start(bf16[32,4096]{1,0:T(8,128)(2,1)S(1)} %get-tuple-element.302), channel_id=1, source_target_pairs={{0,2},{1,3},{2,0},{3,1},{4,6},{5,7},{6,4},{7,5},{8,10},{9,11},{10,... | collective-permute-start | bytes 786440 | tf_op jit(solution)/shard_map/ppermute | solution.py:37
  175.3 8.5 %collective-permute-start.94 = (bf16[32,4096]{1,0:T(8,128)(2,1)S(1)}, bf16[32,4096]{1,0:T(8,128)(2,1)S(1)}, u32[]{:S(2)}, u32[]{:S(2)}) collective-permute-start(bf16[32,4096]{1,0:T(8,128)(2,1)S(1)} %get-tuple-element.305), channel_id=1, source_target_pairs={{0,4},{1,5},{2,6},{3,7},{4,0},{5,1},{6,2},{7,3},{8,12},{9,13},{10,... | collective-permute-start | bytes 786440 | tf_op jit(solution)/shard_map/ppermute | solution.py:37
  176.7 8.2 %collective-permute-start.91 = (bf16[32,2048]{1,0:T(8,128)(2,1)S(1)}, bf16[32,2048]{1,0:T(8,128)(2,1)S(1)}, u32[]{:S(2)}, u32[]{:S(2)}) collective-permute-start(bf16[32,2048]{1,0:T(8,128)(2,1)S(1)} %get-tuple-element.298), channel_id=1, source_target_pairs={{0,1},{1,0},{2,3},{3,2},{4,5},{5,4},{6,7},{7,6},{8,9},{9,8},{10,11... | collective-permute-start | bytes 393224 | tf_op jit(solution)/shard_map/ppermute | solution.py:37
  (92 other events, 458.5 us)
